TPU v7x, 512 devices: a whole 4x8x8 slice. The times are simulated.
512 devices in a mesh: seq: 128 (over z, y, core), tp: 4 (over x).
Axes of the slice: x: 4, y: 8, z: 8, core: 2. Of those that a mesh axis runs over, the one named last changes fastest.
Arguments:
- queries: bfloat16 [16384, 4096], P('seq', 'tp'), may hold values from -128 to 128
- keys: bfloat16 [16384, 4096], P('seq', 'tp'), may hold values from -6 to 6
- values: bfloat16 [16384, 4096], P('seq', 'tp'), may hold values from -18 to 18
- residual_in: bfloat16 [16384, 4096], P('seq', 'tp'), may hold values from -6 to 6
- norm_gain: float32 [4096], replicated, may hold values from 0.1 to 1.9
- routing: int32 [128, 1], replicated, may hold values from 0 to 63; in each aligned block of 128 rows (0 to 127, 128 to 255, ...) at most 4 rows name the same one
- gate_weight: bfloat16 [128, 4096, 512], P('seq', None, 'tp'), may hold values from -0.09375 to 0.09375
- up_weight: bfloat16 [128, 4096, 512], P('seq', None, 'tp'), may hold values from -0.09375 to 0.09375
- down_weight: bfloat16 [128, 512, 4096], P('seq', None, 'tp'), may hold values from -0.1875 to 0.1875
Outputs:
- mixed: bfloat16 [16384, 4096], P('seq', 'tp')
Inputs may be any that keep to these rules, and one draw needn't show every extreme that they name: `routing`: every expert is named by some block; no expert by more than 4 blocks, and one by exactly 4.
All inputs are finite; a program needn't handle non-finite values.
Results may differ from a plain program's by a relative error of at most 0.006.
Values may be sent and summed in bfloat16 or wider, within the bound.
No kernel may reach another device: no remote copies, remote signals or barrier semaphores. Data moves between devices by JAX's collectives and lax.ppermute only.
A program may use at most 64 MiB of HBM per device.

v0:
```python
import math

import jax
import jax.numpy as jnp
from jax import lax
from jax.sharding import PartitionSpec as P

HEAD_DIM = 128
BLOCK = 128
WINDOW = 512


epsilon = 1e-05
masked_score = -1e30


def shifted(block, axis, distance):
    devices = range(lax.axis_size(axis))
    route = [(i - distance, i) for i in devices if i - distance in devices]
    return lax.ppermute(block, axis, route)


def local(
    queries, keys, values, residual_in, norm_gain, routing, gate_weight, up_weight, down_weight
):
    seq_count = lax.axis_size("seq")
    seq_place = lax.axis_index("seq")
    tok_rows = queries.shape[0]
    feat_width = queries.shape[1]
    head_count = feat_width // HEAD_DIM
    prior_count = (WINDOW - 1) // tok_rows + 1
    earlier_keys = []
    earlier_values = []
    for distance in range(1, prior_count + 1):
        moved_keys, moved_values = shifted((keys, values), "seq", distance)
        earlier_keys.insert(0, moved_keys)
        earlier_values.insert(0, moved_values)
    key_all = jnp.concatenate(earlier_keys + [keys], axis=0).reshape(-1, head_count, HEAD_DIM)
    value_all = jnp.concatenate(earlier_values + [values], axis=0).reshape(-1, head_count, HEAD_DIM)
    query_heads = queries.reshape(tok_rows, head_count, HEAD_DIM)
    query_pos = seq_place * tok_rows + jnp.arange(tok_rows, dtype=jnp.int32)
    key_pos = (
        seq_place * tok_rows
        - prior_count * tok_rows
        + jnp.arange((prior_count + 1) * tok_rows, dtype=jnp.int32)
    )
    visible = (
        (key_pos[None, :] >= 0)
        & (key_pos[None, :] <= query_pos[:, None])
        & (key_pos[None, :] > query_pos[:, None] - WINDOW)
    )
    scores = jnp.einsum(
        "qhd,khd->hqk", query_heads, key_all, preferred_element_type=jnp.float32
    ) * (1.0 / math.sqrt(HEAD_DIM))
    scores = jnp.where(visible[None], scores, masked_score)
    top_score = jnp.max(scores, axis=2, keepdims=True)
    expo = jnp.exp(scores - top_score)
    weights_soft = (expo / jnp.sum(expo, axis=2, keepdims=True)).astype(jnp.bfloat16)
    attended = jnp.einsum(
        "hqk,khd->qhd", weights_soft, value_all, preferred_element_type=jnp.float32
    ).reshape(tok_rows, feat_width)
    stream = (residual_in.astype(jnp.float32) + attended).astype(jnp.bfloat16)
    send_width = stream.shape[1]
    blocks_dev = tok_rows // BLOCK
    piece_rows = BLOCK // seq_count
    spread_in = stream.reshape(blocks_dev, seq_count, piece_rows, send_width)
    spread_out = lax.all_to_all(spread_in, "seq", split_axis=1, concat_axis=0, tiled=True)
    block_count = blocks_dev * seq_count
    spread_rows = spread_out.reshape(block_count, piece_rows, send_width)
    expert_ids = routing[:, 0]
    expert_count = seq_count // 2
    most_blocks = min(2 * block_count // expert_count, block_count - expert_count + 1)
    order_index = jnp.arange(block_count, dtype=jnp.int32)
    same_expert = expert_ids[None, :] == expert_ids[:, None]
    rank_of = jnp.sum(same_expert & (order_index[None, :] < order_index[:, None]), axis=1)
    expert_range = jnp.arange(expert_count, dtype=jnp.int32)
    slot_range = jnp.arange(most_blocks, dtype=jnp.int32)
    selector = (
        (expert_ids[None, None, :] == expert_range[:, None, None])
        & (rank_of[None, None, :] == slot_range[None, :, None])
    ).astype(jnp.bfloat16)
    picked = jnp.einsum(
        "erb,bqf->erqf", selector, spread_rows, preferred_element_type=jnp.float32
    ).astype(jnp.bfloat16)
    outgoing = jnp.broadcast_to(
        picked[:, None], (expert_count, 2, most_blocks, piece_rows, send_width)
    )
    outgoing = outgoing.reshape(seq_count, most_blocks, piece_rows, send_width)
    features_full = lax.all_gather(
        lax.all_to_all(outgoing, "seq", split_axis=0, concat_axis=0, tiled=True),
        "tp",
        axis=3,
        tiled=True,
    )
    source_count = features_full.shape[0]
    slot_count = features_full.shape[1]
    stream_f32 = features_full.astype(jnp.float32)
    mean_square = jnp.mean(stream_f32 * stream_f32, axis=3, keepdims=True)
    normed = (stream_f32 * lax.rsqrt(mean_square + epsilon) * norm_gain).astype(jnp.bfloat16)
    normed = normed.reshape(-1, normed.shape[3])
    gate_val = jnp.dot(normed, gate_weight[0], preferred_element_type=jnp.float32)
    up_val = jnp.dot(normed, up_weight[0], preferred_element_type=jnp.float32)
    hidden = (jax.nn.silu(gate_val) * up_val).astype(jnp.bfloat16)
    hidden_half = lax.all_gather(hidden, "tp", axis=1, tiled=True)
    partial_value = jnp.dot(hidden_half, down_weight[0], preferred_element_type=jnp.float32).astype(
        jnp.bfloat16
    )
    partial_value = partial_value.reshape(source_count, slot_count, piece_rows, feat_width)
    returned = lax.all_to_all(partial_value, "seq", split_axis=0, concat_axis=0, tiled=True)
    returned = returned.reshape(expert_count, 2, most_blocks, piece_rows * feat_width)
    combined = jnp.einsum("erb,epry->pby", selector, returned, preferred_element_type=jnp.float32)
    residual_rows = spread_rows
    residual_rows = residual_rows.reshape(block_count, piece_rows * feat_width).astype(jnp.float32)
    finished = (residual_rows + combined[0] + combined[1]).astype(jnp.bfloat16)
    finished = finished.reshape(seq_count, blocks_dev, piece_rows, feat_width)
    restored = lax.all_to_all(finished, "seq", split_axis=0, concat_axis=2, tiled=True)
    return restored.reshape(tok_rows, feat_width)


def solution(mesh):
    in_specs = (
        P("seq", "tp"),
        P("seq", "tp"),
        P("seq", "tp"),
        P("seq", "tp"),
        P(),
        P(),
        P("seq", None, "tp"),
        P("seq", None, "tp"),
        P("seq", None, "tp"),
    )
    out_specs = P("seq", "tp")
    return jax.shard_map(local, mesh=mesh, in_specs=in_specs, out_specs=out_specs, check_vma=False)
```

profile of v0, /device:TPU:1, one launch (start us, length us, event | category | flops | bytes accessed | tf_op | source)
XLA Modules:
  0.0 326.5 jit_solution(96557702983665667)
XLA Ops:
  7.8 4.6 %collective-permute-start.7 = (bf16[128,1024]{0,1:T(8,128)(2,1)S(1)}, bf16[128,1024]{0,1:T(8,128)(2,1)S(1)}, u32[]{:S(2)}, u32[]{:S(2)}) collective-permute-start(bf16[128,1024]{0,1:T(8,128)(2,1)S(1)} %copy.94), channel_id=1, source_target_pairs={{0,4},{4,8},{8,12},{12,16},{16,20},{20,24},{24,28},{28,32},{32,36}... | collective-permute-start | bytes 786440 | tf_op jit(solution)/shard_map/ppermute | solution.py:20
  12.4 3.2 collective-permute-start.6
  15.6 3.9 %collective-permute-start.2 = (bf16[128,1024]{1,0:T(8,128)(2,1)}, bf16[128,1024]{1,0:T(8,128)(2,1)}, u32[]{:S(2)}, u32[]{:S(2)}) collective-permute-start(bf16[128,1024]{1,0:T(8,128)(2,1)} %param.11), channel_id=1, source_target_pairs={{0,8},{4,12},{8,16},{12,20},{16,24},{20,28},{24,32},{28,36},{32,40... | collective-permute-start | bytes 786440 | tf_op jit(solution)/shard_map/ppermute | solution.py:20
  19.5 4.7 %collective-permute-start.1 = (bf16[128,1024]{1,0:T(8,128)(2,1)}, bf16[128,1024]{1,0:T(8,128)(2,1)}, u32[]{:S(2)}, u32[]{:S(2)}) collective-permute-start(bf16[128,1024]{1,0:T(8,128)(2,1)} %param.11), channel_id=1, source_target_pairs={{0,12},{4,16},{8,20},{12,24},{16,28},{20,32},{24,36},{28,40},{32,4... | collective-permute-start | bytes 786440 | tf_op jit(solution)/shard_map/ppermute | solution.py:20
  26.3 12.7 %collective-permute-done = bf16[128,1024]{1,0:T(8,128)(2,1)S(1)} collective-permute-done((bf16[128,1024]{1,0:T(8,128)(2,1)}, bf16[128,1024]{1,0:T(8,128)(2,1)S(1)}, u32[]{:S(2)}, u32[]{:S(2)}) %collective-permute-start) | collective-permute-done | bytes 262176 | tf_op jit(solution)/shard_map/ppermute | solution.py:20
  39.6 10.9 %collective-permute-start.3 = (bf16[128,1024]{1,0:T(8,128)(2,1)}, bf16[128,1024]{1,0:T(8,128)(2,1)S(1)}, u32[]{:S(2)}, u32[]{:S(2)}) collective-permute-start(bf16[128,1024]{1,0:T(8,128)(2,1)} %param.11), channel_id=1, source_target_pairs={{0,4},{4,8},{8,12},{12,16},{16,20},{20,24},{24,28},{28,32},{32,36}... | collective-permute-start | bytes 786440 | tf_op jit(solution)/shard_map/ppermute | solution.py:20
  51.5 2.0 collective-permute-start.5
  54.5 7.2 %collective-permute-start.4 = (bf16[128,1024]{0,1:T(8,128)(2,1)S(1)}, bf16[128,1024]{0,1:T(8,128)(2,1)S(1)}, u32[]{:S(2)}, u32[]{:S(2)}) collective-permute-start(bf16[128,1024]{0,1:T(8,128)(2,1)S(1)} %copy.94), channel_id=1, source_target_pairs={{0,16},{4,20},{8,24},{12,28},{16,32},{20,36},{24,40},{28,44},{32,4... | collective-permute-start | bytes 786440 | tf_op jit(solution)/shard_map/ppermute | solution.py:20
  62.8 6.3 %collective-permute-done.4 = bf16[128,1024]{0,1:T(8,128)(2,1)S(1)} collective-permute-done((bf16[128,1024]{0,1:T(8,128)(2,1)S(1)}, bf16[128,1024]{0,1:T(8,128)(2,1)S(1)}, u32[]{:S(2)}, u32[]{:S(2)}) %collective-permute-start.4) | collective-permute-done | bytes 262176 | tf_op jit(solution)/shard_map/ppermute | solution.py:20
  75.3 4.0 %fusion.38 = (f32[8,128]{1,0:T(8,128)S(1)}, f32[8,128,640]{1,2,0:T(8,128)}) fusion(pred[128,640]{0,1:T(8,128)(4,1)S(1)} %compare_and_fusion, bf16[640,8,128]{0,2,1:T(8,128)(2,1)} %bitcast.90, bf16[128,1024]{1,0:T(8,128)(2,1)S(1)} %copy-done.11), kind=kOutput, calls=%fused_computation.66 | convolution fusion | flops 170394240 | bytes 4280320 | tf_op jit(solution)/shard_map/sub | solution.py:57
  79.3 2.3 fusion.7
  82.8 2.1 reduce.1
  85.8 26.6 %all-to-all-start = ((bf16[128,2,512]{2,1,0:T(2,128)(2,1)}), bf16[128,2,512]{2,1,0:T(2,128)(2,1)S(1)}, u32[]{:S(2)}, u32[]{:S(2)}) async-start(bf16[128,2,512]{2,1,0:T(2,128)(2,1)} %reshape.257), calls=%async_computation | async-start | bytes 524288 | tf_op jit(solution)/shard_map/all_to_all | solution.py:67
  112.6 15.0 %all-to-all-done = bf16[128,2,512]{2,1,0:T(2,128)(2,1)S(1)} async-done(((bf16[128,2,512]{2,1,0:T(2,128)(2,1)}), bf16[128,2,512]{2,1,0:T(2,128)(2,1)S(1)}, u32[]{:S(2)}, u32[]{:S(2)}) %all-to-all-start) | async-done | bytes 262176 | tf_op jit(solution)/shard_map/all_to_all | solution.py:67
  128.9 36.6 %all_to_all.28 = bf16[128,4,1,1024]{3,1,2,0:T(4,128)(2,1)} all-to-all(bf16[128,4,1,1024]{3,1,2,0:T(4,128)(2,1)S(1)} %bitcast.84), channel_id=1, replica_groups=mesh['seq'=128,'tp'=4] {'seq'}, dimensions={0} | all-to-all | bytes 2097152 | tf_op jit(solution)/shard_map/all_to_all | solution.py:90
  165.5 47.2 %all-gather.2.cloned.1.call-done = bf16[128,4,1,4096]{3,1,2,0:T(4,128)(2,1)} async-done(((bf16[128,4,1,1024]{3,1,2,0:T(4,128)(2,1)}), bf16[128,4,1,4096]{3,1,2,0:T(4,128)(2,1)}) %all-gather.2.cloned.1.call-update) | async-done | bytes 4194320 | tf_op jit(solution)/shard_map/all_gather | solution.py:89
  212.8 4.6 %fusion.1 = f32[128,4]{1,0:T(8,128)S(1)} fusion(bf16[128,4,1,4096]{3,1,2,0:T(4,128)(2,1)} %all-gather.2.cloned.1.call-done), kind=kLoop, calls=%fused_computation.3 | loop fusion | flops 6290944 | bytes 4196352 | tf_op jit(solution)/shard_map/reduce_sum | solution.py:98
  217.4 5.0 %fusion.3 = bf16[128,4,1,4096]{3,1,2,0:T(4,128)(2,1)} fusion(bf16[128,4,1,4096]{3,1,2,0:T(4,128)(2,1)S(1)} %copy-done.1, f32[4096]{0:T(1024)S(1)} %copy-done.8, f32[128,4]{1,0:T(8,128)S(1)} %add_rsqrt_fusion), kind=kLoop, calls=%fused_computation.5 | loop fusion | flops 8388608 | bytes 8407040 | tf_op jit(solution)/shard_map/convert_element_type | solution.py:99
  222.5 7.1 %reshape.248 = bf16[512,4096]{1,0:T(8,128)(2,1)} reshape(bf16[128,4,1,4096]{3,1,2,0:T(4,128)(2,1)} %fusion.3) | data formatting | bytes 8388608 | tf_op jit(solution)/shard_map/reshape | solution.py:100
  229.5 3.6 %fusion.12 = f32[512,128]{1,0:T(8,128)S(1)} fusion(bf16[512,4096]{1,0:T(8,128)(2,1)} %reshape.248, bf16[1,4096,128]{2,1,0:T(8,128)(2,1)S(1)} %copy-done.4), kind=kOutput, calls=%fused_computation.21 | convolution fusion | flops 536870912 | bytes 5505024 | tf_op jit(solution)/shard_map/dot_general | solution.py:101
  234.5 11.8 %all_gather.7 = bf16[512,512]{1,0:T(8,128)(2,1)S(1)} all-gather(bf16[512,128]{1,0:T(8,128)(2,1)S(1)} %fusion.9), channel_id=1, replica_groups=mesh['seq'=128,'tp'=4] {'tp'}, dimensions={1}, use_global_device_ids=true | all-gather | bytes 655360 | tf_op jit(solution)/shard_map/all_gather | solution.py:104
  248.2 16.0 %all-to-all-start.2 = ((bf16[128,4,1,1024]{3,1,2,0:T(4,128)(2,1)}), bf16[128,4,1,1024]{3,1,2,0:T(4,128)(2,1)S(1)}, u32[]{:S(2)}, u32[]{:S(2)}) async-start(bf16[128,4,1,1024]{3,1,2,0:T(4,128)(2,1)} %bitcast.12), calls=%async_computation.2 | async-start | bytes 2097152 | tf_op jit(solution)/shard_map/all_to_all | solution.py:109
  264.6 30.4 %all-to-all-done.2 = bf16[128,4,1,1024]{3,1,2,0:T(4,128)(2,1)S(1)} async-done(((bf16[128,4,1,1024]{3,1,2,0:T(4,128)(2,1)}), bf16[128,4,1,1024]{3,1,2,0:T(4,128)(2,1)S(1)}, u32[]{:S(2)}, u32[]{:S(2)}) %all-to-all-start.2) | async-done | bytes 1048608 | tf_op jit(solution)/shard_map/all_to_all | solution.py:109
  297.1 21.5 %all_to_all.29 = bf16[128,2,512]{2,1,0:T(2,128)(2,1)S(1)} all-to-all(bf16[128,2,512]{2,1,0:T(2,128)(2,1)S(1)} %reshape.259), channel_id=1, replica_groups=mesh['seq'=128,'tp'=4] {'seq'}, dimensions={0} | all-to-all | bytes 524288 | tf_op jit(solution)/shard_map/all_to_all | solution.py:116
  (73 shorter events, 23.5 us)
Async XLA Ops:
  6.5 239.8 %copy-start = (bf16[1,512,1024]{2,1,0:T(8,128)(2,1)S(1)}, bf16[1,512,1024]{2,1,0:T(8,128)(2,1)}, u32[]{:S(2)}) copy-start(bf16[1,512,1024]{2,1,0:T(8,128)(2,1)} %param.17) | copy-start | bytes 3145732
  6.5 56.2 %copy-start.5 = (bf16[128,1024]{1,0:T(8,128)(2,1)S(1)}, bf16[128,1024]{1,0:T(8,128)(2,1)}, u32[]{:S(2)}) copy-start(bf16[128,1024]{1,0:T(8,128)(2,1)} %param.11) | copy-start | bytes 786436
  7.8 66.0 %collective-permute-start.7 = (bf16[128,1024]{0,1:T(8,128)(2,1)S(1)}, bf16[128,1024]{0,1:T(8,128)(2,1)S(1)}, u32[]{:S(2)}, u32[]{:S(2)}) collective-permute-start(bf16[128,1024]{0,1:T(8,128)(2,1)S(1)} %copy.94), channel_id=1, source_target_pairs={{0,4},{4,8},{8,12},{12,16},{16,20},{20,24},{24,28},{28,32},{32,36}... | collective-permute-start | bytes 786440 | tf_op jit(solution)/shard_map/ppermute | solution.py:20
  12.4 60.6 %collective-permute-start.6 = (bf16[128,1024]{0,1:T(8,128)(2,1)S(1)}, bf16[128,1024]{0,1:T(8,128)(2,1)S(1)}, u32[]{:S(2)}, u32[]{:S(2)}) collective-permute-start(bf16[128,1024]{0,1:T(8,128)(2,1)S(1)} %copy.94), channel_id=1, source_target_pairs={{0,8},{4,12},{8,16},{12,20},{16,24},{20,28},{24,32},{28,36},{32,40... | collective-permute-start | bytes 786440 | tf_op jit(solution)/shard_map/ppermute | solution.py:20
  15.6 38.9 %collective-permute-start.2 = (bf16[128,1024]{1,0:T(8,128)(2,1)}, bf16[128,1024]{1,0:T(8,128)(2,1)}, u32[]{:S(2)}, u32[]{:S(2)}) collective-permute-start(bf16[128,1024]{1,0:T(8,128)(2,1)} %param.11), channel_id=1, source_target_pairs={{0,8},{4,12},{8,16},{12,20},{16,24},{20,28},{24,32},{28,36},{32,40... | collective-permute-start | bytes 786440 | tf_op jit(solution)/shard_map/ppermute | solution.py:20
  19.5 32.0 %collective-permute-start.1 = (bf16[128,1024]{1,0:T(8,128)(2,1)}, bf16[128,1024]{1,0:T(8,128)(2,1)}, u32[]{:S(2)}, u32[]{:S(2)}) collective-permute-start(bf16[128,1024]{1,0:T(8,128)(2,1)} %param.11), channel_id=1, source_target_pairs={{0,12},{4,16},{8,20},{12,24},{16,28},{20,32},{24,36},{28,40},{32,4... | collective-permute-start | bytes 786440 | tf_op jit(solution)/shard_map/ppermute | solution.py:20
  24.2 14.7 %collective-permute-start = (bf16[128,1024]{1,0:T(8,128)(2,1)}, bf16[128,1024]{1,0:T(8,128)(2,1)S(1)}, u32[]{:S(2)}, u32[]{:S(2)}) collective-permute-start(bf16[128,1024]{1,0:T(8,128)(2,1)} %param.11), channel_id=1, source_target_pairs={{0,16},{4,20},{8,24},{12,28},{16,32},{20,36},{24,40},{28,44},{32,4... | collective-permute-start | bytes 786440 | tf_op jit(solution)/shard_map/ppermute | solution.py:20
  38.9 0.7 copy-start.6
  39.6 23.0 %collective-permute-start.3 = (bf16[128,1024]{1,0:T(8,128)(2,1)}, bf16[128,1024]{1,0:T(8,128)(2,1)S(1)}, u32[]{:S(2)}, u32[]{:S(2)}) collective-permute-start(bf16[128,1024]{1,0:T(8,128)(2,1)} %param.11), channel_id=1, source_target_pairs={{0,4},{4,8},{8,12},{12,16},{16,20},{20,24},{24,28},{28,32},{32,36}... | collective-permute-start | bytes 786440 | tf_op jit(solution)/shard_map/ppermute | solution.py:20
  51.5 19.8 %collective-permute-start.5 = (bf16[128,1024]{0,1:T(8,128)(2,1)S(1)}, bf16[128,1024]{0,1:T(8,128)(2,1)}, u32[]{:S(2)}, u32[]{:S(2)}) collective-permute-start(bf16[128,1024]{0,1:T(8,128)(2,1)S(1)} %copy.94), channel_id=1, source_target_pairs={{0,12},{4,16},{8,20},{12,24},{16,28},{20,32},{24,36},{28,40},{32,4... | collective-permute-start | bytes 786440 | tf_op jit(solution)/shard_map/ppermute | solution.py:20
  54.5 14.6 %collective-permute-start.4 = (bf16[128,1024]{0,1:T(8,128)(2,1)S(1)}, bf16[128,1024]{0,1:T(8,128)(2,1)S(1)}, u32[]{:S(2)}, u32[]{:S(2)}) collective-permute-start(bf16[128,1024]{0,1:T(8,128)(2,1)S(1)} %copy.94), channel_id=1, source_target_pairs={{0,16},{4,20},{8,24},{12,28},{16,32},{20,36},{24,40},{28,44},{32,4... | collective-permute-start | bytes 786440 | tf_op jit(solution)/shard_map/ppermute | solution.py:20
  71.3 4.0 %copy-start.11 = (bf16[128,1024]{1,0:T(8,128)(2,1)S(1)}, bf16[128,1024]{1,0:T(8,128)(2,1)}, u32[]{:S(2)}) copy-start(bf16[128,1024]{1,0:T(8,128)(2,1)} %param.9) | copy-start | bytes 786436
  75.3 4.0 %copy-start.3 = (bf16[640,1024]{0,1:T(8,128)(2,1)S(1)}, bf16[640,1024]{0,1:T(8,128)(2,1)}, u32[]{:S(2)}) copy-start(bf16[640,1024]{0,1:T(8,128)(2,1)} %copy.93) | copy-start | bytes 3932164
  79.3 2.5 copy-start.7
  81.9 30.5 %copy-start.9 = (s32[128,1]{0,1:T(1,128)S(1)}, s32[128,1]{0,1:T(1,128)}, u32[]{:S(2)}) copy-start(s32[128,1]{0,1:T(1,128)} %param.14) | copy-start | bytes 1540
  85.8 41.8 %all-to-all-start = ((bf16[128,2,512]{2,1,0:T(2,128)(2,1)}), bf16[128,2,512]{2,1,0:T(2,128)(2,1)S(1)}, u32[]{:S(2)}, u32[]{:S(2)}) async-start(bf16[128,2,512]{2,1,0:T(2,128)(2,1)} %reshape.257), calls=%async_computation | async-start | bytes 524288 | tf_op jit(solution)/shard_map/all_to_all | solution.py:67
  112.4 100.4 %all-gather.2.cloned.1.call-start = ((), (), s32[]{:S(2)}) async-start(), calls=%async_computation.4 | async-start | bytes 5242880 | tf_op jit(solution)/shard_map/all_gather | solution.py:89
  165.5 51.9 %copy-start.8 = (f32[4096]{0:T(1024)S(1)}, f32[4096]{0:T(1024)}, u32[]{:S(2)}) copy-start(f32[4096]{0:T(1024)} %param.13) | copy-start | bytes 49156
  212.8 4.6 %copy-start.1 = (bf16[128,4,1,4096]{3,1,2,0:T(4,128)(2,1)S(1)}, bf16[128,4,1,4096]{3,1,2,0:T(4,128)(2,1)}, u32[]{:S(2)}) copy-start(bf16[128,4,1,4096]{3,1,2,0:T(4,128)(2,1)} %all-gather.2.cloned.1.call-done) | copy-start | bytes 12582916
  222.5 7.1 %copy-start.4 = (bf16[1,4096,128]{2,1,0:T(8,128)(2,1)S(1)}, bf16[1,4096,128]{2,1,0:T(8,128)(2,1)}, u32[]{:S(2)}) copy-start(bf16[1,4096,128]{2,1,0:T(8,128)(2,1)} %param.15) | copy-start | bytes 3145732
  229.5 3.6 %copy-start.2 = (bf16[512,4096]{1,0:T(8,128)(2,1)S(1)}, bf16[512,4096]{1,0:T(8,128)(2,1)}, u32[]{:S(2)}) copy-start(bf16[512,4096]{1,0:T(8,128)(2,1)} %reshape.248) | copy-start | bytes 12582916
  229.5 3.7 %copy-start.10 = (bf16[1,4096,128]{2,1,0:T(8,128)(2,1)S(1)}, bf16[1,4096,128]{2,1,0:T(8,128)(2,1)}, u32[]{:S(2)}) copy-start(bf16[1,4096,128]{2,1,0:T(8,128)(2,1)} %param.16) | copy-start | bytes 3145732
  248.2 46.9 %all-to-all-start.2 = ((bf16[128,4,1,1024]{3,1,2,0:T(4,128)(2,1)}), bf16[128,4,1,1024]{3,1,2,0:T(4,128)(2,1)S(1)}, u32[]{:S(2)}, u32[]{:S(2)}) async-start(bf16[128,4,1,1024]{3,1,2,0:T(4,128)(2,1)} %bitcast.12), calls=%async_computation.2 | async-start | bytes 2097152 | tf_op jit(solution)/shard_map/all_to_all | solution.py:109
Sparse Core Ops, SparseCore 0:
  165.7 47.0 all-gather.1
where the time goes:
time: 327 us
  waiting for transfers between devices  112 us (34%)
  starting transfers between devices  80.8 us (25%)
  blocking collectives  69.9 us (21%)
  local copies, waits for them, and re-layouts  24.2 us (7%)
  between operations  13.8 us (4%)
  matrix products  13.1 us (4%)
  other arithmetic  13 us (4%)
    all_gather x1, waiting for transfers between devices, local(): lax.all_gather(lax.all_to_all(outgoing, 'seq', split_axis=0, concat_axis=...  47.2 us
    ppermute x8, starting transfers between devices, shifted(): return lax.ppermute(block, axis, route)  38.3 us
    all_to_all x1, blocking collectives, local(): lax.all_to_all(outgoing, 'seq', split_axis=0, concat_axis=0, tiled=True)  36.6 us
    all_to_all x1, waiting for transfers between devices, local(): lax.all_to_all(partial_value, 'seq', split_axis=0, concat_axis=0, tiled=T...  30.4 us
    all_to_all x1, starting transfers between devices, local(): lax.all_to_all(spread_in, 'seq', split_axis=1, concat_axis=0, tiled=True)  26.6 us
    all_to_all x1, blocking collectives, local(): lax.all_to_all(finished, 'seq', split_axis=0, concat_axis=2, tiled=True)  21.5 us
    ppermute x8, waiting for transfers between devices, shifted(): return lax.ppermute(block, axis, route)  19 us
    all_to_all x1, starting transfers between devices, local(): lax.all_to_all(partial_value, 'seq', split_axis=0, concat_axis=0, tiled=T...  16 us
  transfers between devices with their start and end apart: 11, of which 5 were waited for; matrix products, arithmetic and copies ran while one was open for 3% of the time, Pallas kernels for 0%

commit v1 on v0

v1 whole, which is shorter than its diff:
```python
import math

import jax
import jax.numpy as jnp
from jax import lax
from jax.experimental import pallas as pl
from jax.experimental.pallas import tpu as pltpu
from jax.sharding import PartitionSpec as P

HEAD_DIM = 128
BLOCK = 128
WINDOW = 512
TILE = 8

epsilon = 1e-05
masked_score = -1e30
f32 = jnp.float32
bf16 = jnp.bfloat16

VMEM_LIMIT = 40 * 1024 * 1024


def params():
    return pltpu.CompilerParams(vmem_limit_bytes=VMEM_LIMIT)


def vmem():
    return pl.BlockSpec(memory_space=pltpu.VMEM)


def smem():
    return pl.BlockSpec(memory_space=pltpu.SMEM)


def dot(a, b):
    return lax.dot_general(a, b, (((1,), (0,)), ((), ())), preferred_element_type=f32)


def dot_t(a, b):
    return lax.dot_general(a, b, (((1,), (1,)), ((), ())), preferred_element_type=f32)


def attend_kernel(
    place, q, k0, k1, k2, kx0, kx1, kx2, v0, v1, v2, vx0, vx1, vx2, res, out
):
    chip = place[0]
    core = place[1]
    row = lax.broadcasted_iota(jnp.int32, (BLOCK, BLOCK), 0)
    col = lax.broadcasted_iota(jnp.int32, (BLOCK, BLOCK), 1)
    big = jnp.int32(4 * BLOCK)
    shift1 = jnp.where(chip >= 1, 0, big)
    shift2 = jnp.where(chip >= 2, 0, big)
    shiftx = jnp.where((chip >= 2) | (core == 1), 0, big)
    diff = col - row
    visible = jnp.concatenate(
        [
            diff > shift2,
            diff + BLOCK > shiftx,
            diff + BLOCK > shift1,
            diff + BLOCK > shift1,
            diff <= 0,
        ],
        axis=1,
    )
    heads = q.shape[1] // HEAD_DIM
    for h in range(heads):
        s = slice(h * HEAD_DIM, (h + 1) * HEAD_DIM)
        key_all = jnp.concatenate(
            [k2[:, s], kx0[:, s] + kx2[:, s], k1[:, s], kx1[:, s], k0[:, s]], axis=0
        )
        value_all = jnp.concatenate(
            [v2[:, s], vx0[:, s] + vx2[:, s], v1[:, s], vx1[:, s], v0[:, s]], axis=0
        )
        scores = dot_t(q[:, s], key_all) * (1.0 / math.sqrt(HEAD_DIM))
        scores = jnp.where(visible, scores, masked_score)
        top = jnp.max(scores, axis=1, keepdims=True)
        expo = jnp.exp(scores - top)
        weights = (expo * (1.0 / jnp.sum(expo, axis=1, keepdims=True))).astype(bf16)
        attended = dot(weights, value_all)
        stream = res[:, s].astype(f32) + attended
        z_count, core_count = out.shape[0], out.shape[2]
        out[:, h] = stream.reshape(z_count, core_count, TILE, HEAD_DIM).astype(bf16)


def pick_kernel(index, tiles, out):
    @pl.loop(0, out.shape[0], unroll=8)
    def _(i):
        out[i] = tiles[index[i]]


def project_kernel(tiles, gain, gate0, gate1, up0, up1, out, held):
    z_count, heads, slots = tiles.shape[:3]
    rows = z_count * slots * TILE
    squares = jnp.zeros((rows, HEAD_DIM), f32)
    for h in range(heads):
        value = tiles[:, h].astype(f32).reshape(rows, HEAD_DIM)
        squares = squares + value * value
        s = slice(h * HEAD_DIM, (h + 1) * HEAD_DIM)
        held[:, s] = (value * gain[:, s]).astype(bf16)
    high = squares.astype(bf16)
    low = (squares - high.astype(f32)).astype(bf16)
    ones = jnp.ones((TILE, HEAD_DIM), bf16)
    total = dot_t(ones, high) + dot_t(ones, low)
    total_high = total.astype(bf16).astype(f32)
    total_rows = jnp.concatenate([total_high, total - total_high], axis=0).astype(bf16)
    x = held[...]
    parts = out.shape[0]
    for t in range(parts):
        gate = dot(x, jnp.concatenate([gate0[t], gate1[t]], axis=1))
        up = dot(x, jnp.concatenate([up0[t], up1[t]], axis=1))
        width = gate.shape[1]
        out[t, :rows, :width] = gate.astype(bf16)
        out[t, :rows, width:] = up.astype(bf16)
        out[t, rows:, :rows] = total_rows
        out[t, rows:, rows:] = total_rows


def hidden_kernel(features, parts, out):
    count = parts.shape[0]
    rows, width = out.shape
    tail = parts.shape[1] - rows
    sums = parts[:, rows:, :rows].reshape(count * tail, rows)
    weight = jnp.full((count * tail, HEAD_DIM), 1.0 / TILE, bf16)
    square = lax.dot_general(
        sums, weight, (((0,), (0,)), ((), ())), preferred_element_type=f32
    )
    factor = lax.rsqrt(square * (1.0 / features) + epsilon)
    for s in range(0, width, HEAD_DIM):
        gate = sum(parts[t, :rows, s : s + HEAD_DIM].astype(f32) for t in range(count))
        up = sum(
            parts[t, :rows, width + s : width + s + HEAD_DIM].astype(f32) for t in range(count)
        )
        gate = gate * factor
        up = up * factor
        out[:, s : s + HEAD_DIM] = (gate / (1.0 + jnp.exp(-gate)) * up).astype(bf16)


def branch_kernel(hidden, down0, down1, out):
    count = hidden.shape[0]
    half = hidden.shape[2] // 2
    first = jnp.concatenate([hidden[t, :, :half] for t in range(count)], axis=1)
    second = jnp.concatenate([hidden[t, :, half:] for t in range(count)], axis=1)
    z_count, heads, slots = out.shape[:3]
    step = 2 * HEAD_DIM
    for s in range(0, heads * HEAD_DIM, step):
        value = dot(first, down0[:, s : s + step]) + dot(second, down1[:, s : s + step])
        for k in range(0, step, HEAD_DIM):
            part = value[:, k : k + HEAD_DIM].reshape(z_count, slots, TILE, HEAD_DIM)
            out[:, (s + k) // HEAD_DIM] = part.astype(bf16)


def finish_kernel(stream, branch, out):
    z_count, heads, cores = stream.shape[:3]
    for h in range(heads):
        value = stream[:, h].astype(f32) + branch[:, h].astype(f32)
        out[:, h * HEAD_DIM : (h + 1) * HEAD_DIM] = value.reshape(
            z_count * cores * TILE, HEAD_DIM
        ).astype(bf16)


def local(
    queries, keys, values, residual_in, norm_gain, routing, gate_weight, up_weight, down_weight
):
    seq_count = lax.axis_size("seq")
    tp_count = lax.axis_size("tp")
    seq_place = lax.axis_index("seq")
    tp_place = lax.axis_index("tp")
    chips = seq_count // 2
    rows, width = queries.shape
    heads = width // HEAD_DIM
    z_count = rows // (2 * TILE)
    slots = 4

    onward = [(i, i + 2) for i in range(seq_count - 2)]
    to_odd = [(i, i + 1) for i in range(0, seq_count, 2)]
    to_even = [(i + 1, i) for i in range(0, seq_count, 2)]
    swap = to_odd + to_even
    same_core = [[c + 2 * i for i in range(chips)] for c in (0, 1)]

    def move(x, route):
        return lax.ppermute(x, "seq", route)

    k1 = move(keys, onward)
    v1 = move(values, onward)
    k2 = move(k1, onward)
    v2 = move(v1, onward)
    kx0 = move(keys, to_odd)
    vx0 = move(values, to_odd)
    kx1 = move(k1, swap)
    vx1 = move(v1, swap)
    kx2 = move(k2, to_even)
    vx2 = move(v2, to_even)

    def by_features(w):
        w = w[0].reshape(tp_count, width, w.shape[2])
        return lax.all_to_all(w, "tp", 0, 0, tiled=True)

    gate0 = by_features(gate_weight)
    up0 = by_features(up_weight)
    down0 = down_weight[0]
    gate1 = move(gate0, swap)
    up1 = move(up0, swap)
    down1 = move(down0, swap)
    gain = lax.dynamic_slice_in_dim(norm_gain, tp_place * width, width)[None]

    expert = routing[:, 0]
    block_range = jnp.arange(seq_count, dtype=jnp.int32)
    same = expert[None, :] == expert[:, None]
    rank = jnp.sum(same & (block_range[None, :] < block_range[:, None]), axis=1, dtype=jnp.int32)
    slot_of = expert * slots + rank
    slot_range = jnp.arange(chips * slots, dtype=jnp.int32)
    block_of = jnp.sum(
        jnp.where(slot_range[:, None] == slot_of[None, :], block_range[None, :], 0),
        axis=1,
        dtype=jnp.int32,
    )
    place = jnp.stack([seq_place // 2, seq_place % 2]).astype(jnp.int32)

    stream = pl.pallas_call(
        attend_kernel,
        out_shape=jax.ShapeDtypeStruct((z_count, heads, 2, TILE, HEAD_DIM), bf16),
        in_specs=[smem()] + [vmem()] * 14,
        out_specs=vmem(),
        compiler_params=params(),
        name="attend",
    )(place, queries, keys, k1, k2, kx0, kx1, kx2, values, v1, v2, vx0, vx1, vx2, residual_in)

    tiles = lax.all_to_all(
        stream.reshape(seq_count, TILE, HEAD_DIM), "seq", 0, 0, tiled=True
    )

    def pick(index, source):
        return pl.pallas_call(
            pick_kernel,
            out_shape=jax.ShapeDtypeStruct((index.shape[0], TILE, HEAD_DIM), bf16),
            in_specs=[smem(), vmem()],
            out_specs=vmem(),
            compiler_params=params(),
            name="pick",
        )(index, source)

    def same_core_exchange(x):
        x = x.reshape(chips, slots, TILE, HEAD_DIM)
        return lax.all_to_all(x, "seq", 0, 0, tiled=True, axis_index_groups=same_core)

    arrived = same_core_exchange(pick(block_of, tiles))
    arrived = arrived.reshape(z_count, heads, slots, TILE, HEAD_DIM)
    work = z_count * slots * TILE
    hid = 2 * gate0.shape[2]
    parts = pl.pallas_call(
        project_kernel,
        out_shape=jax.ShapeDtypeStruct((tp_count, work + 2 * TILE, 2 * hid), bf16),
        in_specs=[vmem()] * 6,
        out_specs=vmem(),
        scratch_shapes=[pltpu.VMEM((work, width), bf16)],
        compiler_params=params(),
        name="project",
    )(arrived, gain, gate0, gate1, up0, up1)
    parts = lax.all_to_all(parts, "tp", 0, 0, tiled=True)

    def run_hidden(parts_ref, out_ref):
        hidden_kernel(width * tp_count, parts_ref, out_ref)

    hidden = pl.pallas_call(
        run_hidden,
        out_shape=jax.ShapeDtypeStruct((work, hid), bf16),
        in_specs=[vmem()],
        out_specs=vmem(),
        compiler_params=params(),
        name="hidden",
    )(parts)
    hidden = lax.all_gather(hidden, "tp")
    branch = pl.pallas_call(
        branch_kernel,
        out_shape=jax.ShapeDtypeStruct((z_count, heads, slots, TILE, HEAD_DIM), bf16),
        in_specs=[vmem()] * 3,
        out_specs=vmem(),
        compiler_params=params(),
        name="branch",
    )(hidden, down0, down1)
    returned = same_core_exchange(branch).reshape(chips * slots, TILE, HEAD_DIM)
    finished = lax.all_to_all(pick(slot_of, returned), "seq", 0, 0, tiled=True)
    return pl.pallas_call(
        finish_kernel,
        out_shape=jax.ShapeDtypeStruct((rows, width), bf16),
        in_specs=[vmem()] * 2,
        out_specs=vmem(),
        compiler_params=params(),
        name="finish",
    )(stream, finished.reshape(stream.shape))


def solution(mesh):
    in_specs = (
        P("seq", "tp"),
        P("seq", "tp"),
        P("seq", "tp"),
        P("seq", "tp"),
        P(),
        P(),
        P("seq", None, "tp"),
        P("seq", None, "tp"),
        P("seq", None, "tp"),
    )
    out_specs = P("seq", "tp")
    return jax.shard_map(local, mesh=mesh, in_specs=in_specs, out_specs=out_specs, check_vma=False)
```

time: 327 us -> 194 us (0.59)
  waiting for transfers between devices: 112 us -> 28.4 us
  local copies, waits for them, and re-layouts: 24.2 us -> 2.36 us
  Pallas kernels: 0 us -> 15 us
  between operations: 13.8 us -> 0.22 us
  matrix products: 13.1 us -> 0 us
  other arithmetic: 13 us -> 0.36 us
  starting transfers between devices: 80.8 us -> 69.8 us
  blocking collectives: 69.9 us -> 77 us
    all_gather x1 -> x0, waiting for transfers between devices: 47.2 us -> none  [local(): lax.all_gather(lax.all_to_all(outgoing, 'seq', split_axis=0, concat_axis=...]
    ppermute x8 -> x13, waiting for transfers between devices: 19 us -> 0.72 us  [move(): return lax.ppermute(x, 'seq', route)]
    all_to_all x2 -> x4, waiting for transfers between devices: 45.4 us -> 27.7 us  [the longest x1 15 us: same_core_exchange(): lax.all_to_all(x, 'seq', 0, 0, tiled=True, axis_index_groups=same_core)]
    pallas_call x0 -> x7, Pallas kernels: none -> 15 us  [the longest x1 5.54 us: local(): pl.pallas_call(attend_kernel, out_shape=jax.ShapeDtypeStruct((z_count, he...]
    all_to_all x2 -> x4, starting transfers between devices: 42.5 us -> 29.4 us  [the longest x1 16.3 us: local(): lax.all_to_all(stream.reshape(seq_count, TILE, HEAD_DIM), 'seq', 0, 0, ti...]
    unnamed x40 -> x16, local copies, waits for them, and re-layouts: 11.9 us -> 1.67 us
    dot_general x6 -> x0, matrix products: 9.04 us -> none  [the longest x1 3.58 us: local(): jnp.dot(normed, gate_weight[0], preferred_element_type=jnp.float32)]
    reshape x4 -> x0, local copies, waits for them, and re-layouts: 8.86 us -> none  [the longest x1 7.05 us: local(): normed = normed.reshape(-1, normed.shape[3])]
  transfers between devices with their start and end apart: 11 -> 17, of which waited for: 5 -> 4; matrix products, arithmetic and copies ran while one was open for 3% -> 1% of each run, Pallas kernels for 0% -> 5%
where the time goes in v1:
time: 194 us; the launch traced here: 193 us
  blocking collectives  77 us (40%)
  starting transfers between devices  69.8 us (36%)
  waiting for transfers between devices  28.4 us (15%)
  Pallas kernels  15 us (8%)
  local copies, waits for them, and re-layouts  2.36 us (1%)
    ppermute x13, starting transfers between devices, move(): return lax.ppermute(x, 'seq', route)  40.4 us
    all_to_all x1, blocking collectives, local(): finished = lax.all_to_all(pick(slot_of, returned), 'seq', 0, 0, tiled=True)  26.4 us
    all_to_all x1, blocking collectives, same_core_exchange(): lax.all_to_all(x, 'seq', 0, 0, tiled=True, axis_index_groups=same_core)  22.4 us
    all_to_all x1, blocking collectives, local(): parts = lax.all_to_all(parts, 'tp', 0, 0, tiled=True)  17.8 us
    all_to_all x1, starting transfers between devices, local(): lax.all_to_all(stream.reshape(seq_count, TILE, HEAD_DIM), 'seq', 0, 0, ti...  16.3 us
    all_to_all x1, waiting for transfers between devices, same_core_exchange(): lax.all_to_all(x, 'seq', 0, 0, tiled=True, axis_index_groups=same_core)  15 us
    all_gather x1, blocking collectives, local(): hidden = lax.all_gather(hidden, 'tp')  10.5 us
    all_to_all x1, waiting for transfers between devices, local(): lax.all_to_all(stream.reshape(seq_count, TILE, HEAD_DIM), 'seq', 0, 0, ti...  10.2 us
  transfers between devices with their start and end apart: 17, of which 4 were waited for; matrix products, arithmetic and copies ran while one was open for 1% of the time, Pallas kernels for 5%

profile of v1, /device:TPU:1, one launch (start us, length us, event | category | flops | bytes accessed | tf_op | source)
XLA Modules:
  0.0 193.1 jit_solution(15453280754812776708)
XLA Ops:
  0.0 5.0 %all-to-all-start.2 = ((bf16[4,1024,128]{2,1,0:T(8,128)(2,1)}), bf16[4,1024,128]{2,1,0:T(8,128)(2,1)S(1)}, u32[]{:S(2)}, u32[]{:S(2)}) async-start(bf16[4,1024,128]{2,1,0:T(8,128)(2,1)} %bitcast.23), calls=%async_computation.2 | async-start | bytes 2097152 | tf_op jit(solution)/shard_map/all_to_all | solution.py:196
  5.0 3.3 %collective-permute-start = (bf16[128,1024]{1,0:T(8,128)(2,1)S(1)}, bf16[128,1024]{1,0:T(8,128)(2,1)S(1)}, u32[]{:S(2)}, u32[]{:S(2)}) collective-permute-start(bf16[128,1024]{1,0:T(8,128)(2,1)S(1)} %copy-done.2), channel_id=1, source_target_pairs={{0,8},{4,12},{8,16},{12,20},{16,24},{20,28},{24,32},{28,36},{32,40... | collective-permute-start | bytes 786440 | tf_op jit(solution)/shard_map/ppermute | solution.py:181
  8.4 3.9 %collective-permute-start.5 = (bf16[128,1024]{1,0:T(8,128)(2,1)S(1)}, bf16[128,1024]{1,0:T(8,128)(2,1)}, u32[]{:S(2)}, u32[]{:S(2)}) collective-permute-start(bf16[128,1024]{1,0:T(8,128)(2,1)S(1)} %copy-done.3), channel_id=1, source_target_pairs={{0,8},{4,12},{8,16},{12,20},{16,24},{20,28},{24,32},{28,36},{32,40... | collective-permute-start | bytes 786440 | tf_op jit(solution)/shard_map/ppermute | solution.py:181
  12.3 2.5 %all-to-all-done.2.gate0 = bf16[4,1024,128]{2,1,0:T(8,128)(2,1)S(1)} async-done(((bf16[4,1024,128]{2,1,0:T(8,128)(2,1)}), bf16[4,1024,128]{2,1,0:T(8,128)(2,1)S(1)}, u32[]{:S(2)}, u32[]{:S(2)}) %all-to-all-start.2) | async-done | bytes 1048608 | tf_op jit(solution)/shard_map/all_to_all | solution.py:196
  14.7 3.5 %all-to-all-start.3 = ((bf16[4,1024,128]{2,1,0:T(8,128)(2,1)}), bf16[4,1024,128]{2,1,0:T(8,128)(2,1)S(1)}, u32[]{:S(2)}, u32[]{:S(2)}) async-start(bf16[4,1024,128]{2,1,0:T(8,128)(2,1)} %bitcast.24), calls=%async_computation.3 | async-start | bytes 2097152 | tf_op jit(solution)/shard_map/all_to_all | solution.py:196
  19.6 8.3 %collective-permute-start.1 = (bf16[128,1024]{1,0:T(8,128)(2,1)S(1)}, bf16[128,1024]{1,0:T(8,128)(2,1)}, u32[]{:S(2)}, u32[]{:S(2)}) collective-permute-start(bf16[128,1024]{1,0:T(8,128)(2,1)S(1)} %collective-permute-done.k1), channel_id=1, source_target_pairs={{0,8},{4,12},{8,16},{12,20},{16,24},{20,28},{24,32},{28,36},{32,40... | collective-permute-start | bytes 786440 | tf_op jit(solution)/shard_map/ppermute | solution.py:181
  27.9 3.2 %collective-permute-start.6 = (bf16[128,1024]{1,0:T(8,128)(2,1)}, bf16[128,1024]{1,0:T(8,128)(2,1)}, u32[]{:S(2)}, u32[]{:S(2)}) collective-permute-start(bf16[128,1024]{1,0:T(8,128)(2,1)} %collective-permute-done.5.v1), channel_id=1, source_target_pairs={{0,8},{4,12},{8,16},{12,20},{16,24},{20,28},{24,32},{28,36},{32,40... | collective-permute-start | bytes 786440 | tf_op jit(solution)/shard_map/ppermute | solution.py:181
  32.4 5.0 %collective-permute-start.3 = (bf16[128,1024]{1,0:T(8,128)(2,1)S(1)}, bf16[128,1024]{1,0:T(8,128)(2,1)}, u32[]{:S(2)}, u32[]{:S(2)}) collective-permute-start(bf16[128,1024]{1,0:T(8,128)(2,1)S(1)} %collective-permute-done.k1), channel_id=1, source_target_pairs={{0,4},{8,12},{16,20},{24,28},{32,36},{40,44},{48,52},{56,60},{64,6... | collective-permute-start | bytes 786440 | tf_op jit(solution)/shard_map/ppermute | solution.py:181
  40.1 3.1 %collective-permute-start.4 = (bf16[128,1024]{1,0:T(8,128)(2,1)}, bf16[128,1024]{1,0:T(8,128)(2,1)}, u32[]{:S(2)}, u32[]{:S(2)}) collective-permute-start(bf16[128,1024]{1,0:T(8,128)(2,1)} %collective-permute-done.1.k2), channel_id=1, source_target_pairs={{4,0},{12,8},{20,16},{28,24},{36,32},{44,40},{52,48},{60,56},{68,6... | collective-permute-start | bytes 786440 | tf_op jit(solution)/shard_map/ppermute | solution.py:181
  43.2 2.0 %collective-permute-start.9 = (bf16[128,1024]{1,0:T(8,128)(2,1)}, bf16[128,1024]{1,0:T(8,128)(2,1)}, u32[]{:S(2)}, u32[]{:S(2)}) collective-permute-start(bf16[128,1024]{1,0:T(8,128)(2,1)} %collective-permute-done.6.v2), channel_id=1, source_target_pairs={{4,0},{12,8},{20,16},{28,24},{36,32},{44,40},{52,48},{60,56},{68,6... | collective-permute-start | bytes 786440 | tf_op jit(solution)/shard_map/ppermute | solution.py:181
  46.9 5.5 %attend.1.stream = bf16[8,8,2,8,128]{4,3,2,1,0:T(8,128)(2,1)} custom-call(s32[2]{0:T(128)S(1)} %pad_add_fusion.place, bf16[128,1024]{1,0:T(8,128)(2,1)S(1)} %copy-done.1, bf16[128,1024]{1,0:T(8,128)(2,1)S(1)} %copy-done.2, bf16[128,1024]{1,0:T(8,128)(2,1)S(1)} %collective-permute-done.k1, bf16[128,1024]{1,0:T(8,128)(2,1)} %collective-permute-done.1.k2, ...), custom_call_target="tpu_custom_call" | custom-call | tf_op jit(solution)/shard_map/attend/pallas_call | solution.py:219
  52.5 16.3 %all-to-all-start = ((bf16[128,8,128]{2,1,0:T(8,128)(2,1)}), bf16[128,8,128]{2,1,0:T(8,128)(2,1)S(1)}, u32[]{:S(2)}, u32[]{:S(2)}) async-start(bf16[128,8,128]{2,1,0:T(8,128)(2,1)} %bitcast.3), calls=%async_computation | async-start | bytes 524288 | tf_op jit(solution)/shard_map/all_to_all | solution.py:228
  68.9 2.8 %collective-permute-start.11 = (bf16[4,1024,128]{2,1,0:T(8,128)(2,1)S(1)}, bf16[4,1024,128]{2,1,0:T(8,128)(2,1)}, u32[]{:S(2)}, u32[]{:S(2)}) collective-permute-start(bf16[4,1024,128]{2,1,0:T(8,128)(2,1)S(1)} %all-to-all-done.3.up0), channel_id=1, source_target_pairs={{0,4},{8,12},{16,20},{24,28},{32,36},{40,44},{48,52},{56,60},{64,6... | collective-permute-start | bytes 3145736 | tf_op jit(solution)/shard_map/ppermute | solution.py:181
  71.7 1.9 collective-permute-start.10
  73.8 10.2 %all-to-all-done.tiles = bf16[128,8,128]{2,1,0:T(8,128)(2,1)S(1)} async-done(((bf16[128,8,128]{2,1,0:T(8,128)(2,1)}), bf16[128,8,128]{2,1,0:T(8,128)(2,1)S(1)}, u32[]{:S(2)}, u32[]{:S(2)}) %all-to-all-start) | async-done | bytes 262176 | tf_op jit(solution)/shard_map/all_to_all | solution.py:228
  85.8 4.6 %all-to-all-start.1 = ((bf16[64,4,8,128]{3,2,1,0:T(8,128)(2,1)}), bf16[64,4,8,128]{3,2,1,0:T(8,128)(2,1)S(1)}, u32[]{:S(2)}, u32[]{:S(2)}) async-start(bf16[64,4,8,128]{3,2,1,0:T(8,128)(2,1)} %bitcast.4), calls=%async_computation.1 | async-start | bytes 1048576 | tf_op jit(solution)/shard_map/all_to_all | solution.py:244
  90.4 2.3 %collective-permute-start.12 = (bf16[512,1024]{1,0:T(8,128)(2,1)}, bf16[512,1024]{1,0:T(8,128)(2,1)}, u32[]{:S(2)}, u32[]{:S(2)}) collective-permute-start(bf16[512,1024]{1,0:T(8,128)(2,1)} %bitcast.19), channel_id=1, source_target_pairs={{0,4},{8,12},{16,20},{24,28},{32,36},{40,44},{48,52},{56,60},{64,6... | collective-permute-start | bytes 3145736 | tf_op jit(solution)/shard_map/ppermute | solution.py:181
  93.4 15.0 %all-to-all-done.1 = bf16[64,4,8,128]{3,2,1,0:T(8,128)(2,1)S(1)} async-done(((bf16[64,4,8,128]{3,2,1,0:T(8,128)(2,1)}), bf16[64,4,8,128]{3,2,1,0:T(8,128)(2,1)S(1)}, u32[]{:S(2)}, u32[]{:S(2)}) %all-to-all-start.1) | async-done | bytes 524320 | tf_op jit(solution)/shard_map/all_to_all | solution.py:244
  108.4 3.0 %project.1 = bf16[4,272,512]{2,1,0:T(8,128)(2,1)S(1)} custom-call(bf16[8,8,4,8,128]{4,3,2,1,0:T(8,128)(2,1)S(1)} %bitcast.15, f32[1,1024]{1,0:T(1,128)S(1)} %bitcast.22, bf16[4,1024,128]{2,1,0:T(8,128)(2,1)S(1)} %all-to-all-done.2.gate0, bf16[4,1024,128]{2,1,0:T(8,128)(2,1)} %collective-permute-done.10.gate1, bf16[4,1024,128]{2,1,0:T(8,128)(2,1)S(1)} %all-to-all-done.3.up0, ...), custom_call_target="tpu_custom_call" | custom-call | tf_op jit(solution)/shard_map/project/pallas_call | solution.py:250
  111.4 17.8 %all_to_all.35.parts_ref = bf16[4,272,512]{2,1,0:T(8,128)(2,1)S(1)} all-to-all(bf16[4,272,512]{2,1,0:T(8,128)(2,1)S(1)} %project.1), channel_id=1, replica_groups=mesh['seq'=128,'tp'=4] {'tp'}, dimensions={0} | all-to-all | bytes 2228224 | tf_op jit(solution)/shard_map/all_to_all | solution.py:259
  129.5 10.5 %all-gather = bf16[1024,256]{1,0:T(8,128)(2,1)S(1)} all-gather(bf16[256,256]{1,0:T(8,128)(2,1)S(1)} %hidden.1), channel_id=2, replica_groups=mesh['seq'=128,'tp'=4] {'tp'}, dimensions={0}, use_global_device_ids=true | all-gather | bytes 655360 | tf_op jit(solution)/shard_map/all_gather | solution.py:272
  139.9 1.9 %branch.1 = bf16[8,8,4,8,128]{4,3,2,1,0:T(8,128)(2,1)S(1)} custom-call(bf16[4,256,256]{2,1,0:T(8,128)(2,1)S(1)} %bitcast.16, bf16[512,1024]{1,0:T(8,128)(2,1)S(1)} %bitcast.20, bf16[512,1024]{1,0:T(8,128)(2,1)} %collective-permute-done.12.down1), custom_call_target="tpu_custom_call" | custom-call | tf_op jit(solution)/shard_map/branch/pallas_call | solution.py:273
  141.9 22.4 %all_to_all.36 = bf16[64,4,8,128]{3,2,1,0:T(8,128)(2,1)S(1)} all-to-all(bf16[64,4,8,128]{3,2,1,0:T(8,128)(2,1)S(1)} %bitcast.18), channel_id=1, replica_groups={{0,8,16,24,32,40,48,56,64,72,80,88,96,104,112,120,128,136,144,152,160,1..., dimensions={0} | all-to-all | bytes 1048576 | tf_op jit(solution)/shard_map/all_to_all | solution.py:244
  165.0 26.4 %all_to_all.37 = bf16[128,8,128]{2,1,0:T(8,128)(2,1)S(1)} all-to-all(bf16[128,8,128]{2,1,0:T(8,128)(2,1)S(1)} %pick.3), channel_id=1, replica_groups=mesh['seq'=128,'tp'=4] {'seq'}, dimensions={0} | all-to-all | bytes 524288 | tf_op jit(solution)/shard_map/all_to_all | solution.py:282
  (42 shorter events, 12.5 us)
Async XLA Ops:
  0.0 5.0 %copy-start.2 = (bf16[128,1024]{1,0:T(8,128)(2,1)S(1)}, bf16[128,1024]{1,0:T(8,128)(2,1)}, u32[]{:S(2)}) copy-start(bf16[128,1024]{1,0:T(8,128)(2,1)} %k0.1) | copy-start | bytes 786436
  0.0 8.3 %copy-start.3 = (bf16[128,1024]{1,0:T(8,128)(2,1)S(1)}, bf16[128,1024]{1,0:T(8,128)(2,1)}, u32[]{:S(2)}) copy-start(bf16[128,1024]{1,0:T(8,128)(2,1)} %v0.1) | copy-start | bytes 786436
  0.0 14.7 %all-to-all-start.2 = ((bf16[4,1024,128]{2,1,0:T(8,128)(2,1)}), bf16[4,1024,128]{2,1,0:T(8,128)(2,1)S(1)}, u32[]{:S(2)}, u32[]{:S(2)}) async-start(bf16[4,1024,128]{2,1,0:T(8,128)(2,1)} %bitcast.23), calls=%async_computation.2 | async-start | bytes 2097152 | tf_op jit(solution)/shard_map/all_to_all | solution.py:196
  5.0 41.0 %copy-start.1 = (bf16[128,1024]{1,0:T(8,128)(2,1)S(1)}, bf16[128,1024]{1,0:T(8,128)(2,1)}, u32[]{:S(2)}) copy-start(bf16[128,1024]{1,0:T(8,128)(2,1)} %q.1) | copy-start | bytes 786436
  5.0 41.0 %copy-start.4 = (bf16[128,1024]{1,0:T(8,128)(2,1)S(1)}, bf16[128,1024]{1,0:T(8,128)(2,1)}, u32[]{:S(2)}) copy-start(bf16[128,1024]{1,0:T(8,128)(2,1)} %res.1) | copy-start | bytes 786436
  5.0 14.6 %collective-permute-start = (bf16[128,1024]{1,0:T(8,128)(2,1)S(1)}, bf16[128,1024]{1,0:T(8,128)(2,1)S(1)}, u32[]{:S(2)}, u32[]{:S(2)}) collective-permute-start(bf16[128,1024]{1,0:T(8,128)(2,1)S(1)} %copy-done.2), channel_id=1, source_target_pairs={{0,8},{4,12},{8,16},{12,20},{16,24},{20,28},{24,32},{28,36},{32,40... | collective-permute-start | bytes 786440 | tf_op jit(solution)/shard_map/ppermute | solution.py:181
  8.4 19.6 %collective-permute-start.5 = (bf16[128,1024]{1,0:T(8,128)(2,1)S(1)}, bf16[128,1024]{1,0:T(8,128)(2,1)}, u32[]{:S(2)}, u32[]{:S(2)}) collective-permute-start(bf16[128,1024]{1,0:T(8,128)(2,1)S(1)} %copy-done.3), channel_id=1, source_target_pairs={{0,8},{4,12},{8,16},{12,20},{16,24},{20,28},{24,32},{28,36},{32,40... | collective-permute-start | bytes 786440 | tf_op jit(solution)/shard_map/ppermute | solution.py:181
  14.7 37.8 %all-to-all-start.3 = ((bf16[4,1024,128]{2,1,0:T(8,128)(2,1)}), bf16[4,1024,128]{2,1,0:T(8,128)(2,1)S(1)}, u32[]{:S(2)}, u32[]{:S(2)}) async-start(bf16[4,1024,128]{2,1,0:T(8,128)(2,1)} %bitcast.24), calls=%async_computation.3 | async-start | bytes 2097152 | tf_op jit(solution)/shard_map/all_to_all | solution.py:196
  18.2 19.2 %collective-permute-start.2 = (bf16[128,1024]{1,0:T(8,128)(2,1)S(1)}, bf16[128,1024]{1,0:T(8,128)(2,1)S(1)}, u32[]{:S(2)}, u32[]{:S(2)}) collective-permute-start(bf16[128,1024]{1,0:T(8,128)(2,1)S(1)} %copy-done.2), channel_id=1, source_target_pairs={{0,4},{8,12},{16,20},{24,28},{32,36},{40,44},{48,52},{56,60},{64,6... | collective-permute-start | bytes 786440 | tf_op jit(solution)/shard_map/ppermute | solution.py:181
  19.6 20.5 %collective-permute-start.1 = (bf16[128,1024]{1,0:T(8,128)(2,1)S(1)}, bf16[128,1024]{1,0:T(8,128)(2,1)}, u32[]{:S(2)}, u32[]{:S(2)}) collective-permute-start(bf16[128,1024]{1,0:T(8,128)(2,1)S(1)} %collective-permute-done.k1), channel_id=1, source_target_pairs={{0,8},{4,12},{8,16},{12,20},{16,24},{20,28},{24,32},{28,36},{32,40... | collective-permute-start | bytes 786440 | tf_op jit(solution)/shard_map/ppermute | solution.py:181
  27.9 15.3 %collective-permute-start.6 = (bf16[128,1024]{1,0:T(8,128)(2,1)}, bf16[128,1024]{1,0:T(8,128)(2,1)}, u32[]{:S(2)}, u32[]{:S(2)}) collective-permute-start(bf16[128,1024]{1,0:T(8,128)(2,1)} %collective-permute-done.5.v1), channel_id=1, source_target_pairs={{0,8},{4,12},{8,16},{12,20},{16,24},{20,28},{24,32},{28,36},{32,40... | collective-permute-start | bytes 786440 | tf_op jit(solution)/shard_map/ppermute | solution.py:181
  31.1 14.1 %collective-permute-start.7 = (bf16[128,1024]{1,0:T(8,128)(2,1)S(1)}, bf16[128,1024]{1,0:T(8,128)(2,1)}, u32[]{:S(2)}, u32[]{:S(2)}) collective-permute-start(bf16[128,1024]{1,0:T(8,128)(2,1)S(1)} %copy-done.3), channel_id=1, source_target_pairs={{0,4},{8,12},{16,20},{24,28},{32,36},{40,44},{48,52},{56,60},{64,6... | collective-permute-start | bytes 786440 | tf_op jit(solution)/shard_map/ppermute | solution.py:181
  32.4 12.8 %collective-permute-start.3 = (bf16[128,1024]{1,0:T(8,128)(2,1)S(1)}, bf16[128,1024]{1,0:T(8,128)(2,1)}, u32[]{:S(2)}, u32[]{:S(2)}) collective-permute-start(bf16[128,1024]{1,0:T(8,128)(2,1)S(1)} %collective-permute-done.k1), channel_id=1, source_target_pairs={{0,4},{8,12},{16,20},{24,28},{32,36},{40,44},{48,52},{56,60},{64,6... | collective-permute-start | bytes 786440 | tf_op jit(solution)/shard_map/ppermute | solution.py:181
  38.2 7.1 %collective-permute-start.8 = (bf16[128,1024]{1,0:T(8,128)(2,1)}, bf16[128,1024]{1,0:T(8,128)(2,1)}, u32[]{:S(2)}, u32[]{:S(2)}) collective-permute-start(bf16[128,1024]{1,0:T(8,128)(2,1)} %collective-permute-done.5.v1), channel_id=1, source_target_pairs={{0,4},{8,12},{16,20},{24,28},{32,36},{40,44},{48,52},{56,60},{64,6... | collective-permute-start | bytes 786440 | tf_op jit(solution)/shard_map/ppermute | solution.py:181
  40.1 5.2 %collective-permute-start.4 = (bf16[128,1024]{1,0:T(8,128)(2,1)}, bf16[128,1024]{1,0:T(8,128)(2,1)}, u32[]{:S(2)}, u32[]{:S(2)}) collective-permute-start(bf16[128,1024]{1,0:T(8,128)(2,1)} %collective-permute-done.1.k2), channel_id=1, source_target_pairs={{4,0},{12,8},{20,16},{28,24},{36,32},{44,40},{52,48},{60,56},{68,6... | collective-permute-start | bytes 786440 | tf_op jit(solution)/shard_map/ppermute | solution.py:181
  43.2 2.8 %collective-permute-start.9 = (bf16[128,1024]{1,0:T(8,128)(2,1)}, bf16[128,1024]{1,0:T(8,128)(2,1)}, u32[]{:S(2)}, u32[]{:S(2)}) collective-permute-start(bf16[128,1024]{1,0:T(8,128)(2,1)} %collective-permute-done.6.v2), channel_id=1, source_target_pairs={{4,0},{12,8},{20,16},{28,24},{36,32},{44,40},{52,48},{60,56},{68,6... | collective-permute-start | bytes 786440 | tf_op jit(solution)/shard_map/ppermute | solution.py:181
  45.2 23.6 %copy-start.7 = (s32[128,1]{0,1:T(1,128)S(1)}, s32[128,1]{0,1:T(1,128)}, u32[]{:S(2)}) copy-start(s32[128,1]{0,1:T(1,128)} %param.14) | copy-start | bytes 1540
  46.0 1.0 copy-start.6
  52.5 31.5 %all-to-all-start = ((bf16[128,8,128]{2,1,0:T(8,128)(2,1)}), bf16[128,8,128]{2,1,0:T(8,128)(2,1)S(1)}, u32[]{:S(2)}, u32[]{:S(2)}) async-start(bf16[128,8,128]{2,1,0:T(8,128)(2,1)} %bitcast.3), calls=%async_computation | async-start | bytes 524288 | tf_op jit(solution)/shard_map/all_to_all | solution.py:228
  68.9 24.5 %collective-permute-start.11 = (bf16[4,1024,128]{2,1,0:T(8,128)(2,1)S(1)}, bf16[4,1024,128]{2,1,0:T(8,128)(2,1)}, u32[]{:S(2)}, u32[]{:S(2)}) collective-permute-start(bf16[4,1024,128]{2,1,0:T(8,128)(2,1)S(1)} %all-to-all-done.3.up0), channel_id=1, source_target_pairs={{0,4},{8,12},{16,20},{24,28},{32,36},{40,44},{48,52},{56,60},{64,6... | collective-permute-start | bytes 3145736 | tf_op jit(solution)/shard_map/ppermute | solution.py:181
  71.7 21.7 %collective-permute-start.10 = (bf16[4,1024,128]{2,1,0:T(8,128)(2,1)S(1)}, bf16[4,1024,128]{2,1,0:T(8,128)(2,1)}, u32[]{:S(2)}, u32[]{:S(2)}) collective-permute-start(bf16[4,1024,128]{2,1,0:T(8,128)(2,1)S(1)} %all-to-all-done.2.gate0), channel_id=1, source_target_pairs={{0,4},{8,12},{16,20},{24,28},{32,36},{40,44},{48,52},{56,60},{64,6... | collective-permute-start | bytes 3145736 | tf_op jit(solution)/shard_map/ppermute | solution.py:181
  85.8 22.6 %all-to-all-start.1 = ((bf16[64,4,8,128]{3,2,1,0:T(8,128)(2,1)}), bf16[64,4,8,128]{3,2,1,0:T(8,128)(2,1)S(1)}, u32[]{:S(2)}, u32[]{:S(2)}) async-start(bf16[64,4,8,128]{3,2,1,0:T(8,128)(2,1)} %bitcast.4), calls=%async_computation.1 | async-start | bytes 1048576 | tf_op jit(solution)/shard_map/all_to_all | solution.py:244
  90.4 49.5 %collective-permute-start.12 = (bf16[512,1024]{1,0:T(8,128)(2,1)}, bf16[512,1024]{1,0:T(8,128)(2,1)}, u32[]{:S(2)}, u32[]{:S(2)}) collective-permute-start(bf16[512,1024]{1,0:T(8,128)(2,1)} %bitcast.19), channel_id=1, source_target_pairs={{0,4},{8,12},{16,20},{24,28},{32,36},{40,44},{48,52},{56,60},{64,6... | collective-permute-start | bytes 3145736 | tf_op jit(solution)/shard_map/ppermute | solution.py:181
  129.1 10.8 %copy-start = (bf16[1,512,1024]{2,1,0:T(8,128)(2,1)S(1)}, bf16[1,512,1024]{2,1,0:T(8,128)(2,1)}, u32[]{:S(2)}) copy-start(bf16[1,512,1024]{2,1,0:T(8,128)(2,1)} %param.17) | copy-start | bytes 3145732
  (1 other events, 0.7 us)

commit v2 on v1

--- a/solution.py
+++ b/solution.py
@@ -17,7 +17,7 @@
 f32 = jnp.float32
 bf16 = jnp.bfloat16
 
-VMEM_LIMIT = 40 * 1024 * 1024
+VMEM_LIMIT = 14 * 1024 * 1024
 
 
 def params():
@@ -40,45 +40,56 @@
     return lax.dot_general(a, b, (((1,), (1,)), ((), ())), preferred_element_type=f32)
 
 
-def attend_kernel(
-    place, q, k0, k1, k2, kx0, kx1, kx2, v0, v1, v2, vx0, vx1, vx2, res, out
-):
+def attend_near_kernel(place, q, kv0, kv1, kvx1, held, stats):
+    row = lax.broadcasted_iota(jnp.int32, (BLOCK, BLOCK), 0)
+    col = lax.broadcasted_iota(jnp.int32, (BLOCK, BLOCK), 1)
+    diff = col - row
+    shift1 = jnp.where(place[0] >= 1, 0, jnp.int32(4 * BLOCK))
+    past = diff + BLOCK > shift1
+    visible = jnp.concatenate([past, past, diff <= 0], axis=1)
+    tops = jnp.zeros((BLOCK, HEAD_DIM), f32)
+    sums = jnp.zeros((BLOCK, HEAD_DIM), f32)
+    for h in range(q.shape[1] // HEAD_DIM):
+        s = slice(h * HEAD_DIM, (h + 1) * HEAD_DIM)
+        keys = jnp.concatenate([kv[:BLOCK, s] for kv in (kv1, kvx1, kv0)], axis=0)
+        values = jnp.concatenate([kv[BLOCK:, s] for kv in (kv1, kvx1, kv0)], axis=0)
+        scores = dot_t(q[:, s], keys) * (1.0 / math.sqrt(HEAD_DIM))
+        scores = jnp.where(visible, scores, masked_score)
+        top = jnp.max(scores, axis=1, keepdims=True)
+        expo = jnp.exp(scores - top)
+        tops = jnp.where(col == h, top, tops)
+        sums = jnp.where(col == h, jnp.sum(expo, axis=1, keepdims=True), sums)
+        held[:, s] = dot(expo.astype(bf16), values)
+    stats[0] = tops
+    stats[1] = sums
+
+
+def attend_far_kernel(place, q, kv2, kvx0, kvx2, held, stats, res, out, home):
     chip = place[0]
     core = place[1]
     row = lax.broadcasted_iota(jnp.int32, (BLOCK, BLOCK), 0)
     col = lax.broadcasted_iota(jnp.int32, (BLOCK, BLOCK), 1)
+    diff = col - row
     big = jnp.int32(4 * BLOCK)
-    shift1 = jnp.where(chip >= 1, 0, big)
     shift2 = jnp.where(chip >= 2, 0, big)
     shiftx = jnp.where((chip >= 2) | (core == 1), 0, big)
-    diff = col - row
-    visible = jnp.concatenate(
-        [
-            diff > shift2,
-            diff + BLOCK > shiftx,
-            diff + BLOCK > shift1,
-            diff + BLOCK > shift1,
-            diff <= 0,
-        ],
-        axis=1,
-    )
-    heads = q.shape[1] // HEAD_DIM
-    for h in range(heads):
+    visible = jnp.concatenate([diff > shift2, diff + BLOCK > shiftx], axis=1)
+    z_count, core_count = out.shape[0], out.shape[2]
+    for h in range(q.shape[1] // HEAD_DIM):
         s = slice(h * HEAD_DIM, (h + 1) * HEAD_DIM)
-        key_all = jnp.concatenate(
-            [k2[:, s], kx0[:, s] + kx2[:, s], k1[:, s], kx1[:, s], k0[:, s]], axis=0
-        )
-        value_all = jnp.concatenate(
-            [v2[:, s], vx0[:, s] + vx2[:, s], v1[:, s], vx1[:, s], v0[:, s]], axis=0
-        )
-        scores = dot_t(q[:, s], key_all) * (1.0 / math.sqrt(HEAD_DIM))
+        kvx = kvx0[:, s] + kvx2[:, s]
+        keys = jnp.concatenate([kv2[:BLOCK, s], kvx[:BLOCK]], axis=0)
+        values = jnp.concatenate([kv2[BLOCK:, s], kvx[BLOCK:]], axis=0)
+        scores = dot_t(q[:, s], keys) * (1.0 / math.sqrt(HEAD_DIM))
         scores = jnp.where(visible, scores, masked_score)
-        top = jnp.max(scores, axis=1, keepdims=True)
+        near_top = stats[0, :, h : h + 1]
+        top = jnp.maximum(near_top, jnp.max(scores, axis=1, keepdims=True))
         expo = jnp.exp(scores - top)
-        weights = (expo * (1.0 / jnp.sum(expo, axis=1, keepdims=True))).astype(bf16)
-        attended = dot(weights, value_all)
-        stream = res[:, s].astype(f32) + attended
-        z_count, core_count = out.shape[0], out.shape[2]
+        scale = jnp.exp(near_top - top)
+        total = stats[1, :, h : h + 1] * scale + jnp.sum(expo, axis=1, keepdims=True)
+        summed = held[:, s] * scale + dot(expo.astype(bf16), values)
+        stream = res[:, s].astype(f32) + summed * (1.0 / total)
+        home[:, s] = stream.astype(bf16)
         out[:, h] = stream.reshape(z_count, core_count, TILE, HEAD_DIM).astype(bf16)
 
 
@@ -88,7 +99,7 @@
         out[i] = tiles[index[i]]
 
 
-def project_kernel(tiles, gain, gate0, gate1, up0, up1, out, held):
+def project_kernel(tiles, gain, first0, first1, out, held):
     z_count, heads, slots = tiles.shape[:3]
     rows = z_count * slots * TILE
     squares = jnp.zeros((rows, HEAD_DIM), f32)
@@ -106,11 +117,9 @@
     x = held[...]
     parts = out.shape[0]
     for t in range(parts):
-        gate = dot(x, jnp.concatenate([gate0[t], gate1[t]], axis=1))
-        up = dot(x, jnp.concatenate([up0[t], up1[t]], axis=1))
-        width = gate.shape[1]
-        out[t, :rows, :width] = gate.astype(bf16)
-        out[t, :rows, width:] = up.astype(bf16)
+        width = first0.shape[2]
+        out[t, :rows, :width] = dot(x, first0[t]).astype(bf16)
+        out[t, :rows, width:] = dot(x, first1[t]).astype(bf16)
         out[t, rows:, :rows] = total_rows
         out[t, rows:, rows:] = total_rows
 
@@ -125,14 +134,14 @@
         sums, weight, (((0,), (0,)), ((), ())), preferred_element_type=f32
     )
     factor = lax.rsqrt(square * (1.0 / features) + epsilon)
-    for s in range(0, width, HEAD_DIM):
-        gate = sum(parts[t, :rows, s : s + HEAD_DIM].astype(f32) for t in range(count))
-        up = sum(
-            parts[t, :rows, width + s : width + s + HEAD_DIM].astype(f32) for t in range(count)
+    half = width // 2
+    for k in range(2):
+        value = sum(
+            parts[t, :rows, k * width : (k + 1) * width].astype(f32) for t in range(count)
         )
-        gate = gate * factor
-        up = up * factor
-        out[:, s : s + HEAD_DIM] = (gate / (1.0 + jnp.exp(-gate)) * up).astype(bf16)
+        gate = value[:, :half] * factor
+        up = value[:, half:] * factor
+        out[:, k * half : (k + 1) * half] = (gate / (1.0 + jnp.exp(-gate)) * up).astype(bf16)
 
 
 def branch_kernel(hidden, down0, down1, out):
@@ -149,13 +158,11 @@
             out[:, (s + k) // HEAD_DIM] = part.astype(bf16)
 
 
-def finish_kernel(stream, branch, out):
-    z_count, heads, cores = stream.shape[:3]
-    for h in range(heads):
-        value = stream[:, h].astype(f32) + branch[:, h].astype(f32)
-        out[:, h * HEAD_DIM : (h + 1) * HEAD_DIM] = value.reshape(
-            z_count * cores * TILE, HEAD_DIM
-        ).astype(bf16)
+def finish_kernel(home, branch, out):
+    for h in range(branch.shape[1]):
+        s = slice(h * HEAD_DIM, (h + 1) * HEAD_DIM)
+        value = branch[:, h].astype(f32).reshape(home.shape[0], HEAD_DIM)
+        out[:, s] = (home[:, s].astype(f32) + value).astype(bf16)
 
 
 def local(
@@ -180,26 +187,18 @@
     def move(x, route):
         return lax.ppermute(x, "seq", route)
 
-    k1 = move(keys, onward)
-    v1 = move(values, onward)
-    k2 = move(k1, onward)
-    v2 = move(v1, onward)
-    kx0 = move(keys, to_odd)
-    vx0 = move(values, to_odd)
-    kx1 = move(k1, swap)
-    vx1 = move(v1, swap)
-    kx2 = move(k2, to_even)
-    vx2 = move(v2, to_even)
-
-    def by_features(w):
-        w = w[0].reshape(tp_count, width, w.shape[2])
-        return lax.all_to_all(w, "tp", 0, 0, tiled=True)
-
-    gate0 = by_features(gate_weight)
-    up0 = by_features(up_weight)
-    down0 = down_weight[0]
-    gate1 = move(gate0, swap)
-    up1 = move(up0, swap)
+    kv0 = jnp.concatenate([keys, values], axis=0)
+    kv1 = move(kv0, onward)
+    kv2 = move(kv1, onward)
+    kvx0 = move(kv0, to_odd)
+    kvx1 = move(kv1, swap)
+    kvx2 = move(kv2, to_even)
+
+    gate_own, up_own, down0, kvx0 = lax.optimization_barrier(
+        (gate_weight[0], up_weight[0], down_weight[0], kvx0)
+    )
+    both = jnp.concatenate([gate_own, up_own], axis=1).reshape(tp_count, width, -1)
+    first0 = lax.all_to_all(both, "tp", 0, 0, tiled=True)
     down1 = move(down0, swap)
     gain = lax.dynamic_slice_in_dim(norm_gain, tp_place * width, width)[None]
 
@@ -216,14 +215,31 @@
     )
     place = jnp.stack([seq_place // 2, seq_place % 2]).astype(jnp.int32)
 
-    stream = pl.pallas_call(
-        attend_kernel,
-        out_shape=jax.ShapeDtypeStruct((z_count, heads, 2, TILE, HEAD_DIM), bf16),
-        in_specs=[smem()] + [vmem()] * 14,
-        out_specs=vmem(),
-        compiler_params=params(),
-        name="attend",
-    )(place, queries, keys, k1, k2, kx0, kx1, kx2, values, v1, v2, vx0, vx1, vx2, residual_in)
+    held, stats = pl.pallas_call(
+        attend_near_kernel,
+        out_shape=(
+            jax.ShapeDtypeStruct((rows, width), f32),
+            jax.ShapeDtypeStruct((2, BLOCK, HEAD_DIM), f32),
+        ),
+        in_specs=[smem()] + [vmem()] * 4,
+        out_specs=(vmem(), vmem()),
+        compiler_params=params(),
+        name="attend_near",
+    )(place, queries, kv0, kv1, kvx1)
+    place, block_of, slot_of, gain, first0, down1 = lax.optimization_barrier(
+        (place, block_of, slot_of, gain, first0, down1)
+    )
+    stream, home = pl.pallas_call(
+        attend_far_kernel,
+        out_shape=(
+            jax.ShapeDtypeStruct((z_count, heads, 2, TILE, HEAD_DIM), bf16),
+            jax.ShapeDtypeStruct((rows, width), bf16),
+        ),
+        in_specs=[smem()] + [vmem()] * 7,
+        out_specs=(vmem(), vmem()),
+        compiler_params=params(),
+        name="attend_far",
+    )(place, queries, kv2, kvx0, kvx2, held, stats, residual_in)
 
     tiles = lax.all_to_all(
         stream.reshape(seq_count, TILE, HEAD_DIM), "seq", 0, 0, tiled=True
@@ -243,19 +259,21 @@
         x = x.reshape(chips, slots, TILE, HEAD_DIM)
         return lax.all_to_all(x, "seq", 0, 0, tiled=True, axis_index_groups=same_core)
 
+    tiles, first0 = lax.optimization_barrier((tiles, first0))
+    first1 = move(first0, swap)
     arrived = same_core_exchange(pick(block_of, tiles))
     arrived = arrived.reshape(z_count, heads, slots, TILE, HEAD_DIM)
     work = z_count * slots * TILE
-    hid = 2 * gate0.shape[2]
+    hid = first0.shape[2]
     parts = pl.pallas_call(
         project_kernel,
         out_shape=jax.ShapeDtypeStruct((tp_count, work + 2 * TILE, 2 * hid), bf16),
-        in_specs=[vmem()] * 6,
+        in_specs=[vmem()] * 4,
         out_specs=vmem(),
         scratch_shapes=[pltpu.VMEM((work, width), bf16)],
         compiler_params=params(),
         name="project",
-    )(arrived, gain, gate0, gate1, up0, up1)
+    )(arrived, gain, first0, first1)
     parts = lax.all_to_all(parts, "tp", 0, 0, tiled=True)
 
     def run_hidden(parts_ref, out_ref):
@@ -287,7 +305,7 @@
         out_specs=vmem(),
         compiler_params=params(),
         name="finish",
-    )(stream, finished.reshape(stream.shape))
+    )(home, finished.reshape(stream.shape))
 
 
 def solution(mesh):

time: 194 us -> 191 us (0.985)
  blocking collectives: 77 us -> 132 us
  starting transfers between devices: 69.8 us -> 28.7 us
  waiting for transfers between devices: 28.4 us -> 7.28 us
  other arithmetic: 0.36 us -> 3.47 us
  local copies, waits for them, and re-layouts: 2.36 us -> 5.42 us
    all_to_all x0 -> x1, blocking collectives: none -> 32.6 us  [local(): lax.all_to_all(stream.reshape(seq_count, TILE, HEAD_DIM), 'seq', 0, 0, ti...]
    all_to_all x4 -> x1, starting transfers between devices: 29.4 us -> 3.74 us  [local(): first0 = lax.all_to_all(both, 'tp', 0, 0, tiled=True)]
    all_to_all x4 -> x1, waiting for transfers between devices: 27.7 us -> 3.84 us  [local(): first0 = lax.all_to_all(both, 'tp', 0, 0, tiled=True)]
    all_to_all x1 -> x2, blocking collectives: 22.4 us -> 44.6 us  [same_core_exchange(): lax.all_to_all(x, 'seq', 0, 0, tiled=True, axis_index_groups=same_core)]
    ppermute x13 -> x7, starting transfers between devices: 40.4 us -> 25 us  [move(): return lax.ppermute(x, 'seq', route)]
    concatenate x0 -> x1, other arithmetic: none -> 3.1 us  [local(): jnp.concatenate([gate_own, up_own], axis=1).reshape(tp_count, width, -1)]
    ppermute x13 -> x7, waiting for transfers between devices: 0.72 us -> 3.44 us  [move(): return lax.ppermute(x, 'seq', route)]
    unnamed x16 -> x13, local copies, waits for them, and re-layouts: 1.67 us -> 3.76 us
  transfers between devices with their start and end apart: 17 -> 8, of which waited for: 4 -> 2; matrix products, arithmetic and copies ran while one was open for 1% -> 2% of each run, Pallas kernels for 5% -> 2%
where the time goes in v2:
time: 191 us; the launch traced here: 190 us
  blocking collectives  132 us (69%)
  starting transfers between devices  28.7 us (15%)
  Pallas kernels  13.4 us (7%)
  waiting for transfers between devices  7.28 us (4%)
  local copies, waits for them, and re-layouts  5.42 us (3%)
  other arithmetic  3.47 us (2%)
    all_to_all x2, blocking collectives, same_core_exchange(): lax.all_to_all(x, 'seq', 0, 0, tiled=True, axis_index_groups=same_core)  44.6 us
    all_to_all x1, blocking collectives, local(): lax.all_to_all(stream.reshape(seq_count, TILE, HEAD_DIM), 'seq', 0, 0, ti...  32.6 us
    all_to_all x1, blocking collectives, local(): finished = lax.all_to_all(pick(slot_of, returned), 'seq', 0, 0, tiled=True)  26.4 us
    ppermute x7, starting transfers between devices, move(): return lax.ppermute(x, 'seq', route)  25 us
    all_to_all x1, blocking collectives, local(): parts = lax.all_to_all(parts, 'tp', 0, 0, tiled=True)  17.7 us
    all_gather x1, blocking collectives, local(): hidden = lax.all_gather(hidden, 'tp')  10.4 us
    pallas_call x1, Pallas kernels, local(): pl.pallas_call(attend_far_kernel, out_shape=(jax.ShapeDtypeStruct((z_coun...  3.94 us
    all_to_all x1, waiting for transfers between devices, local(): first0 = lax.all_to_all(both, 'tp', 0, 0, tiled=True)  3.84 us
  transfers between devices with their start and end apart: 8, of which 2 were waited for; matrix products, arithmetic and copies ran while one was open for 2% of the time, Pallas kernels for 2%

profile of v2, /device:TPU:1, one launch (start us, length us, event | category | flops | bytes accessed | tf_op | source)
XLA Modules:
  0.0 190.2 jit_solution(9080783279859542443)
XLA Ops:
  1.0 1.0 constant_dynamic-update-slice_fusion.kv0
  1.9 1.3 collective-permute-start
  3.2 4.8 %collective-permute-start.2 = (bf16[256,1024]{1,0:T(8,128)(2,1)S(1)}, bf16[256,1024]{1,0:T(8,128)(2,1)}, u32[]{:S(2)}, u32[]{:S(2)}) collective-permute-start(bf16[256,1024]{1,0:T(8,128)(2,1)S(1)} %constant_dynamic-update-slice_fusion.kv0), channel_id=1, source_target_pairs={{0,8},{4,12},{8,16},{12,20},{16,24},{20,28},{24,32},{28,36},{32,40... | collective-permute-start | bytes 1572872 | tf_op jit(solution)/shard_map/ppermute | solution.py:188
  8.1 3.4 %collective-permute-done.kvx0 = bf16[256,1024]{1,0:T(8,128)(2,1)S(1)} collective-permute-done((bf16[256,1024]{1,0:T(8,128)(2,1)S(1)}, bf16[256,1024]{1,0:T(8,128)(2,1)S(1)}, u32[]{:S(2)}, u32[]{:S(2)}) %collective-permute-start) | collective-permute-done | bytes 524320 | tf_op jit(solution)/shard_map/ppermute | solution.py:188
  11.5 3.1 %pad_maximum_fusion = bf16[4096,256]{1,0:T(8,128)(2,1)} fusion(bf16[4096,128]{1,0:T(8,128)(2,1)} %bitcast.27, bf16[4096,128]{1,0:T(8,128)(2,1)} %bitcast.28), kind=kLoop, calls=%fused_computation | loop fusion | flops 4194304 | bytes 4194304 | tf_op jit(solution)/shard_map/concatenate | solution.py:200
  14.6 3.7 %all-to-all-start = ((bf16[4,1024,256]{2,1,0:T(8,128)(2,1)}), bf16[4,1024,256]{2,1,0:T(8,128)(2,1)S(1)}, u32[]{:S(2)}, u32[]{:S(2)}) async-start(bf16[4,1024,256]{2,1,0:T(8,128)(2,1)} %bitcast.26), calls=%async_computation | async-start | bytes 4194304 | tf_op jit(solution)/shard_map/all_to_all | solution.py:201
  18.4 3.0 %collective-permute-start.3 = (bf16[256,1024]{1,0:T(8,128)(2,1)}, bf16[256,1024]{1,0:T(8,128)(2,1)}, u32[]{:S(2)}, u32[]{:S(2)}) collective-permute-start(bf16[256,1024]{1,0:T(8,128)(2,1)} %collective-permute-done.2.kv1), channel_id=1, source_target_pairs={{0,8},{4,12},{8,16},{12,20},{16,24},{20,28},{24,32},{28,36},{32,40... | collective-permute-start | bytes 1572872 | tf_op jit(solution)/shard_map/ppermute | solution.py:188
  21.3 5.3 %collective-permute-start.1 = (bf16[512,1024]{1,0:T(8,128)(2,1)}, bf16[512,1024]{1,0:T(8,128)(2,1)}, u32[]{:S(2)}, u32[]{:S(2)}) collective-permute-start(bf16[512,1024]{1,0:T(8,128)(2,1)} %bitcast.21), channel_id=1, source_target_pairs={{0,4},{8,12},{16,20},{24,28},{32,36},{40,44},{48,52},{56,60},{64,6... | collective-permute-start | bytes 3145736 | tf_op jit(solution)/shard_map/ppermute | solution.py:188
  27.3 1.9 %collective-permute-start.5 = (bf16[256,1024]{1,0:T(8,128)(2,1)}, bf16[256,1024]{1,0:T(8,128)(2,1)S(1)}, u32[]{:S(2)}, u32[]{:S(2)}) collective-permute-start(bf16[256,1024]{1,0:T(8,128)(2,1)} %collective-permute-done.2.kv1), channel_id=1, source_target_pairs={{0,4},{8,12},{16,20},{24,28},{32,36},{40,44},{48,52},{56,60},{64,6... | collective-permute-start | bytes 1572872 | tf_op jit(solution)/shard_map/ppermute | solution.py:188
  29.3 6.4 %collective-permute-start.4 = (bf16[256,1024]{1,0:T(8,128)(2,1)}, bf16[256,1024]{1,0:T(8,128)(2,1)}, u32[]{:S(2)}, u32[]{:S(2)}) collective-permute-start(bf16[256,1024]{1,0:T(8,128)(2,1)} %collective-permute-done.3.kv2), channel_id=1, source_target_pairs={{4,0},{12,8},{20,16},{28,24},{36,32},{44,40},{52,48},{60,56},{68,6... | collective-permute-start | bytes 1572872 | tf_op jit(solution)/shard_map/ppermute | solution.py:188
  36.1 3.3 %attend_near.1 = (f32[128,1024]{1,0:T(8,128)S(1)}, f32[2,128,128]{2,1,0:T(8,128)S(1)}) custom-call(s32[2]{0:T(128)S(1)} %pad_add_fusion.place, bf16[128,1024]{1,0:T(8,128)(2,1)S(1)} %copy-done.1, bf16[256,1024]{1,0:T(8,128)(2,1)S(1)} %constant_dynamic-update-slice_fusion.kv0, bf16[256,1024]{1,0:T(8,128)(2,1)} %collective-permute-done.2.kv1, ...), custom_call_target="tpu_custom_call" | custom-call | tf_op jit(solution)/shard_map/attend_near/pallas_call | solution.py:218
  40.1 3.8 %all-to-all-done.first0 = bf16[4,1024,256]{2,1,0:T(8,128)(2,1)S(1)} async-done(((bf16[4,1024,256]{2,1,0:T(8,128)(2,1)}), bf16[4,1024,256]{2,1,0:T(8,128)(2,1)S(1)}, u32[]{:S(2)}, u32[]{:S(2)}) %all-to-all-start) | async-done | bytes 2097184 | tf_op jit(solution)/shard_map/all_to_all | solution.py:201
  44.0 1.0 copy-done.3
  46.0 3.9 %attend_far.1 = (bf16[8,8,2,8,128]{4,3,2,1,0:T(8,128)(2,1)S(1)}, bf16[128,1024]{1,0:T(8,128)(2,1)S(1)}) custom-call(s32[2]{0:T(128)S(1)} %pad_add_fusion.place, bf16[128,1024]{1,0:T(8,128)(2,1)S(1)} %copy-done.1, bf16[256,1024]{1,0:T(8,128)(2,1)} %collective-permute-done.3.kv2, bf16[256,1024]{1,0:T(8,128)(2,1)S(1)} %collective-permute-done.kvx0, ...), custom_call_target="tpu_custom_call" | custom-call | tf_op jit(solution)/shard_map/attend_far/pallas_call | solution.py:232
  49.9 32.6 %all_to_all.30.tiles = bf16[128,8,128]{2,1,0:T(8,128)(2,1)S(1)} all-to-all(bf16[128,8,128]{2,1,0:T(8,128)(2,1)S(1)} %bitcast.24), channel_id=1, replica_groups=mesh['seq'=128,'tp'=4] {'seq'}, dimensions={0} | all-to-all | bytes 524288 | tf_op jit(solution)/shard_map/all_to_all | solution.py:244
  82.5 2.3 %collective-permute-start.6 = (bf16[4,1024,256]{2,1,0:T(8,128)(2,1)S(1)}, bf16[4,1024,256]{2,1,0:T(8,128)(2,1)S(1)}, u32[]{:S(2)}, u32[]{:S(2)}) collective-permute-start(bf16[4,1024,256]{2,1,0:T(8,128)(2,1)S(1)} %all-to-all-done.first0), channel_id=1, source_target_pairs={{0,4},{8,12},{16,20},{24,28},{32,36},{40,44},{48,52},{56,60},{64,6... | collective-permute-start | bytes 6291464 | tf_op jit(solution)/shard_map/ppermute | solution.py:188
  84.8 1.0 pick.2
  85.8 21.9 %all_to_all.31 = bf16[64,4,8,128]{3,2,1,0:T(8,128)(2,1)S(1)} all-to-all(bf16[64,4,8,128]{3,2,1,0:T(8,128)(2,1)S(1)} %bitcast.17), channel_id=1, replica_groups={{0,8,16,24,32,40,48,56,64,72,80,88,96,104,112,120,128,136,144,152,160,1..., dimensions={0} | all-to-all | bytes 1048576 | tf_op jit(solution)/shard_map/all_to_all | solution.py:260
  107.7 1.4 project.1
  109.1 17.7 %all_to_all.32.parts_ref = bf16[4,272,512]{2,1,0:T(8,128)(2,1)S(1)} all-to-all(bf16[4,272,512]{2,1,0:T(8,128)(2,1)S(1)} %project.1), channel_id=1, replica_groups=mesh['seq'=128,'tp'=4] {'tp'}, dimensions={0} | all-to-all | bytes 2228224 | tf_op jit(solution)/shard_map/all_to_all | solution.py:277
  127.2 10.4 %all-gather = bf16[1024,256]{1,0:T(8,128)(2,1)S(1)} all-gather(bf16[256,256]{1,0:T(8,128)(2,1)S(1)} %hidden.1), channel_id=2, replica_groups=mesh['seq'=128,'tp'=4] {'tp'}, dimensions={0}, use_global_device_ids=true | all-gather | bytes 655360 | tf_op jit(solution)/shard_map/all_gather | solution.py:290
  137.6 1.9 %branch.1 = bf16[8,8,4,8,128]{4,3,2,1,0:T(8,128)(2,1)S(1)} custom-call(bf16[4,256,256]{2,1,0:T(8,128)(2,1)S(1)} %bitcast.18, bf16[512,1024]{1,0:T(8,128)(2,1)S(1)} %bitcast.22, bf16[512,1024]{1,0:T(8,128)(2,1)} %collective-permute-done.1.down1), custom_call_target="tpu_custom_call" | custom-call | tf_op jit(solution)/shard_map/branch/pallas_call | solution.py:291
  139.6 22.7 %all_to_all.33 = bf16[64,4,8,128]{3,2,1,0:T(8,128)(2,1)S(1)} all-to-all(bf16[64,4,8,128]{3,2,1,0:T(8,128)(2,1)S(1)} %bitcast.20), channel_id=1, replica_groups={{0,8,16,24,32,40,48,56,64,72,80,88,96,104,112,120,128,136,144,152,160,1..., dimensions={0} | all-to-all | bytes 1048576 | tf_op jit(solution)/shard_map/all_to_all | solution.py:260
  163.0 26.4 %all_to_all.34 = bf16[128,8,128]{2,1,0:T(8,128)(2,1)S(1)} all-to-all(bf16[128,8,128]{2,1,0:T(8,128)(2,1)S(1)} %pick.3), channel_id=1, replica_groups=mesh['seq'=128,'tp'=4] {'seq'}, dimensions={0} | all-to-all | bytes 524288 | tf_op jit(solution)/shard_map/all_to_all | solution.py:300
  (26 shorter events, 5.7 us)
Async XLA Ops:
  1.9 9.6 %collective-permute-start = (bf16[256,1024]{1,0:T(8,128)(2,1)S(1)}, bf16[256,1024]{1,0:T(8,128)(2,1)S(1)}, u32[]{:S(2)}, u32[]{:S(2)}) collective-permute-start(bf16[256,1024]{1,0:T(8,128)(2,1)S(1)} %constant_dynamic-update-slice_fusion.kv0), channel_id=1, source_target_pairs={{0,4},{8,12},{16,20},{24,28},{32,36},{40,44},{48,52},{56,60},{64,6... | collective-permute-start | bytes 1572872 | tf_op jit(solution)/shard_map/ppermute | solution.py:188
  3.2 15.1 %collective-permute-start.2 = (bf16[256,1024]{1,0:T(8,128)(2,1)S(1)}, bf16[256,1024]{1,0:T(8,128)(2,1)}, u32[]{:S(2)}, u32[]{:S(2)}) collective-permute-start(bf16[256,1024]{1,0:T(8,128)(2,1)S(1)} %constant_dynamic-update-slice_fusion.kv0), channel_id=1, source_target_pairs={{0,8},{4,12},{8,16},{12,20},{16,24},{20,28},{24,32},{28,36},{32,40... | collective-permute-start | bytes 1572872 | tf_op jit(solution)/shard_map/ppermute | solution.py:188
  14.6 21.1 %copy-start.5 = (s32[128,1]{0,1:T(1,128)S(1)}, s32[128,1]{0,1:T(1,128)}, u32[]{:S(2)}) copy-start(s32[128,1]{0,1:T(1,128)} %param.14) | copy-start | bytes 1540
  14.6 21.5 %copy-start.1 = (bf16[128,1024]{1,0:T(8,128)(2,1)S(1)}, bf16[128,1024]{1,0:T(8,128)(2,1)}, u32[]{:S(2)}) copy-start(bf16[128,1024]{1,0:T(8,128)(2,1)} %q.3) | copy-start | bytes 786436
  14.6 29.4 %all-to-all-start = ((bf16[4,1024,256]{2,1,0:T(8,128)(2,1)}), bf16[4,1024,256]{2,1,0:T(8,128)(2,1)S(1)}, u32[]{:S(2)}, u32[]{:S(2)}) async-start(bf16[4,1024,256]{2,1,0:T(8,128)(2,1)} %bitcast.26), calls=%async_computation | async-start | bytes 4194304 | tf_op jit(solution)/shard_map/all_to_all | solution.py:201
  18.4 10.9 %collective-permute-start.3 = (bf16[256,1024]{1,0:T(8,128)(2,1)}, bf16[256,1024]{1,0:T(8,128)(2,1)}, u32[]{:S(2)}, u32[]{:S(2)}) collective-permute-start(bf16[256,1024]{1,0:T(8,128)(2,1)} %collective-permute-done.2.kv1), channel_id=1, source_target_pairs={{0,8},{4,12},{8,16},{12,20},{16,24},{20,28},{24,32},{28,36},{32,40... | collective-permute-start | bytes 1572872 | tf_op jit(solution)/shard_map/ppermute | solution.py:188
  21.3 18.8 %collective-permute-start.1 = (bf16[512,1024]{1,0:T(8,128)(2,1)}, bf16[512,1024]{1,0:T(8,128)(2,1)}, u32[]{:S(2)}, u32[]{:S(2)}) collective-permute-start(bf16[512,1024]{1,0:T(8,128)(2,1)} %bitcast.21), channel_id=1, source_target_pairs={{0,4},{8,12},{16,20},{24,28},{32,36},{40,44},{48,52},{56,60},{64,6... | collective-permute-start | bytes 3145736 | tf_op jit(solution)/shard_map/ppermute | solution.py:188
  27.3 8.7 %collective-permute-start.5 = (bf16[256,1024]{1,0:T(8,128)(2,1)}, bf16[256,1024]{1,0:T(8,128)(2,1)S(1)}, u32[]{:S(2)}, u32[]{:S(2)}) collective-permute-start(bf16[256,1024]{1,0:T(8,128)(2,1)} %collective-permute-done.2.kv1), channel_id=1, source_target_pairs={{0,4},{8,12},{16,20},{24,28},{32,36},{40,44},{48,52},{56,60},{64,6... | collective-permute-start | bytes 1572872 | tf_op jit(solution)/shard_map/ppermute | solution.py:188
  29.3 14.7 %collective-permute-start.4 = (bf16[256,1024]{1,0:T(8,128)(2,1)}, bf16[256,1024]{1,0:T(8,128)(2,1)}, u32[]{:S(2)}, u32[]{:S(2)}) collective-permute-start(bf16[256,1024]{1,0:T(8,128)(2,1)} %collective-permute-done.3.kv2), channel_id=1, source_target_pairs={{4,0},{12,8},{20,16},{28,24},{36,32},{44,40},{52,48},{60,56},{68,6... | collective-permute-start | bytes 1572872 | tf_op jit(solution)/shard_map/ppermute | solution.py:188
  39.3 0.8 copy-start.2
  44.0 1.0 copy-start.3
  45.0 0.9 copy-start.4
  82.5 25.2 %collective-permute-start.6 = (bf16[4,1024,256]{2,1,0:T(8,128)(2,1)S(1)}, bf16[4,1024,256]{2,1,0:T(8,128)(2,1)S(1)}, u32[]{:S(2)}, u32[]{:S(2)}) collective-permute-start(bf16[4,1024,256]{2,1,0:T(8,128)(2,1)S(1)} %all-to-all-done.first0), channel_id=1, source_target_pairs={{0,4},{8,12},{16,20},{24,28},{32,36},{40,44},{48,52},{56,60},{64,6... | collective-permute-start | bytes 6291464 | tf_op jit(solution)/shard_map/ppermute | solution.py:188
  109.1 28.5 %copy-start = (bf16[1,512,1024]{2,1,0:T(8,128)(2,1)S(1)}, bf16[1,512,1024]{2,1,0:T(8,128)(2,1)}, u32[]{:S(2)}) copy-start(bf16[1,512,1024]{2,1,0:T(8,128)(2,1)} %param.17) | copy-start | bytes 3145732

commit v3 on v2

--- a/solution.py
+++ b/solution.py
@@ -32,6 +32,10 @@
     return pl.BlockSpec(memory_space=pltpu.SMEM)
 
 
+def anywhere():
+    return pl.BlockSpec(memory_space=pl.ANY)
+
+
 def dot(a, b):
     return lax.dot_general(a, b, (((1,), (0,)), ((), ())), preferred_element_type=f32)
 
@@ -40,7 +44,7 @@
     return lax.dot_general(a, b, (((1,), (1,)), ((), ())), preferred_element_type=f32)
 
 
-def attend_near_kernel(place, q, kv0, kv1, kvx1, held, stats):
+def attend_near_kernel(place, q, kv0, kv1, kvx1, _, held, stats):
     row = lax.broadcasted_iota(jnp.int32, (BLOCK, BLOCK), 0)
     col = lax.broadcasted_iota(jnp.int32, (BLOCK, BLOCK), 1)
     diff = col - row
@@ -64,7 +68,15 @@
     stats[1] = sums
 
 
-def attend_far_kernel(place, q, kv2, kvx0, kvx2, held, stats, res, out, home):
+def attend_far_kernel(place, *refs):
+    given, (out, home), scratch, sems = refs[:7], refs[7:9], refs[9:16], refs[16]
+    copies = [
+        pltpu.make_async_copy(source, target, sems.at[i])
+        for i, (source, target) in enumerate(zip(given, scratch))
+    ]
+    for copy in copies:
+        copy.start()
+    q, kv2, kvx0, kvx2, held, stats, res = scratch
     chip = place[0]
     core = place[1]
     row = lax.broadcasted_iota(jnp.int32, (BLOCK, BLOCK), 0)
@@ -74,6 +86,8 @@
     shift2 = jnp.where(chip >= 2, 0, big)
     shiftx = jnp.where((chip >= 2) | (core == 1), 0, big)
     visible = jnp.concatenate([diff > shift2, diff + BLOCK > shiftx], axis=1)
+    for copy in copies:
+        copy.wait()
     z_count, core_count = out.shape[0], out.shape[2]
     for h in range(q.shape[1] // HEAD_DIM):
         s = slice(h * HEAD_DIM, (h + 1) * HEAD_DIM)
@@ -194,8 +208,8 @@
     kvx1 = move(kv1, swap)
     kvx2 = move(kv2, to_even)
 
-    gate_own, up_own, down0, kvx0 = lax.optimization_barrier(
-        (gate_weight[0], up_weight[0], down_weight[0], kvx0)
+    gate_own, up_own, down0, kv0 = lax.optimization_barrier(
+        (gate_weight[0], up_weight[0], down_weight[0], kv0)
     )
     both = jnp.concatenate([gate_own, up_own], axis=1).reshape(tp_count, width, -1)
     first0 = lax.all_to_all(both, "tp", 0, 0, tiled=True)
@@ -215,28 +229,40 @@
     )
     place = jnp.stack([seq_place // 2, seq_place % 2]).astype(jnp.int32)
 
+    place, block_of, slot_of, gain, first0, down1 = lax.optimization_barrier(
+        (place, block_of, slot_of, gain, first0, down1)
+    )
     held, stats = pl.pallas_call(
         attend_near_kernel,
         out_shape=(
             jax.ShapeDtypeStruct((rows, width), f32),
             jax.ShapeDtypeStruct((2, BLOCK, HEAD_DIM), f32),
         ),
-        in_specs=[smem()] + [vmem()] * 4,
+        in_specs=[smem()] + [vmem()] * 5,
         out_specs=(vmem(), vmem()),
         compiler_params=params(),
         name="attend_near",
-    )(place, queries, kv0, kv1, kvx1)
-    place, block_of, slot_of, gain, first0, down1 = lax.optimization_barrier(
-        (place, block_of, slot_of, gain, first0, down1)
-    )
+    )(place, queries, kv0, kv1, kvx1, residual_in)
+    pair = pltpu.VMEM((2 * rows, width), bf16)
+    single = pltpu.VMEM((rows, width), bf16)
     stream, home = pl.pallas_call(
         attend_far_kernel,
         out_shape=(
             jax.ShapeDtypeStruct((z_count, heads, 2, TILE, HEAD_DIM), bf16),
             jax.ShapeDtypeStruct((rows, width), bf16),
         ),
-        in_specs=[smem()] + [vmem()] * 7,
+        in_specs=[smem()] + [anywhere()] * 7,
         out_specs=(vmem(), vmem()),
+        scratch_shapes=[
+            single,
+            pair,
+            pair,
+            pair,
+            pltpu.VMEM((rows, width), f32),
+            pltpu.VMEM((2, BLOCK, HEAD_DIM), f32),
+            single,
+            pltpu.SemaphoreType.DMA((7,)),
+        ],
         compiler_params=params(),
         name="attend_far",
     )(place, queries, kv2, kvx0, kvx2, held, stats, residual_in)

time: 191 us -> 188 us (0.984)
  waiting for transfers between devices: 7.28 us -> 1.43 us
  local copies, waits for them, and re-layouts: 5.42 us -> 2.65 us
  starting transfers between devices: 28.7 us -> 31.3 us
  blocking collectives: 132 us -> 134 us
    ppermute x7, waiting for transfers between devices: 3.44 us -> 0.02 us  [move(): return lax.ppermute(x, 'seq', route)]
    unnamed x13 -> x9, local copies, waits for them, and re-layouts: 3.76 us -> 0.98 us
    all_to_all x1, blocking collectives: 32.6 us -> 35 us  [local(): lax.all_to_all(stream.reshape(seq_count, TILE, HEAD_DIM), 'seq', 0, 0, ti...]
    all_to_all x1, waiting for transfers between devices: 3.84 us -> 1.41 us  [local(): first0 = lax.all_to_all(both, 'tp', 0, 0, tiled=True)]
    ppermute x7, starting transfers between devices: 25 us -> 27.2 us  [move(): return lax.ppermute(x, 'seq', route)]
  transfers between devices with their start and end apart: 8 -> 8, of which waited for: 2 -> 1; matrix products, arithmetic and copies ran while one was open for 2% -> 2% of each run, Pallas kernels for 2% -> 2%
where the time goes in v3:
time: 188 us
  blocking collectives  134 us (71%)
  starting transfers between devices  31.3 us (17%)
  Pallas kernels  14.4 us (8%)
  other arithmetic  3.48 us (2%)
  local copies, waits for them, and re-layouts  2.65 us (1%)
    all_to_all x2, blocking collectives, same_core_exchange(): lax.all_to_all(x, 'seq', 0, 0, tiled=True, axis_index_groups=same_core)  44.6 us
    all_to_all x1, blocking collectives, local(): lax.all_to_all(stream.reshape(seq_count, TILE, HEAD_DIM), 'seq', 0, 0, ti...  35 us
    ppermute x7, starting transfers between devices, move(): return lax.ppermute(x, 'seq', route)  27.2 us
    all_to_all x1, blocking collectives, local(): finished = lax.all_to_all(pick(slot_of, returned), 'seq', 0, 0, tiled=True)  26.4 us
    all_to_all x1, blocking collectives, local(): parts = lax.all_to_all(parts, 'tp', 0, 0, tiled=True)  17.7 us
    all_gather x1, blocking collectives, local(): hidden = lax.all_gather(hidden, 'tp')  10.4 us
    pallas_call x1, Pallas kernels, local(): pl.pallas_call(attend_far_kernel, out_shape=(jax.ShapeDtypeStruct((z_coun...  4.81 us
    all_to_all x1, starting transfers between devices, local(): first0 = lax.all_to_all(both, 'tp', 0, 0, tiled=True)  4.14 us
  transfers between devices with their start and end apart: 8, of which 1 were waited for; matrix products, arithmetic and copies ran while one was open for 2% of the time, Pallas kernels for 2%

profile of v3, /device:TPU:1, one launch (start us, length us, event | category | flops | bytes accessed | tf_op | source)
XLA Modules:
  0.0 187.7 jit_solution(1657397168349179665)
XLA Ops:
  0.0 1.0 constant_dynamic-update-slice_fusion.1
  1.0 1.0 constant_dynamic-update-slice_fusion.kv0
  1.9 4.8 %collective-permute-start.1 = (bf16[256,1024]{1,0:T(8,128)(2,1)S(1)}, bf16[256,1024]{1,0:T(8,128)(2,1)}, u32[]{:S(2)}, u32[]{:S(2)}) collective-permute-start(bf16[256,1024]{1,0:T(8,128)(2,1)S(1)} %constant_dynamic-update-slice_fusion.kv0), channel_id=1, source_target_pairs={{0,8},{4,12},{8,16},{12,20},{16,24},{20,28},{24,32},{28,36},{32,40... | collective-permute-start | bytes 1572872 | tf_op jit(solution)/shard_map/ppermute | solution.py:202
  6.8 3.1 %pad_maximum_fusion = bf16[4096,256]{1,0:T(8,128)(2,1)} fusion(bf16[4096,128]{1,0:T(8,128)(2,1)} %bitcast.27, bf16[4096,128]{1,0:T(8,128)(2,1)} %bitcast.28), kind=kLoop, calls=%fused_computation | loop fusion | flops 4194304 | bytes 4194304 | tf_op jit(solution)/shard_map/concatenate | solution.py:214
  9.9 4.1 %all-to-all-start = ((bf16[4,1024,256]{2,1,0:T(8,128)(2,1)}), bf16[4,1024,256]{2,1,0:T(8,128)(2,1)S(1)}, u32[]{:S(2)}, u32[]{:S(2)}) async-start(bf16[4,1024,256]{2,1,0:T(8,128)(2,1)} %bitcast.26), calls=%async_computation | async-start | bytes 4194304 | tf_op jit(solution)/shard_map/all_to_all | solution.py:215
  14.0 6.5 %collective-permute-start.2 = (bf16[256,1024]{1,0:T(8,128)(2,1)}, bf16[256,1024]{1,0:T(8,128)(2,1)}, u32[]{:S(2)}, u32[]{:S(2)}) collective-permute-start(bf16[256,1024]{1,0:T(8,128)(2,1)} %collective-permute-done.1.kv1), channel_id=1, source_target_pairs={{0,8},{4,12},{8,16},{12,20},{16,24},{20,28},{24,32},{28,36},{32,40... | collective-permute-start | bytes 1572872 | tf_op jit(solution)/shard_map/ppermute | solution.py:202
  20.5 4.7 %collective-permute-start = (bf16[512,1024]{1,0:T(8,128)(2,1)}, bf16[512,1024]{1,0:T(8,128)(2,1)}, u32[]{:S(2)}, u32[]{:S(2)}) collective-permute-start(bf16[512,1024]{1,0:T(8,128)(2,1)} %bitcast.21), channel_id=1, source_target_pairs={{0,4},{8,12},{16,20},{24,28},{32,36},{40,44},{48,52},{56,60},{64,6... | collective-permute-start | bytes 3145736 | tf_op jit(solution)/shard_map/ppermute | solution.py:202
  25.3 1.3 collective-permute-start.3
  27.3 3.8 %collective-permute-start.5 = (bf16[256,1024]{1,0:T(8,128)(2,1)}, bf16[256,1024]{1,0:T(8,128)(2,1)}, u32[]{:S(2)}, u32[]{:S(2)}) collective-permute-start(bf16[256,1024]{1,0:T(8,128)(2,1)} %collective-permute-done.1.kv1), channel_id=1, source_target_pairs={{0,4},{8,12},{16,20},{24,28},{32,36},{40,44},{48,52},{56,60},{64,6... | collective-permute-start | bytes 1572872 | tf_op jit(solution)/shard_map/ppermute | solution.py:202
  31.1 3.8 %collective-permute-start.4 = (bf16[256,1024]{1,0:T(8,128)(2,1)}, bf16[256,1024]{1,0:T(8,128)(2,1)}, u32[]{:S(2)}, u32[]{:S(2)}) collective-permute-start(bf16[256,1024]{1,0:T(8,128)(2,1)} %collective-permute-done.2.refs_1_), channel_id=1, source_target_pairs={{4,0},{12,8},{20,16},{28,24},{36,32},{44,40},{52,48},{60,56},{68,6... | collective-permute-start | bytes 1572872 | tf_op jit(solution)/shard_map/ppermute | solution.py:202
  35.3 1.4 all-to-all-done.first0
  36.7 3.4 %attend_near.1 = (f32[128,1024]{1,0:T(8,128)S(1)}, f32[2,128,128]{2,1,0:T(8,128)S(1)}) custom-call(s32[2]{0:T(128)S(1)} %pad_add_fusion.place, bf16[128,1024]{1,0:T(8,128)(2,1)S(1)} %copy-done.1, bf16[256,1024]{1,0:T(8,128)(2,1)S(1)} %constant_dynamic-update-slice_fusion.kv0, bf16[256,1024]{1,0:T(8,128)(2,1)} %collective-permute-done.1.kv1, ...), custom_call_target="tpu_custom_call" | custom-call | tf_op jit(solution)/shard_map/attend_near/pallas_call | solution.py:235
  40.2 4.8 %attend_far.1 = (bf16[8,8,2,8,128]{4,3,2,1,0:T(8,128)(2,1)S(1)}, bf16[128,1024]{1,0:T(8,128)(2,1)S(1)}) custom-call(s32[2]{0:T(128)S(1)} %pad_add_fusion.place, bf16[128,1024]{1,0:T(8,128)(2,1)S(1)} %copy-done.1, bf16[256,1024]{1,0:T(8,128)(2,1)} %collective-permute-done.2.refs_1_, bf16[256,1024]{1,0:T(8,128)(2,1)} %collective-permute-done.3.refs_2_, ...), custom_call_target="tpu_custom_call" | custom-call | tf_op jit(solution)/shard_map/attend_far/pallas_call | solution.py:248
  45.0 35.0 %all_to_all.30.tiles = bf16[128,8,128]{2,1,0:T(8,128)(2,1)S(1)} all-to-all(bf16[128,8,128]{2,1,0:T(8,128)(2,1)S(1)} %bitcast.24), channel_id=1, replica_groups=mesh['seq'=128,'tp'=4] {'seq'}, dimensions={0} | all-to-all | bytes 524288 | tf_op jit(solution)/shard_map/all_to_all | solution.py:270
  80.0 2.3 %collective-permute-start.6 = (bf16[4,1024,256]{2,1,0:T(8,128)(2,1)S(1)}, bf16[4,1024,256]{2,1,0:T(8,128)(2,1)S(1)}, u32[]{:S(2)}, u32[]{:S(2)}) collective-permute-start(bf16[4,1024,256]{2,1,0:T(8,128)(2,1)S(1)} %all-to-all-done.first0), channel_id=1, source_target_pairs={{0,4},{8,12},{16,20},{24,28},{32,36},{40,44},{48,52},{56,60},{64,6... | collective-permute-start | bytes 6291464 | tf_op jit(solution)/shard_map/ppermute | solution.py:202
  82.3 1.0 pick.2
  83.3 21.9 %all_to_all.31 = bf16[64,4,8,128]{3,2,1,0:T(8,128)(2,1)S(1)} all-to-all(bf16[64,4,8,128]{3,2,1,0:T(8,128)(2,1)S(1)} %bitcast.17), channel_id=1, replica_groups={{0,8,16,24,32,40,48,56,64,72,80,88,96,104,112,120,128,136,144,152,160,1..., dimensions={0} | all-to-all | bytes 1048576 | tf_op jit(solution)/shard_map/all_to_all | solution.py:286
  105.2 1.4 project.1
  106.6 17.7 %all_to_all.32.parts_ref = bf16[4,272,512]{2,1,0:T(8,128)(2,1)S(1)} all-to-all(bf16[4,272,512]{2,1,0:T(8,128)(2,1)S(1)} %project.1), channel_id=1, replica_groups=mesh['seq'=128,'tp'=4] {'tp'}, dimensions={0} | all-to-all | bytes 2228224 | tf_op jit(solution)/shard_map/all_to_all | solution.py:303
  124.7 10.4 %all-gather = bf16[1024,256]{1,0:T(8,128)(2,1)S(1)} all-gather(bf16[256,256]{1,0:T(8,128)(2,1)S(1)} %hidden.1), channel_id=2, replica_groups=mesh['seq'=128,'tp'=4] {'tp'}, dimensions={0}, use_global_device_ids=true | all-gather | bytes 655360 | tf_op jit(solution)/shard_map/all_gather | solution.py:316
  135.1 1.9 %branch.1 = bf16[8,8,4,8,128]{4,3,2,1,0:T(8,128)(2,1)S(1)} custom-call(bf16[4,256,256]{2,1,0:T(8,128)(2,1)S(1)} %bitcast.18, bf16[512,1024]{1,0:T(8,128)(2,1)S(1)} %bitcast.22, bf16[512,1024]{1,0:T(8,128)(2,1)} %collective-permute-done.down1), custom_call_target="tpu_custom_call" | custom-call | tf_op jit(solution)/shard_map/branch/pallas_call | solution.py:317
  137.1 22.7 %all_to_all.33 = bf16[64,4,8,128]{3,2,1,0:T(8,128)(2,1)S(1)} all-to-all(bf16[64,4,8,128]{3,2,1,0:T(8,128)(2,1)S(1)} %bitcast.20), channel_id=1, replica_groups={{0,8,16,24,32,40,48,56,64,72,80,88,96,104,112,120,128,136,144,152,160,1..., dimensions={0} | all-to-all | bytes 1048576 | tf_op jit(solution)/shard_map/all_to_all | solution.py:286
  160.5 26.4 %all_to_all.34 = bf16[128,8,128]{2,1,0:T(8,128)(2,1)S(1)} all-to-all(bf16[128,8,128]{2,1,0:T(8,128)(2,1)S(1)} %pick.3), channel_id=1, replica_groups=mesh['seq'=128,'tp'=4] {'seq'}, dimensions={0} | all-to-all | bytes 524288 | tf_op jit(solution)/shard_map/all_to_all | solution.py:326
  187.0 0.8 finish.1
  (22 shorter events, 2.2 us)
Async XLA Ops:
  1.9 12.1 %collective-permute-start.1 = (bf16[256,1024]{1,0:T(8,128)(2,1)S(1)}, bf16[256,1024]{1,0:T(8,128)(2,1)}, u32[]{:S(2)}, u32[]{:S(2)}) collective-permute-start(bf16[256,1024]{1,0:T(8,128)(2,1)S(1)} %constant_dynamic-update-slice_fusion.kv0), channel_id=1, source_target_pairs={{0,8},{4,12},{8,16},{12,20},{16,24},{20,28},{24,32},{28,36},{32,40... | collective-permute-start | bytes 1572872 | tf_op jit(solution)/shard_map/ppermute | solution.py:202
  9.9 25.1 %copy-start.3 = (s32[128,1]{0,1:T(1,128)S(1)}, s32[128,1]{0,1:T(1,128)}, u32[]{:S(2)}) copy-start(s32[128,1]{0,1:T(1,128)} %param.14) | copy-start | bytes 1540
  9.9 26.8 %copy-start.1 = (bf16[128,1024]{1,0:T(8,128)(2,1)S(1)}, bf16[128,1024]{1,0:T(8,128)(2,1)}, u32[]{:S(2)}) copy-start(bf16[128,1024]{1,0:T(8,128)(2,1)} %refs_0_.1) | copy-start | bytes 786436
  9.9 26.8 %copy-start.2 = (bf16[128,1024]{1,0:T(8,128)(2,1)S(1)}, bf16[128,1024]{1,0:T(8,128)(2,1)}, u32[]{:S(2)}) copy-start(bf16[128,1024]{1,0:T(8,128)(2,1)} %refs_6_.1) | copy-start | bytes 786436
  9.9 26.8 %all-to-all-start = ((bf16[4,1024,256]{2,1,0:T(8,128)(2,1)}), bf16[4,1024,256]{2,1,0:T(8,128)(2,1)S(1)}, u32[]{:S(2)}, u32[]{:S(2)}) async-start(bf16[4,1024,256]{2,1,0:T(8,128)(2,1)} %bitcast.26), calls=%async_computation | async-start | bytes 4194304 | tf_op jit(solution)/shard_map/all_to_all | solution.py:215
  14.0 17.1 %collective-permute-start.2 = (bf16[256,1024]{1,0:T(8,128)(2,1)}, bf16[256,1024]{1,0:T(8,128)(2,1)}, u32[]{:S(2)}, u32[]{:S(2)}) collective-permute-start(bf16[256,1024]{1,0:T(8,128)(2,1)} %collective-permute-done.1.kv1), channel_id=1, source_target_pairs={{0,8},{4,12},{8,16},{12,20},{16,24},{20,28},{24,32},{28,36},{32,40... | collective-permute-start | bytes 1572872 | tf_op jit(solution)/shard_map/ppermute | solution.py:202
  20.5 14.7 %collective-permute-start = (bf16[512,1024]{1,0:T(8,128)(2,1)}, bf16[512,1024]{1,0:T(8,128)(2,1)}, u32[]{:S(2)}, u32[]{:S(2)}) collective-permute-start(bf16[512,1024]{1,0:T(8,128)(2,1)} %bitcast.21), channel_id=1, source_target_pairs={{0,4},{8,12},{16,20},{24,28},{32,36},{40,44},{48,52},{56,60},{64,6... | collective-permute-start | bytes 3145736 | tf_op jit(solution)/shard_map/ppermute | solution.py:202
  25.3 14.8 %collective-permute-start.3 = (bf16[256,1024]{1,0:T(8,128)(2,1)S(1)}, bf16[256,1024]{1,0:T(8,128)(2,1)}, u32[]{:S(2)}, u32[]{:S(2)}) collective-permute-start(bf16[256,1024]{1,0:T(8,128)(2,1)S(1)} %constant_dynamic-update-slice_fusion.kv0), channel_id=1, source_target_pairs={{0,4},{8,12},{16,20},{24,28},{32,36},{40,44},{48,52},{56,60},{64,6... | collective-permute-start | bytes 1572872 | tf_op jit(solution)/shard_map/ppermute | solution.py:202
  27.3 9.4 %collective-permute-start.5 = (bf16[256,1024]{1,0:T(8,128)(2,1)}, bf16[256,1024]{1,0:T(8,128)(2,1)}, u32[]{:S(2)}, u32[]{:S(2)}) collective-permute-start(bf16[256,1024]{1,0:T(8,128)(2,1)} %collective-permute-done.1.kv1), channel_id=1, source_target_pairs={{0,4},{8,12},{16,20},{24,28},{32,36},{40,44},{48,52},{56,60},{64,6... | collective-permute-start | bytes 1572872 | tf_op jit(solution)/shard_map/ppermute | solution.py:202
  31.1 9.0 %collective-permute-start.4 = (bf16[256,1024]{1,0:T(8,128)(2,1)}, bf16[256,1024]{1,0:T(8,128)(2,1)}, u32[]{:S(2)}, u32[]{:S(2)}) collective-permute-start(bf16[256,1024]{1,0:T(8,128)(2,1)} %collective-permute-done.2.refs_1_), channel_id=1, source_target_pairs={{4,0},{12,8},{20,16},{28,24},{36,32},{44,40},{52,48},{60,56},{68,6... | collective-permute-start | bytes 1572872 | tf_op jit(solution)/shard_map/ppermute | solution.py:202
  80.0 25.2 %collective-permute-start.6 = (bf16[4,1024,256]{2,1,0:T(8,128)(2,1)S(1)}, bf16[4,1024,256]{2,1,0:T(8,128)(2,1)S(1)}, u32[]{:S(2)}, u32[]{:S(2)}) collective-permute-start(bf16[4,1024,256]{2,1,0:T(8,128)(2,1)S(1)} %all-to-all-done.first0), channel_id=1, source_target_pairs={{0,4},{8,12},{16,20},{24,28},{32,36},{40,44},{48,52},{56,60},{64,6... | collective-permute-start | bytes 6291464 | tf_op jit(solution)/shard_map/ppermute | solution.py:202
  106.6 28.5 %copy-start = (bf16[1,512,1024]{2,1,0:T(8,128)(2,1)S(1)}, bf16[1,512,1024]{2,1,0:T(8,128)(2,1)}, u32[]{:S(2)}) copy-start(bf16[1,512,1024]{2,1,0:T(8,128)(2,1)} %param.17) | copy-start | bytes 3145732

commit v4 on v2

--- a/solution.py
+++ b/solution.py
@@ -40,7 +40,7 @@
     return lax.dot_general(a, b, (((1,), (1,)), ((), ())), preferred_element_type=f32)
 
 
-def attend_near_kernel(place, q, kv0, kv1, kvx1, held, stats):
+def attend_near_kernel(place, q, kv0, kv1, kvx1, _, held, stats):
     row = lax.broadcasted_iota(jnp.int32, (BLOCK, BLOCK), 0)
     col = lax.broadcasted_iota(jnp.int32, (BLOCK, BLOCK), 1)
     diff = col - row
@@ -192,10 +192,9 @@
     kv2 = move(kv1, onward)
     kvx0 = move(kv0, to_odd)
     kvx1 = move(kv1, swap)
-    kvx2 = move(kv2, to_even)
-
-    gate_own, up_own, down0, kvx0 = lax.optimization_barrier(
-        (gate_weight[0], up_weight[0], down_weight[0], kvx0)
+
+    gate_own, up_own, down0, kv0 = lax.optimization_barrier(
+        (gate_weight[0], up_weight[0], down_weight[0], kv0)
     )
     both = jnp.concatenate([gate_own, up_own], axis=1).reshape(tp_count, width, -1)
     first0 = lax.all_to_all(both, "tp", 0, 0, tiled=True)
@@ -215,20 +214,20 @@
     )
     place = jnp.stack([seq_place // 2, seq_place % 2]).astype(jnp.int32)
 
+    place, block_of, slot_of, gain = lax.optimization_barrier((place, block_of, slot_of, gain))
     held, stats = pl.pallas_call(
         attend_near_kernel,
         out_shape=(
             jax.ShapeDtypeStruct((rows, width), f32),
             jax.ShapeDtypeStruct((2, BLOCK, HEAD_DIM), f32),
         ),
-        in_specs=[smem()] + [vmem()] * 4,
+        in_specs=[smem()] + [vmem()] * 5,
         out_specs=(vmem(), vmem()),
         compiler_params=params(),
         name="attend_near",
-    )(place, queries, kv0, kv1, kvx1)
-    place, block_of, slot_of, gain, first0, down1 = lax.optimization_barrier(
-        (place, block_of, slot_of, gain, first0, down1)
-    )
+    )(place, queries, kv0, kv1, kvx1, residual_in)
+    kv2, held, stats = lax.optimization_barrier((kv2, held, stats))
+    kvx2 = move(kv2, to_even)
     stream, home = pl.pallas_call(
         attend_far_kernel,
         out_shape=(
@@ -240,6 +239,7 @@
         compiler_params=params(),
         name="attend_far",
     )(place, queries, kv2, kvx0, kvx2, held, stats, residual_in)
+    stream, first0, down1 = lax.optimization_barrier((stream, first0, down1))
 
     tiles = lax.all_to_all(
         stream.reshape(seq_count, TILE, HEAD_DIM), "seq", 0, 0, tiled=True

time: 191 us -> 188 us (0.984)
  starting transfers between devices: 28.7 us -> 25.1 us
  local copies, waits for them, and re-layouts: 5.42 us -> 2.65 us
  waiting for transfers between devices: 7.28 us -> 9.21 us
    ppermute x7, waiting for transfers between devices: 3.44 us -> 9.21 us  [move(): return lax.ppermute(x, 'seq', route)]
    ppermute x7, starting transfers between devices: 25 us -> 21 us  [move(): return lax.ppermute(x, 'seq', route)]
    all_to_all x1, waiting for transfers between devices: 3.84 us -> 0.01 us  [local(): first0 = lax.all_to_all(both, 'tp', 0, 0, tiled=True)]
    unnamed x13 -> x9, local copies, waits for them, and re-layouts: 3.76 us -> 0.98 us
  transfers between devices with their start and end apart: 8 -> 8, of which waited for: 2 -> 3; matrix products, arithmetic and copies ran while one was open for 2% -> 2% of each run, Pallas kernels for 2% -> 4%
where the time goes in v4:
time: 188 us; the launch traced here: 187 us
  blocking collectives  133 us (71%)
  starting transfers between devices  25.1 us (13%)
  Pallas kernels  13.2 us (7%)
  waiting for transfers between devices  9.21 us (5%)
  other arithmetic  3.48 us (2%)
  local copies, waits for them, and re-layouts  2.65 us (1%)
    all_to_all x2, blocking collectives, same_core_exchange(): lax.all_to_all(x, 'seq', 0, 0, tiled=True, axis_index_groups=same_core)  44.6 us
    all_to_all x1, blocking collectives, local(): lax.all_to_all(stream.reshape(seq_count, TILE, HEAD_DIM), 'seq', 0, 0, ti...  34.1 us
    all_to_all x1, blocking collectives, local(): finished = lax.all_to_all(pick(slot_of, returned), 'seq', 0, 0, tiled=True)  26.4 us
    ppermute x7, starting transfers between devices, move(): return lax.ppermute(x, 'seq', route)  21 us
    all_to_all x1, blocking collectives, local(): parts = lax.all_to_all(parts, 'tp', 0, 0, tiled=True)  17.7 us
    all_gather x1, blocking collectives, local(): hidden = lax.all_gather(hidden, 'tp')  10.4 us
    ppermute x7, waiting for transfers between devices, move(): return lax.ppermute(x, 'seq', route)  9.21 us
    all_to_all x1, starting transfers between devices, local(): first0 = lax.all_to_all(both, 'tp', 0, 0, tiled=True)  4.14 us
  transfers between devices with their start and end apart: 8, of which 3 were waited for; matrix products, arithmetic and copies ran while one was open for 2% of the time, Pallas kernels for 4%

profile of v4, /device:TPU:1, one launch (start us, length us, event | category | flops | bytes accessed | tf_op | source)
XLA Modules:
  0.0 187.2 jit_solution(2823143641872390516)
XLA Ops:
  0.0 1.0 constant_dynamic-update-slice_fusion.1
  1.0 1.0 constant_dynamic-update-slice_fusion.kv0
  1.9 4.8 %collective-permute-start = (bf16[256,1024]{1,0:T(8,128)(2,1)S(1)}, bf16[256,1024]{1,0:T(8,128)(2,1)}, u32[]{:S(2)}, u32[]{:S(2)}) collective-permute-start(bf16[256,1024]{1,0:T(8,128)(2,1)S(1)} %constant_dynamic-update-slice_fusion.kv0), channel_id=1, source_target_pairs={{0,8},{4,12},{8,16},{12,20},{16,24},{20,28},{24,32},{28,36},{32,40... | collective-permute-start | bytes 1572872 | tf_op jit(solution)/shard_map/ppermute | solution.py:188
  6.8 3.1 %pad_maximum_fusion = bf16[4096,256]{1,0:T(8,128)(2,1)} fusion(bf16[4096,128]{1,0:T(8,128)(2,1)} %bitcast.27, bf16[4096,128]{1,0:T(8,128)(2,1)} %bitcast.28), kind=kLoop, calls=%fused_computation | loop fusion | flops 4194304 | bytes 4194304 | tf_op jit(solution)/shard_map/concatenate | solution.py:199
  9.9 4.1 %all-to-all-start = ((bf16[4,1024,256]{2,1,0:T(8,128)(2,1)}), bf16[4,1024,256]{2,1,0:T(8,128)(2,1)S(1)}, u32[]{:S(2)}, u32[]{:S(2)}) async-start(bf16[4,1024,256]{2,1,0:T(8,128)(2,1)} %bitcast.26), calls=%async_computation | async-start | bytes 4194304 | tf_op jit(solution)/shard_map/all_to_all | solution.py:200
  14.0 1.3 collective-permute-start.3
  15.3 6.4 %collective-permute-start.5 = (bf16[512,1024]{1,0:T(8,128)(2,1)}, bf16[512,1024]{1,0:T(8,128)(2,1)}, u32[]{:S(2)}, u32[]{:S(2)}) collective-permute-start(bf16[512,1024]{1,0:T(8,128)(2,1)} %bitcast.21), channel_id=1, source_target_pairs={{0,4},{8,12},{16,20},{24,28},{32,36},{40,44},{48,52},{56,60},{64,6... | collective-permute-start | bytes 3145736 | tf_op jit(solution)/shard_map/ppermute | solution.py:188
  22.5 1.9 %collective-permute-start.2 = (bf16[256,1024]{1,0:T(8,128)(2,1)}, bf16[256,1024]{1,0:T(8,128)(2,1)S(1)}, u32[]{:S(2)}, u32[]{:S(2)}) collective-permute-start(bf16[256,1024]{1,0:T(8,128)(2,1)} %collective-permute-done.kv1), channel_id=1, source_target_pairs={{0,4},{8,12},{16,20},{24,28},{32,36},{40,44},{48,52},{56,60},{64,6... | collective-permute-start | bytes 1572872 | tf_op jit(solution)/shard_map/ppermute | solution.py:188
  24.4 1.3 collective-permute-start.1
  26.5 3.3 %attend_near.1 = (f32[128,1024]{1,0:T(8,128)S(1)}, f32[2,128,128]{2,1,0:T(8,128)S(1)}) custom-call(s32[2]{0:T(128)S(1)} %pad_add_fusion.place, bf16[128,1024]{1,0:T(8,128)(2,1)S(1)} %copy-done.1, bf16[256,1024]{1,0:T(8,128)(2,1)S(1)} %constant_dynamic-update-slice_fusion.kv0, bf16[256,1024]{1,0:T(8,128)(2,1)} %collective-permute-done.kv1, ...), custom_call_target="tpu_custom_call" | custom-call | tf_op jit(solution)/shard_map/attend_near/pallas_call | solution.py:218
  29.8 7.4 %collective-permute-done.1.kv2 = bf16[256,1024]{1,0:T(8,128)(2,1)S(1)} collective-permute-done((bf16[256,1024]{1,0:T(8,128)(2,1)}, bf16[256,1024]{1,0:T(8,128)(2,1)S(1)}, u32[]{:S(2)}, u32[]{:S(2)}) %collective-permute-start.1) | collective-permute-done | bytes 524320 | tf_op jit(solution)/shard_map/ppermute | solution.py:188
  37.1 2.9 %collective-permute-start.4 = (bf16[256,1024]{1,0:T(8,128)(2,1)S(1)}, bf16[256,1024]{1,0:T(8,128)(2,1)S(1)}, u32[]{:S(2)}, u32[]{:S(2)}) collective-permute-start(bf16[256,1024]{1,0:T(8,128)(2,1)S(1)} %collective-permute-done.1.kv2), channel_id=1, source_target_pairs={{4,0},{12,8},{20,16},{28,24},{36,32},{44,40},{52,48},{60,56},{68,6... | collective-permute-start | bytes 1572872 | tf_op jit(solution)/shard_map/ppermute | solution.py:188
  40.1 1.5 collective-permute-done.4.kvx2
  41.6 3.8 %attend_far.1 = (bf16[8,8,2,8,128]{4,3,2,1,0:T(8,128)(2,1)S(1)}, bf16[128,1024]{1,0:T(8,128)(2,1)S(1)}) custom-call(s32[2]{0:T(128)S(1)} %pad_add_fusion.place, bf16[128,1024]{1,0:T(8,128)(2,1)S(1)} %copy-done.1, bf16[256,1024]{1,0:T(8,128)(2,1)S(1)} %collective-permute-done.1.kv2, bf16[256,1024]{1,0:T(8,128)(2,1)} %collective-permute-done.3.kvx0, ...), custom_call_target="tpu_custom_call" | custom-call | tf_op jit(solution)/shard_map/attend_far/pallas_call | solution.py:231
  45.4 34.1 %all_to_all.30.tiles = bf16[128,8,128]{2,1,0:T(8,128)(2,1)S(1)} all-to-all(bf16[128,8,128]{2,1,0:T(8,128)(2,1)S(1)} %bitcast.24), channel_id=1, replica_groups=mesh['seq'=128,'tp'=4] {'seq'}, dimensions={0} | all-to-all | bytes 524288 | tf_op jit(solution)/shard_map/all_to_all | solution.py:244
  79.5 2.3 %collective-permute-start.6 = (bf16[4,1024,256]{2,1,0:T(8,128)(2,1)S(1)}, bf16[4,1024,256]{2,1,0:T(8,128)(2,1)S(1)}, u32[]{:S(2)}, u32[]{:S(2)}) collective-permute-start(bf16[4,1024,256]{2,1,0:T(8,128)(2,1)S(1)} %all-to-all-done.first0), channel_id=1, source_target_pairs={{0,4},{8,12},{16,20},{24,28},{32,36},{40,44},{48,52},{56,60},{64,6... | collective-permute-start | bytes 6291464 | tf_op jit(solution)/shard_map/ppermute | solution.py:188
  81.7 1.0 pick.2
  82.7 21.9 %all_to_all.31 = bf16[64,4,8,128]{3,2,1,0:T(8,128)(2,1)S(1)} all-to-all(bf16[64,4,8,128]{3,2,1,0:T(8,128)(2,1)S(1)} %bitcast.17), channel_id=1, replica_groups={{0,8,16,24,32,40,48,56,64,72,80,88,96,104,112,120,128,136,144,152,160,1..., dimensions={0} | all-to-all | bytes 1048576 | tf_op jit(solution)/shard_map/all_to_all | solution.py:260
  104.7 1.4 project.1
  106.1 17.7 %all_to_all.32.parts_ref = bf16[4,272,512]{2,1,0:T(8,128)(2,1)S(1)} all-to-all(bf16[4,272,512]{2,1,0:T(8,128)(2,1)S(1)} %project.1), channel_id=1, replica_groups=mesh['seq'=128,'tp'=4] {'tp'}, dimensions={0} | all-to-all | bytes 2228224 | tf_op jit(solution)/shard_map/all_to_all | solution.py:277
  124.2 10.4 %all-gather = bf16[1024,256]{1,0:T(8,128)(2,1)S(1)} all-gather(bf16[256,256]{1,0:T(8,128)(2,1)S(1)} %hidden.1), channel_id=2, replica_groups=mesh['seq'=128,'tp'=4] {'tp'}, dimensions={0}, use_global_device_ids=true | all-gather | bytes 655360 | tf_op jit(solution)/shard_map/all_gather | solution.py:290
  134.6 1.9 %branch.1 = bf16[8,8,4,8,128]{4,3,2,1,0:T(8,128)(2,1)S(1)} custom-call(bf16[4,256,256]{2,1,0:T(8,128)(2,1)S(1)} %bitcast.18, bf16[512,1024]{1,0:T(8,128)(2,1)S(1)} %bitcast.22, bf16[512,1024]{1,0:T(8,128)(2,1)} %collective-permute-done.5.down1), custom_call_target="tpu_custom_call" | custom-call | tf_op jit(solution)/shard_map/branch/pallas_call | solution.py:291
  136.5 22.7 %all_to_all.33 = bf16[64,4,8,128]{3,2,1,0:T(8,128)(2,1)S(1)} all-to-all(bf16[64,4,8,128]{3,2,1,0:T(8,128)(2,1)S(1)} %bitcast.20), channel_id=1, replica_groups={{0,8,16,24,32,40,48,56,64,72,80,88,96,104,112,120,128,136,144,152,160,1..., dimensions={0} | all-to-all | bytes 1048576 | tf_op jit(solution)/shard_map/all_to_all | solution.py:260
  160.0 26.4 %all_to_all.34 = bf16[128,8,128]{2,1,0:T(8,128)(2,1)S(1)} all-to-all(bf16[128,8,128]{2,1,0:T(8,128)(2,1)S(1)} %pick.3), channel_id=1, replica_groups=mesh['seq'=128,'tp'=4] {'seq'}, dimensions={0} | all-to-all | bytes 524288 | tf_op jit(solution)/shard_map/all_to_all | solution.py:300
  (22 shorter events, 3.3 us)
Async XLA Ops:
  1.9 20.5 %collective-permute-start = (bf16[256,1024]{1,0:T(8,128)(2,1)S(1)}, bf16[256,1024]{1,0:T(8,128)(2,1)}, u32[]{:S(2)}, u32[]{:S(2)}) collective-permute-start(bf16[256,1024]{1,0:T(8,128)(2,1)S(1)} %constant_dynamic-update-slice_fusion.kv0), channel_id=1, source_target_pairs={{0,8},{4,12},{8,16},{12,20},{16,24},{20,28},{24,32},{28,36},{32,40... | collective-permute-start | bytes 1572872 | tf_op jit(solution)/shard_map/ppermute | solution.py:188
  9.9 15.9 %copy-start.3 = (s32[128,1]{0,1:T(1,128)S(1)}, s32[128,1]{0,1:T(1,128)}, u32[]{:S(2)}) copy-start(s32[128,1]{0,1:T(1,128)} %param.14) | copy-start | bytes 1540
  9.9 16.6 %copy-start.1 = (bf16[128,1024]{1,0:T(8,128)(2,1)S(1)}, bf16[128,1024]{1,0:T(8,128)(2,1)}, u32[]{:S(2)}) copy-start(bf16[128,1024]{1,0:T(8,128)(2,1)} %q.3) | copy-start | bytes 786436
  9.9 16.6 %copy-start.2 = (bf16[128,1024]{1,0:T(8,128)(2,1)S(1)}, bf16[128,1024]{1,0:T(8,128)(2,1)}, u32[]{:S(2)}) copy-start(bf16[128,1024]{1,0:T(8,128)(2,1)} %res.1) | copy-start | bytes 786436
  9.9 35.5 %all-to-all-start = ((bf16[4,1024,256]{2,1,0:T(8,128)(2,1)}), bf16[4,1024,256]{2,1,0:T(8,128)(2,1)S(1)}, u32[]{:S(2)}, u32[]{:S(2)}) async-start(bf16[4,1024,256]{2,1,0:T(8,128)(2,1)} %bitcast.26), calls=%async_computation | async-start | bytes 4194304 | tf_op jit(solution)/shard_map/all_to_all | solution.py:200
  14.0 26.0 %collective-permute-start.3 = (bf16[256,1024]{1,0:T(8,128)(2,1)S(1)}, bf16[256,1024]{1,0:T(8,128)(2,1)}, u32[]{:S(2)}, u32[]{:S(2)}) collective-permute-start(bf16[256,1024]{1,0:T(8,128)(2,1)S(1)} %constant_dynamic-update-slice_fusion.kv0), channel_id=1, source_target_pairs={{0,4},{8,12},{16,20},{24,28},{32,36},{40,44},{48,52},{56,60},{64,6... | collective-permute-start | bytes 1572872 | tf_op jit(solution)/shard_map/ppermute | solution.py:188
  15.3 30.0 %collective-permute-start.5 = (bf16[512,1024]{1,0:T(8,128)(2,1)}, bf16[512,1024]{1,0:T(8,128)(2,1)}, u32[]{:S(2)}, u32[]{:S(2)}) collective-permute-start(bf16[512,1024]{1,0:T(8,128)(2,1)} %bitcast.21), channel_id=1, source_target_pairs={{0,4},{8,12},{16,20},{24,28},{32,36},{40,44},{48,52},{56,60},{64,6... | collective-permute-start | bytes 3145736 | tf_op jit(solution)/shard_map/ppermute | solution.py:188
  22.5 4.0 %collective-permute-start.2 = (bf16[256,1024]{1,0:T(8,128)(2,1)}, bf16[256,1024]{1,0:T(8,128)(2,1)S(1)}, u32[]{:S(2)}, u32[]{:S(2)}) collective-permute-start(bf16[256,1024]{1,0:T(8,128)(2,1)} %collective-permute-done.kv1), channel_id=1, source_target_pairs={{0,4},{8,12},{16,20},{24,28},{32,36},{40,44},{48,52},{56,60},{64,6... | collective-permute-start | bytes 1572872 | tf_op jit(solution)/shard_map/ppermute | solution.py:188
  24.4 12.7 %collective-permute-start.1 = (bf16[256,1024]{1,0:T(8,128)(2,1)}, bf16[256,1024]{1,0:T(8,128)(2,1)S(1)}, u32[]{:S(2)}, u32[]{:S(2)}) collective-permute-start(bf16[256,1024]{1,0:T(8,128)(2,1)} %collective-permute-done.kv1), channel_id=1, source_target_pairs={{0,8},{4,12},{8,16},{12,20},{16,24},{20,28},{24,32},{28,36},{32,40... | collective-permute-start | bytes 1572872 | tf_op jit(solution)/shard_map/ppermute | solution.py:188
  37.1 4.4 %collective-permute-start.4 = (bf16[256,1024]{1,0:T(8,128)(2,1)S(1)}, bf16[256,1024]{1,0:T(8,128)(2,1)S(1)}, u32[]{:S(2)}, u32[]{:S(2)}) collective-permute-start(bf16[256,1024]{1,0:T(8,128)(2,1)S(1)} %collective-permute-done.1.kv2), channel_id=1, source_target_pairs={{4,0},{12,8},{20,16},{28,24},{36,32},{44,40},{52,48},{60,56},{68,6... | collective-permute-start | bytes 1572872 | tf_op jit(solution)/shard_map/ppermute | solution.py:188
  79.5 25.2 %collective-permute-start.6 = (bf16[4,1024,256]{2,1,0:T(8,128)(2,1)S(1)}, bf16[4,1024,256]{2,1,0:T(8,128)(2,1)S(1)}, u32[]{:S(2)}, u32[]{:S(2)}) collective-permute-start(bf16[4,1024,256]{2,1,0:T(8,128)(2,1)S(1)} %all-to-all-done.first0), channel_id=1, source_target_pairs={{0,4},{8,12},{16,20},{24,28},{32,36},{40,44},{48,52},{56,60},{64,6... | collective-permute-start | bytes 6291464 | tf_op jit(solution)/shard_map/ppermute | solution.py:188
  106.1 28.5 %copy-start = (bf16[1,512,1024]{2,1,0:T(8,128)(2,1)S(1)}, bf16[1,512,1024]{2,1,0:T(8,128)(2,1)}, u32[]{:S(2)}) copy-start(bf16[1,512,1024]{2,1,0:T(8,128)(2,1)} %param.17) | copy-start | bytes 3145732

commit v5 on v4

--- a/solution.py
+++ b/solution.py
@@ -40,7 +40,7 @@
     return lax.dot_general(a, b, (((1,), (1,)), ((), ())), preferred_element_type=f32)
 
 
-def attend_near_kernel(place, q, kv0, kv1, kvx1, _, held, stats):
+def attend_near_kernel(place, q, k0, k1, kx1, v0, v1, vx1, _, held, stats):
     row = lax.broadcasted_iota(jnp.int32, (BLOCK, BLOCK), 0)
     col = lax.broadcasted_iota(jnp.int32, (BLOCK, BLOCK), 1)
     diff = col - row
@@ -51,8 +51,8 @@
     sums = jnp.zeros((BLOCK, HEAD_DIM), f32)
     for h in range(q.shape[1] // HEAD_DIM):
         s = slice(h * HEAD_DIM, (h + 1) * HEAD_DIM)
-        keys = jnp.concatenate([kv[:BLOCK, s] for kv in (kv1, kvx1, kv0)], axis=0)
-        values = jnp.concatenate([kv[BLOCK:, s] for kv in (kv1, kvx1, kv0)], axis=0)
+        keys = jnp.concatenate([k1[:, s], kx1[:, s], k0[:, s]], axis=0)
+        values = jnp.concatenate([v1[:, s], vx1[:, s], v0[:, s]], axis=0)
         scores = dot_t(q[:, s], keys) * (1.0 / math.sqrt(HEAD_DIM))
         scores = jnp.where(visible, scores, masked_score)
         top = jnp.max(scores, axis=1, keepdims=True)
@@ -64,7 +64,7 @@
     stats[1] = sums
 
 
-def attend_far_kernel(place, q, kv2, kvx0, kvx2, held, stats, res, out, home):
+def attend_far_kernel(place, q, k2, kx0, kx2, v2, vx0, vx2, held, stats, res, out, home):
     chip = place[0]
     core = place[1]
     row = lax.broadcasted_iota(jnp.int32, (BLOCK, BLOCK), 0)
@@ -77,9 +77,8 @@
     z_count, core_count = out.shape[0], out.shape[2]
     for h in range(q.shape[1] // HEAD_DIM):
         s = slice(h * HEAD_DIM, (h + 1) * HEAD_DIM)
-        kvx = kvx0[:, s] + kvx2[:, s]
-        keys = jnp.concatenate([kv2[:BLOCK, s], kvx[:BLOCK]], axis=0)
-        values = jnp.concatenate([kv2[BLOCK:, s], kvx[BLOCK:]], axis=0)
+        keys = jnp.concatenate([k2[:, s], kx0[:, s] + kx2[:, s]], axis=0)
+        values = jnp.concatenate([v2[:, s], vx0[:, s] + vx2[:, s]], axis=0)
         scores = dot_t(q[:, s], keys) * (1.0 / math.sqrt(HEAD_DIM))
         scores = jnp.where(visible, scores, masked_score)
         near_top = stats[0, :, h : h + 1]
@@ -187,17 +186,25 @@
     def move(x, route):
         return lax.ppermute(x, "seq", route)
 
-    kv0 = jnp.concatenate([keys, values], axis=0)
-    kv1 = move(kv0, onward)
-    kv2 = move(kv1, onward)
-    kvx0 = move(kv0, to_odd)
-    kvx1 = move(kv1, swap)
-
-    gate_own, up_own, down0, kv0 = lax.optimization_barrier(
-        (gate_weight[0], up_weight[0], down_weight[0], kv0)
-    )
-    both = jnp.concatenate([gate_own, up_own], axis=1).reshape(tp_count, width, -1)
-    first0 = lax.all_to_all(both, "tp", 0, 0, tiled=True)
+    k1 = move(keys, onward)
+    v1 = move(values, onward)
+    k2 = move(k1, onward)
+    v2 = move(v1, onward)
+    kx0 = move(keys, to_odd)
+    vx0 = move(values, to_odd)
+    kx1 = move(k1, swap)
+    vx1 = move(v1, swap)
+
+    gate_own, up_own, down0 = gate_weight[0], up_weight[0], down_weight[0]
+    def by_features_now(w):
+        return lax.all_to_all(w.reshape(tp_count, width, -1), "tp", 0, 0, tiled=True)
+
+    def by_features(w):
+        w = lax.all_gather(w, "tp")
+        return lax.dynamic_slice_in_dim(w, tp_place * width, width, 1)
+
+    up0 = by_features_now(up_own)
+    gate0 = by_features(gate_own)
     down1 = move(down0, swap)
     gain = lax.dynamic_slice_in_dim(norm_gain, tp_place * width, width)[None]
 
@@ -221,26 +228,28 @@
             jax.ShapeDtypeStruct((rows, width), f32),
             jax.ShapeDtypeStruct((2, BLOCK, HEAD_DIM), f32),
         ),
-        in_specs=[smem()] + [vmem()] * 5,
+        in_specs=[smem()] + [vmem()] * 8,
         out_specs=(vmem(), vmem()),
         compiler_params=params(),
         name="attend_near",
-    )(place, queries, kv0, kv1, kvx1, residual_in)
-    kv2, held, stats = lax.optimization_barrier((kv2, held, stats))
-    kvx2 = move(kv2, to_even)
+    )(place, queries, keys, k1, kx1, values, v1, vx1, residual_in)
+    k2, v2, held, stats = lax.optimization_barrier((k2, v2, held, stats))
+    kx2 = move(k2, to_even)
+    vx2 = move(v2, to_even)
     stream, home = pl.pallas_call(
         attend_far_kernel,
         out_shape=(
             jax.ShapeDtypeStruct((z_count, heads, 2, TILE, HEAD_DIM), bf16),
             jax.ShapeDtypeStruct((rows, width), bf16),
         ),
-        in_specs=[smem()] + [vmem()] * 7,
+        in_specs=[smem()] + [vmem()] * 10,
         out_specs=(vmem(), vmem()),
         compiler_params=params(),
         name="attend_far",
-    )(place, queries, kv2, kvx0, kvx2, held, stats, residual_in)
-    stream, first0, down1 = lax.optimization_barrier((stream, first0, down1))
-
+    )(place, queries, k2, kx0, kx2, v2, vx0, vx2, held, stats, residual_in)
+
+    stream, up0 = lax.optimization_barrier((stream, up0))
+    first0 = jnp.concatenate([gate0, up0], axis=2)
     tiles = lax.all_to_all(
         stream.reshape(seq_count, TILE, HEAD_DIM), "seq", 0, 0, tiled=True
     )

time: 188 us -> 199 us (1.059)
  blocking collectives: 133 us -> 75.6 us
  starting transfers between devices: 25.1 us -> 59.9 us
  waiting for transfers between devices: 9.21 us -> 30.1 us
  between operations: 0.17 us -> 13.7 us
  Pallas kernels: 13.2 us -> 15.3 us
    all_to_all x1 -> x0, blocking collectives: 34.1 us -> none  [local(): lax.all_to_all(stream.reshape(seq_count, TILE, HEAD_DIM), 'seq', 0, 0, ti...]
    all_to_all x1 -> x3, starting transfers between devices: 4.14 us -> 27.9 us  [the longest x1 14.7 us: local(): lax.all_to_all(stream.reshape(seq_count, TILE, HEAD_DIM), 'seq', 0, 0, ti...]
    all_to_all x2 -> x1, blocking collectives: 44.6 us -> 21.1 us  [same_core_exchange(): lax.all_to_all(x, 'seq', 0, 0, tiled=True, axis_index_groups=same_core)]
    all_to_all x1 -> x3, waiting for transfers between devices: 0.01 us -> 21.4 us  [the longest x1 15.8 us: same_core_exchange(): lax.all_to_all(x, 'seq', 0, 0, tiled=True, axis_index_groups=same_core)]
    ppermute x7 -> x12, starting transfers between devices: 21 us -> 32 us  [move(): return lax.ppermute(x, 'seq', route)]
    ppermute x7 -> x12, waiting for transfers between devices: 9.21 us -> 1.13 us  [move(): return lax.ppermute(x, 'seq', route)]
    all_gather x0 -> x1, waiting for transfers between devices: none -> 6.88 us  [by_features(): w = lax.all_gather(w, 'tp')]
  transfers between devices with their start and end apart: 8 -> 16, of which waited for: 3 -> 4; matrix products, arithmetic and copies ran while one was open for 2% -> 2% of each run, Pallas kernels for 4% -> 6%
where the time goes in v5:
time: 199 us; the launch traced here: 198 us
  blocking collectives  75.6 us (38%)
  starting transfers between devices  59.9 us (30%)
  waiting for transfers between devices  30.1 us (15%)
  Pallas kernels  15.3 us (8%)
  between operations  13.7 us (7%)
  local copies, waits for them, and re-layouts  2.01 us (1%)
    ppermute x12, starting transfers between devices, move(): return lax.ppermute(x, 'seq', route)  32 us
    all_to_all x1, blocking collectives, local(): finished = lax.all_to_all(pick(slot_of, returned), 'seq', 0, 0, tiled=True)  26.3 us
    all_to_all x1, blocking collectives, same_core_exchange(): lax.all_to_all(x, 'seq', 0, 0, tiled=True, axis_index_groups=same_core)  21.1 us
    all_to_all x1, blocking collectives, local(): parts = lax.all_to_all(parts, 'tp', 0, 0, tiled=True)  16.9 us
    all_to_all x1, waiting for transfers between devices, same_core_exchange(): lax.all_to_all(x, 'seq', 0, 0, tiled=True, axis_index_groups=same_core)  15.8 us
    all_to_all x1, starting transfers between devices, local(): lax.all_to_all(stream.reshape(seq_count, TILE, HEAD_DIM), 'seq', 0, 0, ti...  14.7 us
    all_gather x1, blocking collectives, local(): hidden = lax.all_gather(hidden, 'tp')  11.3 us
    all_to_all x1, starting transfers between devices, same_core_exchange(): lax.all_to_all(x, 'seq', 0, 0, tiled=True, axis_index_groups=same_core)  8.96 us
  transfers between devices with their start and end apart: 16, of which 4 were waited for; matrix products, arithmetic and copies ran while one was open for 2% of the time, Pallas kernels for 6%

profile of v5, /device:TPU:1, one launch (start us, length us, event | category | flops | bytes accessed | tf_op | source)
XLA Modules:
  0.0 198.5 jit_solution(2936026799988530243)
XLA Ops:
  7.3 4.0 %collective-permute-start = (bf16[128,1024]{1,0:T(8,128)(2,1)}, bf16[128,1024]{1,0:T(8,128)(2,1)S(1)}, u32[]{:S(2)}, u32[]{:S(2)}) collective-permute-start(bf16[128,1024]{1,0:T(8,128)(2,1)} %k0.1), channel_id=1, source_target_pairs={{0,8},{4,12},{8,16},{12,20},{16,24},{20,28},{24,32},{28,36},{32,40... | collective-permute-start | bytes 786440 | tf_op jit(solution)/shard_map/ppermute | solution.py:187
  11.3 3.2 %collective-permute-start.2 = (bf16[128,1024]{1,0:T(8,128)(2,1)}, bf16[128,1024]{1,0:T(8,128)(2,1)S(1)}, u32[]{:S(2)}, u32[]{:S(2)}) collective-permute-start(bf16[128,1024]{1,0:T(8,128)(2,1)} %v0.1), channel_id=1, source_target_pairs={{0,8},{4,12},{8,16},{12,20},{16,24},{20,28},{24,32},{28,36},{32,40... | collective-permute-start | bytes 786440 | tf_op jit(solution)/shard_map/ppermute | solution.py:187
  15.8 4.3 %all-to-all-start = ((bf16[4,1024,128]{2,1,0:T(8,128)(2,1)}), bf16[4,1024,128]{2,1,0:T(8,128)(2,1)}, u32[]{:S(2)}, u32[]{:S(2)}) async-start(bf16[4,1024,128]{2,1,0:T(8,128)(2,1)} %bitcast.22), calls=%async_computation | async-start | bytes 2097152 | tf_op jit(solution)/shard_map/all_to_all | solution.py:200
  20.3 3.2 %collective-permute-start.1 = (bf16[128,1024]{1,0:T(8,128)(2,1)S(1)}, bf16[128,1024]{1,0:T(8,128)(2,1)S(1)}, u32[]{:S(2)}, u32[]{:S(2)}) collective-permute-start(bf16[128,1024]{1,0:T(8,128)(2,1)S(1)} %collective-permute-done.k1), channel_id=1, source_target_pairs={{0,8},{4,12},{8,16},{12,20},{16,24},{20,28},{24,32},{28,36},{32,40... | collective-permute-start | bytes 786440 | tf_op jit(solution)/shard_map/ppermute | solution.py:187
  23.5 4.0 %collective-permute-start.4 = (bf16[128,1024]{1,0:T(8,128)(2,1)S(1)}, bf16[128,1024]{1,0:T(8,128)(2,1)S(1)}, u32[]{:S(2)}, u32[]{:S(2)}) collective-permute-start(bf16[128,1024]{1,0:T(8,128)(2,1)S(1)} %collective-permute-done.k1), channel_id=1, source_target_pairs={{0,4},{8,12},{16,20},{24,28},{32,36},{40,44},{48,52},{56,60},{64,6... | collective-permute-start | bytes 786440 | tf_op jit(solution)/shard_map/ppermute | solution.py:187
  27.6 3.9 %collective-permute-start.3 = (bf16[128,1024]{1,0:T(8,128)(2,1)S(1)}, bf16[128,1024]{1,0:T(8,128)(2,1)S(1)}, u32[]{:S(2)}, u32[]{:S(2)}) collective-permute-start(bf16[128,1024]{1,0:T(8,128)(2,1)S(1)} %collective-permute-done.2.v1), channel_id=1, source_target_pairs={{0,8},{4,12},{8,16},{12,20},{16,24},{20,28},{24,32},{28,36},{32,40... | collective-permute-start | bytes 786440 | tf_op jit(solution)/shard_map/ppermute | solution.py:187
  31.4 2.2 %collective-permute-start.5 = (bf16[128,1024]{1,0:T(8,128)(2,1)S(1)}, bf16[128,1024]{1,0:T(8,128)(2,1)S(1)}, u32[]{:S(2)}, u32[]{:S(2)}) collective-permute-start(bf16[128,1024]{1,0:T(8,128)(2,1)S(1)} %collective-permute-done.2.v1), channel_id=1, source_target_pairs={{0,4},{8,12},{16,20},{24,28},{32,36},{40,44},{48,52},{56,60},{64,6... | collective-permute-start | bytes 786440 | tf_op jit(solution)/shard_map/ppermute | solution.py:187
  35.9 2.8 %attend_near.1 = (f32[128,1024]{1,0:T(8,128)S(1)}, f32[2,128,128]{2,1,0:T(8,128)S(1)}) custom-call(s32[2]{0:T(128)S(1)} %pad_add_fusion.place, bf16[128,1024]{1,0:T(8,128)(2,1)S(1)} %copy-done.1, bf16[128,1024]{1,0:T(8,128)(2,1)S(1)} %copy-done.3, bf16[128,1024]{1,0:T(8,128)(2,1)S(1)} %collective-permute-done.k1, ...), custom_call_target="tpu_custom_call" | custom-call | tf_op jit(solution)/shard_map/attend_near/pallas_call | solution.py:225
  38.7 3.1 %collective-permute-start.7 = (bf16[128,1024]{1,0:T(8,128)(2,1)S(1)}, bf16[128,1024]{1,0:T(8,128)(2,1)S(1)}, u32[]{:S(2)}, u32[]{:S(2)}) collective-permute-start(bf16[128,1024]{1,0:T(8,128)(2,1)S(1)} %collective-permute-done.1.k2), channel_id=1, source_target_pairs={{4,0},{12,8},{20,16},{28,24},{36,32},{44,40},{52,48},{60,56},{68,6... | collective-permute-start | bytes 786440 | tf_op jit(solution)/shard_map/ppermute | solution.py:187
  44.2 4.0 %attend_far.1 = (bf16[8,8,2,8,128]{4,3,2,1,0:T(8,128)(2,1)}, bf16[128,1024]{1,0:T(8,128)(2,1)S(1)}) custom-call(s32[2]{0:T(128)S(1)} %pad_add_fusion.place, bf16[128,1024]{1,0:T(8,128)(2,1)S(1)} %copy-done.1, bf16[128,1024]{1,0:T(8,128)(2,1)S(1)} %collective-permute-done.1.k2, bf16[128,1024]{1,0:T(8,128)(2,1)S(1)} %collective-permute-done.6.kx0, ...), custom_call_target="tpu_custom_call" | custom-call | tf_op jit(solution)/shard_map/attend_far/pallas_call | solution.py:239
  48.2 14.7 %all-to-all-start.1 = ((bf16[128,8,128]{2,1,0:T(8,128)(2,1)}), bf16[128,8,128]{2,1,0:T(8,128)(2,1)S(1)}, u32[]{:S(2)}, u32[]{:S(2)}) async-start(bf16[128,8,128]{2,1,0:T(8,128)(2,1)} %bitcast.5), calls=%async_computation.1 | async-start | bytes 524288 | tf_op jit(solution)/shard_map/all_to_all | solution.py:253
  62.9 6.9 %all-gather.3.cloned.1.call-done = bf16[4,4096,128]{2,1,0:T(8,128)(2,1)} async-done(((bf16[1,4096,128]{2,1,0:T(8,128)(2,1)}), bf16[4,4096,128]{2,1,0:T(8,128)(2,1)}) %all-gather.3.cloned.1.call-update) | async-done | bytes 4194320 | tf_op jit(solution)/shard_map/all_gather | solution.py:203
  72.5 5.6 %all-to-all-done.1.tiles = bf16[128,8,128]{2,1,0:T(8,128)(2,1)S(1)} async-done(((bf16[128,8,128]{2,1,0:T(8,128)(2,1)}), bf16[128,8,128]{2,1,0:T(8,128)(2,1)S(1)}, u32[]{:S(2)}, u32[]{:S(2)}) %all-to-all-start.1) | async-done | bytes 262176 | tf_op jit(solution)/shard_map/all_to_all | solution.py:253
  78.1 2.3 %collective-permute-start.10 = (bf16[4,1024,256]{2,1,0:T(8,128)(2,1)S(1)}, bf16[4,1024,256]{2,1,0:T(8,128)(2,1)}, u32[]{:S(2)}, u32[]{:S(2)}) collective-permute-start(bf16[4,1024,256]{2,1,0:T(8,128)(2,1)S(1)} %pad_maximum_fusion.first0), channel_id=1, source_target_pairs={{0,4},{8,12},{16,20},{24,28},{32,36},{40,44},{48,52},{56,60},{64,6... | collective-permute-start | bytes 6291464 | tf_op jit(solution)/shard_map/ppermute | solution.py:187
  80.4 1.8 pick.2
  82.2 9.0 %all-to-all-start.2 = ((bf16[64,4,8,128]{3,2,1,0:T(8,128)(2,1)}), bf16[64,4,8,128]{3,2,1,0:T(8,128)(2,1)S(1)}, u32[]{:S(2)}, u32[]{:S(2)}) async-start(bf16[64,4,8,128]{3,2,1,0:T(8,128)(2,1)} %bitcast.6), calls=%async_computation.2 | async-start | bytes 1048576 | tf_op jit(solution)/shard_map/all_to_all | solution.py:269
  91.2 2.2 %collective-permute-start.11 = (bf16[512,1024]{1,0:T(8,128)(2,1)}, bf16[512,1024]{1,0:T(8,128)(2,1)}, u32[]{:S(2)}, u32[]{:S(2)}) collective-permute-start(bf16[512,1024]{1,0:T(8,128)(2,1)} %bitcast.18), channel_id=1, source_target_pairs={{0,4},{8,12},{16,20},{24,28},{32,36},{40,44},{48,52},{56,60},{64,6... | collective-permute-start | bytes 3145736 | tf_op jit(solution)/shard_map/ppermute | solution.py:187
  93.4 15.8 %all-to-all-done.2 = bf16[64,4,8,128]{3,2,1,0:T(8,128)(2,1)S(1)} async-done(((bf16[64,4,8,128]{3,2,1,0:T(8,128)(2,1)}), bf16[64,4,8,128]{3,2,1,0:T(8,128)(2,1)S(1)}, u32[]{:S(2)}, u32[]{:S(2)}) %all-to-all-start.2) | async-done | bytes 524320 | tf_op jit(solution)/shard_map/all_to_all | solution.py:269
  109.2 3.0 %project.1 = bf16[4,272,512]{2,1,0:T(8,128)(2,1)S(1)} custom-call(bf16[8,8,4,8,128]{4,3,2,1,0:T(8,128)(2,1)S(1)} %bitcast.14, f32[1,1024]{1,0:T(1,128)S(1)} %bitcast.21, bf16[4,1024,256]{2,1,0:T(8,128)(2,1)S(1)} %pad_maximum_fusion.first0, bf16[4,1024,256]{2,1,0:T(8,128)(2,1)} %collective-permute-done.10.first1), custom_call_target="tpu_custom_call" | custom-call | tf_op jit(solution)/shard_map/project/pallas_call | solution.py:277
  112.2 16.9 %all_to_all.30.parts_ref = bf16[4,272,512]{2,1,0:T(8,128)(2,1)S(1)} all-to-all(bf16[4,272,512]{2,1,0:T(8,128)(2,1)S(1)} %project.1), channel_id=1, replica_groups=mesh['seq'=128,'tp'=4] {'tp'}, dimensions={0} | all-to-all | bytes 2228224 | tf_op jit(solution)/shard_map/all_to_all | solution.py:286
  129.5 11.3 %all-gather = bf16[1024,256]{1,0:T(8,128)(2,1)S(1)} all-gather(bf16[256,256]{1,0:T(8,128)(2,1)S(1)} %hidden.1), channel_id=2, replica_groups=mesh['seq'=128,'tp'=4] {'tp'}, dimensions={0}, use_global_device_ids=true | all-gather | bytes 655360 | tf_op jit(solution)/shard_map/all_gather | solution.py:299
  140.8 1.9 branch.1
  142.7 21.1 %all_to_all.31 = bf16[64,4,8,128]{3,2,1,0:T(8,128)(2,1)S(1)} all-to-all(bf16[64,4,8,128]{3,2,1,0:T(8,128)(2,1)S(1)} %bitcast.17), channel_id=1, replica_groups={{0,8,16,24,32,40,48,56,64,72,80,88,96,104,112,120,128,136,144,152,160,1..., dimensions={0} | all-to-all | bytes 1048576 | tf_op jit(solution)/shard_map/all_to_all | solution.py:269
  164.5 26.3 %all_to_all.32 = bf16[128,8,128]{2,1,0:T(8,128)(2,1)S(1)} all-to-all(bf16[128,8,128]{2,1,0:T(8,128)(2,1)S(1)} %pick.3), channel_id=1, replica_groups=mesh['seq'=128,'tp'=4] {'seq'}, dimensions={0} | all-to-all | bytes 524288 | tf_op jit(solution)/shard_map/all_to_all | solution.py:309
  (40 shorter events, 11.4 us)
Async XLA Ops:
  6.5 29.4 %copy-start.3 = (bf16[128,1024]{1,0:T(8,128)(2,1)S(1)}, bf16[128,1024]{1,0:T(8,128)(2,1)}, u32[]{:S(2)}) copy-start(bf16[128,1024]{1,0:T(8,128)(2,1)} %k0.1) | copy-start | bytes 786436
  6.5 28.0 %copy-start.4 = (bf16[128,1024]{1,0:T(8,128)(2,1)S(1)}, bf16[128,1024]{1,0:T(8,128)(2,1)}, u32[]{:S(2)}) copy-start(bf16[128,1024]{1,0:T(8,128)(2,1)} %v0.1) | copy-start | bytes 786436
  6.5 13.6 %copy-start.5 = (s32[128,1]{0,1:T(1,128)S(1)}, s32[128,1]{0,1:T(1,128)}, u32[]{:S(2)}) copy-start(s32[128,1]{0,1:T(1,128)} %param.14) | copy-start | bytes 1540
  6.5 29.4 %copy-start.1 = (bf16[128,1024]{1,0:T(8,128)(2,1)S(1)}, bf16[128,1024]{1,0:T(8,128)(2,1)}, u32[]{:S(2)}) copy-start(bf16[128,1024]{1,0:T(8,128)(2,1)} %q.3) | copy-start | bytes 786436
  6.5 29.4 %copy-start.2 = (bf16[128,1024]{1,0:T(8,128)(2,1)S(1)}, bf16[128,1024]{1,0:T(8,128)(2,1)}, u32[]{:S(2)}) copy-start(bf16[128,1024]{1,0:T(8,128)(2,1)} %res.1) | copy-start | bytes 786436
  6.5 63.2 %all-gather.3.cloned.1.call-start = ((), (), s32[]{:S(2)}) async-start(), calls=%async_computation.6 | async-start | bytes 5242880 | tf_op jit(solution)/shard_map/all_gather | solution.py:203
  7.3 13.0 %collective-permute-start = (bf16[128,1024]{1,0:T(8,128)(2,1)}, bf16[128,1024]{1,0:T(8,128)(2,1)S(1)}, u32[]{:S(2)}, u32[]{:S(2)}) collective-permute-start(bf16[128,1024]{1,0:T(8,128)(2,1)} %k0.1), channel_id=1, source_target_pairs={{0,8},{4,12},{8,16},{12,20},{16,24},{20,28},{24,32},{28,36},{32,40... | collective-permute-start | bytes 786440 | tf_op jit(solution)/shard_map/ppermute | solution.py:187
  11.3 16.2 %collective-permute-start.2 = (bf16[128,1024]{1,0:T(8,128)(2,1)}, bf16[128,1024]{1,0:T(8,128)(2,1)S(1)}, u32[]{:S(2)}, u32[]{:S(2)}) collective-permute-start(bf16[128,1024]{1,0:T(8,128)(2,1)} %v0.1), channel_id=1, source_target_pairs={{0,8},{4,12},{8,16},{12,20},{16,24},{20,28},{24,32},{28,36},{32,40... | collective-permute-start | bytes 786440 | tf_op jit(solution)/shard_map/ppermute | solution.py:187
  14.5 28.5 %collective-permute-start.6 = (bf16[128,1024]{1,0:T(8,128)(2,1)}, bf16[128,1024]{1,0:T(8,128)(2,1)S(1)}, u32[]{:S(2)}, u32[]{:S(2)}) collective-permute-start(bf16[128,1024]{1,0:T(8,128)(2,1)} %k0.1), channel_id=1, source_target_pairs={{0,4},{8,12},{16,20},{24,28},{32,36},{40,44},{48,52},{56,60},{64,6... | collective-permute-start | bytes 786440 | tf_op jit(solution)/shard_map/ppermute | solution.py:187
  15.8 32.3 %all-to-all-start = ((bf16[4,1024,128]{2,1,0:T(8,128)(2,1)}), bf16[4,1024,128]{2,1,0:T(8,128)(2,1)}, u32[]{:S(2)}, u32[]{:S(2)}) async-start(bf16[4,1024,128]{2,1,0:T(8,128)(2,1)} %bitcast.22), calls=%async_computation | async-start | bytes 2097152 | tf_op jit(solution)/shard_map/all_to_all | solution.py:200
  20.3 18.4 %collective-permute-start.1 = (bf16[128,1024]{1,0:T(8,128)(2,1)S(1)}, bf16[128,1024]{1,0:T(8,128)(2,1)S(1)}, u32[]{:S(2)}, u32[]{:S(2)}) collective-permute-start(bf16[128,1024]{1,0:T(8,128)(2,1)S(1)} %collective-permute-done.k1), channel_id=1, source_target_pairs={{0,8},{4,12},{8,16},{12,20},{16,24},{20,28},{24,32},{28,36},{32,40... | collective-permute-start | bytes 786440 | tf_op jit(solution)/shard_map/ppermute | solution.py:187
  23.5 11.0 %collective-permute-start.4 = (bf16[128,1024]{1,0:T(8,128)(2,1)S(1)}, bf16[128,1024]{1,0:T(8,128)(2,1)S(1)}, u32[]{:S(2)}, u32[]{:S(2)}) collective-permute-start(bf16[128,1024]{1,0:T(8,128)(2,1)S(1)} %collective-permute-done.k1), channel_id=1, source_target_pairs={{0,4},{8,12},{16,20},{24,28},{32,36},{40,44},{48,52},{56,60},{64,6... | collective-permute-start | bytes 786440 | tf_op jit(solution)/shard_map/ppermute | solution.py:187
  27.6 11.1 %collective-permute-start.3 = (bf16[128,1024]{1,0:T(8,128)(2,1)S(1)}, bf16[128,1024]{1,0:T(8,128)(2,1)S(1)}, u32[]{:S(2)}, u32[]{:S(2)}) collective-permute-start(bf16[128,1024]{1,0:T(8,128)(2,1)S(1)} %collective-permute-done.2.v1), channel_id=1, source_target_pairs={{0,8},{4,12},{8,16},{12,20},{16,24},{20,28},{24,32},{28,36},{32,40... | collective-permute-start | bytes 786440 | tf_op jit(solution)/shard_map/ppermute | solution.py:187
  31.4 4.4 %collective-permute-start.5 = (bf16[128,1024]{1,0:T(8,128)(2,1)S(1)}, bf16[128,1024]{1,0:T(8,128)(2,1)S(1)}, u32[]{:S(2)}, u32[]{:S(2)}) collective-permute-start(bf16[128,1024]{1,0:T(8,128)(2,1)S(1)} %collective-permute-done.2.v1), channel_id=1, source_target_pairs={{0,4},{8,12},{16,20},{24,28},{32,36},{40,44},{48,52},{56,60},{64,6... | collective-permute-start | bytes 786440 | tf_op jit(solution)/shard_map/ppermute | solution.py:187
  34.6 8.5 %collective-permute-start.8 = (bf16[128,1024]{1,0:T(8,128)(2,1)S(1)}, bf16[128,1024]{1,0:T(8,128)(2,1)S(1)}, u32[]{:S(2)}, u32[]{:S(2)}) collective-permute-start(bf16[128,1024]{1,0:T(8,128)(2,1)S(1)} %copy-done.4), channel_id=1, source_target_pairs={{0,4},{8,12},{16,20},{24,28},{32,36},{40,44},{48,52},{56,60},{64,6... | collective-permute-start | bytes 786440 | tf_op jit(solution)/shard_map/ppermute | solution.py:187
  38.7 4.4 %collective-permute-start.7 = (bf16[128,1024]{1,0:T(8,128)(2,1)S(1)}, bf16[128,1024]{1,0:T(8,128)(2,1)S(1)}, u32[]{:S(2)}, u32[]{:S(2)}) collective-permute-start(bf16[128,1024]{1,0:T(8,128)(2,1)S(1)} %collective-permute-done.1.k2), channel_id=1, source_target_pairs={{4,0},{12,8},{20,16},{28,24},{36,32},{44,40},{52,48},{60,56},{68,6... | collective-permute-start | bytes 786440 | tf_op jit(solution)/shard_map/ppermute | solution.py:187
  41.8 2.4 %collective-permute-start.9 = (bf16[128,1024]{1,0:T(8,128)(2,1)S(1)}, bf16[128,1024]{1,0:T(8,128)(2,1)S(1)}, u32[]{:S(2)}, u32[]{:S(2)}) collective-permute-start(bf16[128,1024]{1,0:T(8,128)(2,1)S(1)} %collective-permute-done.3.v2), channel_id=1, source_target_pairs={{4,0},{12,8},{20,16},{28,24},{36,32},{44,40},{52,48},{60,56},{68,6... | collective-permute-start | bytes 786440 | tf_op jit(solution)/shard_map/ppermute | solution.py:187
  48.2 30.0 %all-to-all-start.1 = ((bf16[128,8,128]{2,1,0:T(8,128)(2,1)}), bf16[128,8,128]{2,1,0:T(8,128)(2,1)S(1)}, u32[]{:S(2)}, u32[]{:S(2)}) async-start(bf16[128,8,128]{2,1,0:T(8,128)(2,1)} %bitcast.5), calls=%async_computation.1 | async-start | bytes 524288 | tf_op jit(solution)/shard_map/all_to_all | solution.py:253
  78.1 31.0 %collective-permute-start.10 = (bf16[4,1024,256]{2,1,0:T(8,128)(2,1)S(1)}, bf16[4,1024,256]{2,1,0:T(8,128)(2,1)}, u32[]{:S(2)}, u32[]{:S(2)}) collective-permute-start(bf16[4,1024,256]{2,1,0:T(8,128)(2,1)S(1)} %pad_maximum_fusion.first0), channel_id=1, source_target_pairs={{0,4},{8,12},{16,20},{24,28},{32,36},{40,44},{48,52},{56,60},{64,6... | collective-permute-start | bytes 6291464 | tf_op jit(solution)/shard_map/ppermute | solution.py:187
  82.2 27.0 %all-to-all-start.2 = ((bf16[64,4,8,128]{3,2,1,0:T(8,128)(2,1)}), bf16[64,4,8,128]{3,2,1,0:T(8,128)(2,1)S(1)}, u32[]{:S(2)}, u32[]{:S(2)}) async-start(bf16[64,4,8,128]{3,2,1,0:T(8,128)(2,1)} %bitcast.6), calls=%async_computation.2 | async-start | bytes 1048576 | tf_op jit(solution)/shard_map/all_to_all | solution.py:269
  91.2 49.6 %collective-permute-start.11 = (bf16[512,1024]{1,0:T(8,128)(2,1)}, bf16[512,1024]{1,0:T(8,128)(2,1)}, u32[]{:S(2)}, u32[]{:S(2)}) collective-permute-start(bf16[512,1024]{1,0:T(8,128)(2,1)} %bitcast.18), channel_id=1, source_target_pairs={{0,4},{8,12},{16,20},{24,28},{32,36},{40,44},{48,52},{56,60},{64,6... | collective-permute-start | bytes 3145736 | tf_op jit(solution)/shard_map/ppermute | solution.py:187
  112.2 28.6 %copy-start = (bf16[1,512,1024]{2,1,0:T(8,128)(2,1)S(1)}, bf16[1,512,1024]{2,1,0:T(8,128)(2,1)}, u32[]{:S(2)}) copy-start(bf16[1,512,1024]{2,1,0:T(8,128)(2,1)} %param.17) | copy-start | bytes 3145732
Sparse Core Ops, SparseCore 0:
  9.5 60.2 all-gather.2

commit v6 on v5

--- a/solution.py
+++ b/solution.py
@@ -98,49 +98,51 @@
         out[i] = tiles[index[i]]
 
 
-def project_kernel(tiles, gain, first0, first1, out, held):
+def scale_kernel(tiles, gain, out):
     z_count, heads, slots = tiles.shape[:3]
     rows = z_count * slots * TILE
+    count = out.shape[0]
     squares = jnp.zeros((rows, HEAD_DIM), f32)
     for h in range(heads):
         value = tiles[:, h].astype(f32).reshape(rows, HEAD_DIM)
         squares = squares + value * value
         s = slice(h * HEAD_DIM, (h + 1) * HEAD_DIM)
-        held[:, s] = (value * gain[:, s]).astype(bf16)
+        scaled = (value * gain[:, s]).astype(bf16)
+        for t in range(count):
+            out[t, :rows, s] = scaled
     high = squares.astype(bf16)
     low = (squares - high.astype(f32)).astype(bf16)
     ones = jnp.ones((TILE, HEAD_DIM), bf16)
     total = dot_t(ones, high) + dot_t(ones, low)
     total_high = total.astype(bf16).astype(f32)
     total_rows = jnp.concatenate([total_high, total - total_high], axis=0).astype(bf16)
-    x = held[...]
-    parts = out.shape[0]
-    for t in range(parts):
-        width = first0.shape[2]
-        out[t, :rows, :width] = dot(x, first0[t]).astype(bf16)
-        out[t, :rows, width:] = dot(x, first1[t]).astype(bf16)
-        out[t, rows:, :rows] = total_rows
-        out[t, rows:, rows:] = total_rows
-
-
-def hidden_kernel(features, parts, out):
-    count = parts.shape[0]
+    for t in range(count):
+        for s in range(0, out.shape[2], rows):
+            out[t, rows:, s : s + rows] = total_rows
+
+
+def hidden_kernel(features, scaled, gate0, gate1, up0, up1, out):
+    count = scaled.shape[0]
     rows, width = out.shape
-    tail = parts.shape[1] - rows
-    sums = parts[:, rows:, :rows].reshape(count * tail, rows)
+    tail = scaled.shape[1] - rows
+    depth = scaled.shape[2]
+    sums = scaled[:, rows:, :rows].reshape(count * tail, rows)
     weight = jnp.full((count * tail, HEAD_DIM), 1.0 / TILE, bf16)
     square = lax.dot_general(
         sums, weight, (((0,), (0,)), ((), ())), preferred_element_type=f32
     )
     factor = lax.rsqrt(square * (1.0 / features) + epsilon)
+    gate = jnp.zeros((rows, width), f32)
+    up = jnp.zeros((rows, width), f32)
+    for t in range(count):
+        k = slice(t * depth, (t + 1) * depth)
+        x = scaled[t, :rows]
+        gate = gate + dot(x, jnp.concatenate([gate0[k], gate1[k]], axis=1))
+        up = up + dot(x, jnp.concatenate([up0[k], up1[k]], axis=1))
     half = width // 2
-    for k in range(2):
-        value = sum(
-            parts[t, :rows, k * width : (k + 1) * width].astype(f32) for t in range(count)
-        )
-        gate = value[:, :half] * factor
-        up = value[:, half:] * factor
-        out[:, k * half : (k + 1) * half] = (gate / (1.0 + jnp.exp(-gate)) * up).astype(bf16)
+    for s in (slice(0, half), slice(half, width)):
+        g = gate[:, s] * factor
+        out[:, s] = (g / (1.0 + jnp.exp(-g)) * (up[:, s] * factor)).astype(bf16)
 
 
 def branch_kernel(hidden, down0, down1, out):
@@ -195,16 +197,9 @@
     kx1 = move(k1, swap)
     vx1 = move(v1, swap)
 
-    gate_own, up_own, down0 = gate_weight[0], up_weight[0], down_weight[0]
-    def by_features_now(w):
-        return lax.all_to_all(w.reshape(tp_count, width, -1), "tp", 0, 0, tiled=True)
-
-    def by_features(w):
-        w = lax.all_gather(w, "tp")
-        return lax.dynamic_slice_in_dim(w, tp_place * width, width, 1)
-
-    up0 = by_features_now(up_own)
-    gate0 = by_features(gate_own)
+    gate0, up0, down0 = gate_weight[0], up_weight[0], down_weight[0]
+    gate1 = move(gate0, swap)
+    up1 = move(up0, swap)
     down1 = move(down0, swap)
     gain = lax.dynamic_slice_in_dim(norm_gain, tp_place * width, width)[None]
 
@@ -248,8 +243,6 @@
         name="attend_far",
     )(place, queries, k2, kx0, kx2, v2, vx0, vx2, held, stats, residual_in)
 
-    stream, up0 = lax.optimization_barrier((stream, up0))
-    first0 = jnp.concatenate([gate0, up0], axis=2)
     tiles = lax.all_to_all(
         stream.reshape(seq_count, TILE, HEAD_DIM), "seq", 0, 0, tiled=True
     )
@@ -268,34 +261,32 @@
         x = x.reshape(chips, slots, TILE, HEAD_DIM)
         return lax.all_to_all(x, "seq", 0, 0, tiled=True, axis_index_groups=same_core)
 
-    tiles, first0 = lax.optimization_barrier((tiles, first0))
-    first1 = move(first0, swap)
     arrived = same_core_exchange(pick(block_of, tiles))
+    arrived, gate1, up1, down1 = lax.optimization_barrier((arrived, gate1, up1, down1))
     arrived = arrived.reshape(z_count, heads, slots, TILE, HEAD_DIM)
     work = z_count * slots * TILE
-    hid = first0.shape[2]
-    parts = pl.pallas_call(
-        project_kernel,
-        out_shape=jax.ShapeDtypeStruct((tp_count, work + 2 * TILE, 2 * hid), bf16),
-        in_specs=[vmem()] * 4,
+    hid = 2 * gate0.shape[1]
+    scaled = pl.pallas_call(
+        scale_kernel,
+        out_shape=jax.ShapeDtypeStruct((tp_count, work + 2 * TILE, width), bf16),
+        in_specs=[vmem()] * 2,
         out_specs=vmem(),
-        scratch_shapes=[pltpu.VMEM((work, width), bf16)],
-        compiler_params=params(),
-        name="project",
-    )(arrived, gain, first0, first1)
-    parts = lax.all_to_all(parts, "tp", 0, 0, tiled=True)
-
-    def run_hidden(parts_ref, out_ref):
-        hidden_kernel(width * tp_count, parts_ref, out_ref)
+        compiler_params=params(),
+        name="scale",
+    )(arrived, gain)
+    scaled = lax.all_to_all(scaled, "tp", 0, 0, tiled=True)
+
+    def run_hidden(*refs):
+        hidden_kernel(width * tp_count, *refs)
 
     hidden = pl.pallas_call(
         run_hidden,
         out_shape=jax.ShapeDtypeStruct((work, hid), bf16),
-        in_specs=[vmem()],
+        in_specs=[vmem()] * 5,
         out_specs=vmem(),
         compiler_params=params(),
         name="hidden",
-    )(parts)
+    )(scaled, gate0, gate1, up0, up1)
     hidden = lax.all_gather(hidden, "tp")
     branch = pl.pallas_call(
         branch_kernel,

time: 199 us -> 197 us (0.990)
  blocking collectives: 75.6 us -> 89 us
  between operations: 13.7 us -> 0.31 us
  local copies, waits for them, and re-layouts: 2.01 us -> 5.44 us
  starting transfers between devices: 59.9 us -> 56.5 us
  waiting for transfers between devices: 30.1 us -> 27.2 us
    all_to_all x1, blocking collectives: 16.9 us -> 29.8 us  [local(): scaled = lax.all_to_all(scaled, 'tp', 0, 0, tiled=True)]
    all_gather x1 -> x0, waiting for transfers between devices: 6.88 us -> none  [by_features(): w = lax.all_gather(w, 'tp')]
    unnamed x12 -> x14, local copies, waits for them, and re-layouts: 0.02 us -> 4.75 us
    all_to_all x1, starting transfers between devices: 8.96 us -> 4.63 us  [same_core_exchange(): lax.all_to_all(x, 'seq', 0, 0, tiled=True, axis_index_groups=same_core)]
    all_to_all x1 -> x0, starting transfers between devices: 4.26 us -> none  [by_features_now(): lax.all_to_all(w.reshape(tp_count, width, -1), 'tp', 0, 0, tiled=True)]
    ppermute x12 -> x13, starting transfers between devices: 32 us -> 35.8 us  [move(): return lax.ppermute(x, 'seq', route)]
    pallas_call x1, Pallas kernels: 3.02 us -> 0.39 us  [local(): pl.pallas_call(scale_kernel, out_shape=jax.ShapeDtypeStruct((tp_count, wo...]
    pallas_call x1, Pallas kernels: 0.34 us -> 2.83 us  [local(): pl.pallas_call(run_hidden, out_shape=jax.ShapeDtypeStruct((work, hid), bf...]
  transfers between devices with their start and end apart: 16 -> 15, of which waited for: 4 -> 3; matrix products, arithmetic and copies ran while one was open for 2% -> 1% of each run, Pallas kernels for 6% -> 3%
where the time goes in v6:
time: 197 us; the launch traced here: 196 us
  blocking collectives  89 us (45%)
  starting transfers between devices  56.5 us (29%)
  waiting for transfers between devices  27.2 us (14%)
  Pallas kernels  16 us (8%)
  local copies, waits for them, and re-layouts  5.44 us (3%)
    ppermute x13, starting transfers between devices, move(): return lax.ppermute(x, 'seq', route)  35.8 us
    all_to_all x1, blocking collectives, local(): scaled = lax.all_to_all(scaled, 'tp', 0, 0, tiled=True)  29.8 us
    all_to_all x1, blocking collectives, local(): finished = lax.all_to_all(pick(slot_of, returned), 'seq', 0, 0, tiled=True)  26.4 us
    all_to_all x1, blocking collectives, same_core_exchange(): lax.all_to_all(x, 'seq', 0, 0, tiled=True, axis_index_groups=same_core)  21.6 us
    all_to_all x1, waiting for transfers between devices, same_core_exchange(): lax.all_to_all(x, 'seq', 0, 0, tiled=True, axis_index_groups=same_core)  18 us
    all_to_all x1, starting transfers between devices, local(): lax.all_to_all(stream.reshape(seq_count, TILE, HEAD_DIM), 'seq', 0, 0, ti...  16 us
    all_gather x1, blocking collectives, local(): hidden = lax.all_gather(hidden, 'tp')  11.1 us
    all_to_all x1, waiting for transfers between devices, local(): lax.all_to_all(stream.reshape(seq_count, TILE, HEAD_DIM), 'seq', 0, 0, ti...  8.08 us
  transfers between devices with their start and end apart: 15, of which 3 were waited for; matrix products, arithmetic and copies ran while one was open for 1% of the time, Pallas kernels for 3%

profile of v6, /device:TPU:1, one launch (start us, length us, event | category | flops | bytes accessed | tf_op | source)
XLA Modules:
  0.0 196.1 jit_solution(13268441715599515268)
XLA Ops:
  0.0 4.0 %collective-permute-start = (bf16[128,1024]{1,0:T(8,128)(2,1)}, bf16[128,1024]{1,0:T(8,128)(2,1)S(1)}, u32[]{:S(2)}, u32[]{:S(2)}) collective-permute-start(bf16[128,1024]{1,0:T(8,128)(2,1)} %k0.1), channel_id=1, source_target_pairs={{0,8},{4,12},{8,16},{12,20},{16,24},{20,28},{24,32},{28,36},{32,40... | collective-permute-start | bytes 786440 | tf_op jit(solution)/shard_map/ppermute | solution.py:189
  4.0 3.2 %collective-permute-start.2 = (bf16[128,1024]{1,0:T(8,128)(2,1)}, bf16[128,1024]{1,0:T(8,128)(2,1)S(1)}, u32[]{:S(2)}, u32[]{:S(2)}) collective-permute-start(bf16[128,1024]{1,0:T(8,128)(2,1)} %v0.1), channel_id=1, source_target_pairs={{0,8},{4,12},{8,16},{12,20},{16,24},{20,28},{24,32},{28,36},{32,40... | collective-permute-start | bytes 786440 | tf_op jit(solution)/shard_map/ppermute | solution.py:189
  9.5 6.5 %collective-permute-start.4 = (bf16[128,1024]{1,0:T(8,128)(2,1)S(1)}, bf16[128,1024]{1,0:T(8,128)(2,1)}, u32[]{:S(2)}, u32[]{:S(2)}) collective-permute-start(bf16[128,1024]{1,0:T(8,128)(2,1)S(1)} %collective-permute-done.k1), channel_id=1, source_target_pairs={{0,4},{8,12},{16,20},{24,28},{32,36},{40,44},{48,52},{56,60},{64,6... | collective-permute-start | bytes 786440 | tf_op jit(solution)/shard_map/ppermute | solution.py:189
  16.0 4.0 %collective-permute-start.1 = (bf16[128,1024]{1,0:T(8,128)(2,1)S(1)}, bf16[128,1024]{1,0:T(8,128)(2,1)S(1)}, u32[]{:S(2)}, u32[]{:S(2)}) collective-permute-start(bf16[128,1024]{1,0:T(8,128)(2,1)S(1)} %collective-permute-done.k1), channel_id=1, source_target_pairs={{0,8},{4,12},{8,16},{12,20},{16,24},{20,28},{24,32},{28,36},{32,40... | collective-permute-start | bytes 786440 | tf_op jit(solution)/shard_map/ppermute | solution.py:189
  20.0 2.2 %collective-permute-start.5 = (bf16[128,1024]{1,0:T(8,128)(2,1)S(1)}, bf16[128,1024]{1,0:T(8,128)(2,1)}, u32[]{:S(2)}, u32[]{:S(2)}) collective-permute-start(bf16[128,1024]{1,0:T(8,128)(2,1)S(1)} %collective-permute-done.2.v1), channel_id=1, source_target_pairs={{0,4},{8,12},{16,20},{24,28},{32,36},{40,44},{48,52},{56,60},{64,6... | collective-permute-start | bytes 786440 | tf_op jit(solution)/shard_map/ppermute | solution.py:189
  22.2 1.6 collective-permute-start.3
  25.4 1.4 collective-permute-start.8
  30.7 3.2 %attend_near.1 = (f32[128,1024]{1,0:T(8,128)S(1)}, f32[2,128,128]{2,1,0:T(8,128)S(1)}) custom-call(s32[2]{0:T(128)S(1)} %pad_add_fusion.place, bf16[128,1024]{1,0:T(8,128)(2,1)S(1)} %copy-done.2, bf16[128,1024]{1,0:T(8,128)(2,1)S(1)} %copy-done.5, bf16[128,1024]{1,0:T(8,128)(2,1)S(1)} %collective-permute-done.k1, ...), custom_call_target="tpu_custom_call" | custom-call | tf_op jit(solution)/shard_map/attend_near/pallas_call | solution.py:220
  33.9 3.1 %collective-permute-start.7 = (bf16[128,1024]{1,0:T(8,128)(2,1)S(1)}, bf16[128,1024]{1,0:T(8,128)(2,1)S(1)}, u32[]{:S(2)}, u32[]{:S(2)}) collective-permute-start(bf16[128,1024]{1,0:T(8,128)(2,1)S(1)} %collective-permute-done.1.k2), channel_id=1, source_target_pairs={{4,0},{12,8},{20,16},{28,24},{36,32},{44,40},{52,48},{60,56},{68,6... | collective-permute-start | bytes 786440 | tf_op jit(solution)/shard_map/ppermute | solution.py:189
  40.4 4.0 %attend_far.1 = (bf16[8,8,2,8,128]{4,3,2,1,0:T(8,128)(2,1)}, bf16[128,1024]{1,0:T(8,128)(2,1)S(1)}) custom-call(s32[2]{0:T(128)S(1)} %pad_add_fusion.place, bf16[128,1024]{1,0:T(8,128)(2,1)S(1)} %copy-done.2, bf16[128,1024]{1,0:T(8,128)(2,1)S(1)} %collective-permute-done.1.k2, bf16[128,1024]{1,0:T(8,128)(2,1)S(1)} %collective-permute-done.6.kx0, ...), custom_call_target="tpu_custom_call" | custom-call | tf_op jit(solution)/shard_map/attend_far/pallas_call | solution.py:234
  44.4 16.0 %all-to-all-start = ((bf16[128,8,128]{2,1,0:T(8,128)(2,1)}), bf16[128,8,128]{2,1,0:T(8,128)(2,1)S(1)}, u32[]{:S(2)}, u32[]{:S(2)}) async-start(bf16[128,8,128]{2,1,0:T(8,128)(2,1)} %bitcast.4), calls=%async_computation | async-start | bytes 524288 | tf_op jit(solution)/shard_map/all_to_all | solution.py:246
  60.4 2.8 %collective-permute-start.10 = (bf16[4096,128]{1,0:T(8,128)(2,1)S(1)}, bf16[4096,128]{1,0:T(8,128)(2,1)}, u32[]{:S(2)}, u32[]{:S(2)}) collective-permute-start(bf16[4096,128]{1,0:T(8,128)(2,1)S(1)} %bitcast.19), channel_id=1, source_target_pairs={{0,4},{8,12},{16,20},{24,28},{32,36},{40,44},{48,52},{56,60},{64,6... | collective-permute-start | bytes 3145736 | tf_op jit(solution)/shard_map/ppermute | solution.py:189
  63.3 1.9 collective-permute-start.11
  65.2 2.4 %collective-permute-start.12 = (bf16[512,1024]{1,0:T(8,128)(2,1)}, bf16[512,1024]{1,0:T(8,128)(2,1)}, u32[]{:S(2)}, u32[]{:S(2)}) collective-permute-start(bf16[512,1024]{1,0:T(8,128)(2,1)} %bitcast.8.down0), channel_id=1, source_target_pairs={{0,4},{8,12},{16,20},{24,28},{32,36},{40,44},{48,52},{56,60},{64,6... | collective-permute-start | bytes 3145736 | tf_op jit(solution)/shard_map/ppermute | solution.py:189
  67.6 8.1 %all-to-all-done.tiles = bf16[128,8,128]{2,1,0:T(8,128)(2,1)S(1)} async-done(((bf16[128,8,128]{2,1,0:T(8,128)(2,1)}), bf16[128,8,128]{2,1,0:T(8,128)(2,1)S(1)}, u32[]{:S(2)}, u32[]{:S(2)}) %all-to-all-start) | async-done | bytes 262176 | tf_op jit(solution)/shard_map/all_to_all | solution.py:246
  75.7 1.8 pick.2
  77.5 4.6 %all-to-all-start.1 = ((bf16[64,4,8,128]{3,2,1,0:T(8,128)(2,1)}), bf16[64,4,8,128]{3,2,1,0:T(8,128)(2,1)S(1)}, u32[]{:S(2)}, u32[]{:S(2)}) async-start(bf16[64,4,8,128]{3,2,1,0:T(8,128)(2,1)} %bitcast.5), calls=%async_computation.1 | async-start | bytes 1048576 | tf_op jit(solution)/shard_map/all_to_all | solution.py:262
  82.1 18.0 %all-to-all-done.1 = bf16[64,4,8,128]{3,2,1,0:T(8,128)(2,1)S(1)} async-done(((bf16[64,4,8,128]{3,2,1,0:T(8,128)(2,1)}), bf16[64,4,8,128]{3,2,1,0:T(8,128)(2,1)S(1)}, u32[]{:S(2)}, u32[]{:S(2)}) %all-to-all-start.1) | async-done | bytes 524320 | tf_op jit(solution)/shard_map/all_to_all | solution.py:262
  100.5 29.8 %all_to_all.25.refs_0_ = bf16[4,272,1024]{2,1,0:T(8,128)(2,1)S(1)} all-to-all(bf16[4,272,1024]{2,1,0:T(8,128)(2,1)S(1)} %scale.1), channel_id=1, replica_groups=mesh['seq'=128,'tp'=4] {'tp'}, dimensions={0} | all-to-all | bytes 4456448 | tf_op jit(solution)/shard_map/all_to_all | solution.py:277
  130.3 2.8 %hidden.1 = bf16[256,256]{1,0:T(8,128)(2,1)S(1)} custom-call(bf16[4,272,1024]{2,1,0:T(8,128)(2,1)S(1)} %all_to_all.25.refs_0_, bf16[4096,128]{1,0:T(8,128)(2,1)S(1)} %bitcast.20, bf16[4096,128]{1,0:T(8,128)(2,1)} %collective-permute-done.10.refs_2_, bf16[4096,128]{1,0:T(8,128)(2,1)S(1)} %bitcast.22, bf16[4096,128]{1,0:T(8,128)(2,1)} %collective-permute-done.11.refs_4_), custom_call_target="tpu_custom_call" | custom-call | tf_op jit(solution)/shard_map/hidden/pallas_call | solution.py:282
  133.2 11.1 %all-gather = bf16[1024,256]{1,0:T(8,128)(2,1)S(1)} all-gather(bf16[256,256]{1,0:T(8,128)(2,1)S(1)} %hidden.1), channel_id=2, replica_groups=mesh['seq'=128,'tp'=4] {'tp'}, dimensions={0}, use_global_device_ids=true | all-gather | bytes 655360 | tf_op jit(solution)/shard_map/all_gather | solution.py:290
  144.3 2.2 %branch.1 = bf16[8,8,4,8,128]{4,3,2,1,0:T(8,128)(2,1)S(1)} custom-call(bf16[4,256,256]{2,1,0:T(8,128)(2,1)S(1)} %bitcast.15, bf16[512,1024]{1,0:T(8,128)(2,1)} %bitcast.8.down0, bf16[512,1024]{1,0:T(8,128)(2,1)} %collective-permute-done.12.down1), custom_call_target="tpu_custom_call" | custom-call | tf_op jit(solution)/shard_map/branch/pallas_call | solution.py:291
  146.5 21.6 %all_to_all.26 = bf16[64,4,8,128]{3,2,1,0:T(8,128)(2,1)S(1)} all-to-all(bf16[64,4,8,128]{3,2,1,0:T(8,128)(2,1)S(1)} %bitcast.18), channel_id=1, replica_groups={{0,8,16,24,32,40,48,56,64,72,80,88,96,104,112,120,128,136,144,152,160,1..., dimensions={0} | all-to-all | bytes 1048576 | tf_op jit(solution)/shard_map/all_to_all | solution.py:262
  168.9 26.4 %all_to_all.27 = bf16[128,8,128]{2,1,0:T(8,128)(2,1)S(1)} all-to-all(bf16[128,8,128]{2,1,0:T(8,128)(2,1)S(1)} %pick.3), channel_id=1, replica_groups=mesh['seq'=128,'tp'=4] {'seq'}, dimensions={0} | all-to-all | bytes 524288 | tf_op jit(solution)/shard_map/all_to_all | solution.py:300
  (37 shorter events, 12.8 us)
Async XLA Ops:
  0.0 9.5 %collective-permute-start = (bf16[128,1024]{1,0:T(8,128)(2,1)}, bf16[128,1024]{1,0:T(8,128)(2,1)S(1)}, u32[]{:S(2)}, u32[]{:S(2)}) collective-permute-start(bf16[128,1024]{1,0:T(8,128)(2,1)} %k0.1), channel_id=1, source_target_pairs={{0,8},{4,12},{8,16},{12,20},{16,24},{20,28},{24,32},{28,36},{32,40... | collective-permute-start | bytes 786440 | tf_op jit(solution)/shard_map/ppermute | solution.py:189
  4.0 15.9 %collective-permute-start.2 = (bf16[128,1024]{1,0:T(8,128)(2,1)}, bf16[128,1024]{1,0:T(8,128)(2,1)S(1)}, u32[]{:S(2)}, u32[]{:S(2)}) collective-permute-start(bf16[128,1024]{1,0:T(8,128)(2,1)} %v0.1), channel_id=1, source_target_pairs={{0,8},{4,12},{8,16},{12,20},{16,24},{20,28},{24,32},{28,36},{32,40... | collective-permute-start | bytes 786440 | tf_op jit(solution)/shard_map/ppermute | solution.py:189
  7.3 31.1 %collective-permute-start.6 = (bf16[128,1024]{1,0:T(8,128)(2,1)}, bf16[128,1024]{1,0:T(8,128)(2,1)S(1)}, u32[]{:S(2)}, u32[]{:S(2)}) collective-permute-start(bf16[128,1024]{1,0:T(8,128)(2,1)} %k0.1), channel_id=1, source_target_pairs={{0,4},{8,12},{16,20},{24,28},{32,36},{40,44},{48,52},{56,60},{64,6... | collective-permute-start | bytes 786440 | tf_op jit(solution)/shard_map/ppermute | solution.py:189
  9.5 15.9 %collective-permute-start.4 = (bf16[128,1024]{1,0:T(8,128)(2,1)S(1)}, bf16[128,1024]{1,0:T(8,128)(2,1)}, u32[]{:S(2)}, u32[]{:S(2)}) collective-permute-start(bf16[128,1024]{1,0:T(8,128)(2,1)S(1)} %collective-permute-done.k1), channel_id=1, source_target_pairs={{0,4},{8,12},{16,20},{24,28},{32,36},{40,44},{48,52},{56,60},{64,6... | collective-permute-start | bytes 786440 | tf_op jit(solution)/shard_map/ppermute | solution.py:189
  16.0 18.0 %collective-permute-start.1 = (bf16[128,1024]{1,0:T(8,128)(2,1)S(1)}, bf16[128,1024]{1,0:T(8,128)(2,1)S(1)}, u32[]{:S(2)}, u32[]{:S(2)}) collective-permute-start(bf16[128,1024]{1,0:T(8,128)(2,1)S(1)} %collective-permute-done.k1), channel_id=1, source_target_pairs={{0,8},{4,12},{8,16},{12,20},{16,24},{20,28},{24,32},{28,36},{32,40... | collective-permute-start | bytes 786440 | tf_op jit(solution)/shard_map/ppermute | solution.py:189
  20.0 6.9 %collective-permute-start.5 = (bf16[128,1024]{1,0:T(8,128)(2,1)S(1)}, bf16[128,1024]{1,0:T(8,128)(2,1)}, u32[]{:S(2)}, u32[]{:S(2)}) collective-permute-start(bf16[128,1024]{1,0:T(8,128)(2,1)S(1)} %collective-permute-done.2.v1), channel_id=1, source_target_pairs={{0,4},{8,12},{16,20},{24,28},{32,36},{40,44},{48,52},{56,60},{64,6... | collective-permute-start | bytes 786440 | tf_op jit(solution)/shard_map/ppermute | solution.py:189
  22.2 11.7 %collective-permute-start.3 = (bf16[128,1024]{1,0:T(8,128)(2,1)S(1)}, bf16[128,1024]{1,0:T(8,128)(2,1)S(1)}, u32[]{:S(2)}, u32[]{:S(2)}) collective-permute-start(bf16[128,1024]{1,0:T(8,128)(2,1)S(1)} %collective-permute-done.2.v1), channel_id=1, source_target_pairs={{0,8},{4,12},{8,16},{12,20},{16,24},{20,28},{24,32},{28,36},{32,40... | collective-permute-start | bytes 786440 | tf_op jit(solution)/shard_map/ppermute | solution.py:189
  25.4 35.0 %copy-start = (bf16[1,4096,128]{2,1,0:T(8,128)(2,1)S(1)}, bf16[1,4096,128]{2,1,0:T(8,128)(2,1)}, u32[]{:S(2)}) copy-start(bf16[1,4096,128]{2,1,0:T(8,128)(2,1)} %param.15) | copy-start | bytes 3145732
  25.4 37.8 %copy-start.1 = (bf16[1,4096,128]{2,1,0:T(8,128)(2,1)S(1)}, bf16[1,4096,128]{2,1,0:T(8,128)(2,1)}, u32[]{:S(2)}) copy-start(bf16[1,4096,128]{2,1,0:T(8,128)(2,1)} %param.16) | copy-start | bytes 3145732
  25.4 12.9 %collective-permute-start.8 = (bf16[128,1024]{1,0:T(8,128)(2,1)}, bf16[128,1024]{1,0:T(8,128)(2,1)S(1)}, u32[]{:S(2)}, u32[]{:S(2)}) collective-permute-start(bf16[128,1024]{1,0:T(8,128)(2,1)} %v0.1), channel_id=1, source_target_pairs={{0,4},{8,12},{16,20},{24,28},{32,36},{40,44},{48,52},{56,60},{64,6... | collective-permute-start | bytes 786440 | tf_op jit(solution)/shard_map/ppermute | solution.py:189
  26.9 1.0 copy-start.2
  27.8 0.9 copy-start.3
  28.8 0.9 copy-start.5
  29.7 0.9 copy-start.6
  33.9 4.4 %collective-permute-start.7 = (bf16[128,1024]{1,0:T(8,128)(2,1)S(1)}, bf16[128,1024]{1,0:T(8,128)(2,1)S(1)}, u32[]{:S(2)}, u32[]{:S(2)}) collective-permute-start(bf16[128,1024]{1,0:T(8,128)(2,1)S(1)} %collective-permute-done.1.k2), channel_id=1, source_target_pairs={{4,0},{12,8},{20,16},{28,24},{36,32},{44,40},{52,48},{60,56},{68,6... | collective-permute-start | bytes 786440 | tf_op jit(solution)/shard_map/ppermute | solution.py:189
  37.0 2.4 %collective-permute-start.9 = (bf16[128,1024]{1,0:T(8,128)(2,1)S(1)}, bf16[128,1024]{1,0:T(8,128)(2,1)S(1)}, u32[]{:S(2)}, u32[]{:S(2)}) collective-permute-start(bf16[128,1024]{1,0:T(8,128)(2,1)S(1)} %collective-permute-done.3.v2), channel_id=1, source_target_pairs={{4,0},{12,8},{20,16},{28,24},{36,32},{44,40},{52,48},{60,56},{68,6... | collective-permute-start | bytes 786440 | tf_op jit(solution)/shard_map/ppermute | solution.py:189
  39.5 0.9 copy-start.4
  44.4 31.3 %all-to-all-start = ((bf16[128,8,128]{2,1,0:T(8,128)(2,1)}), bf16[128,8,128]{2,1,0:T(8,128)(2,1)S(1)}, u32[]{:S(2)}, u32[]{:S(2)}) async-start(bf16[128,8,128]{2,1,0:T(8,128)(2,1)} %bitcast.4), calls=%async_computation | async-start | bytes 524288 | tf_op jit(solution)/shard_map/all_to_all | solution.py:246
  60.4 21.7 %collective-permute-start.10 = (bf16[4096,128]{1,0:T(8,128)(2,1)S(1)}, bf16[4096,128]{1,0:T(8,128)(2,1)}, u32[]{:S(2)}, u32[]{:S(2)}) collective-permute-start(bf16[4096,128]{1,0:T(8,128)(2,1)S(1)} %bitcast.19), channel_id=1, source_target_pairs={{0,4},{8,12},{16,20},{24,28},{32,36},{40,44},{48,52},{56,60},{64,6... | collective-permute-start | bytes 3145736 | tf_op jit(solution)/shard_map/ppermute | solution.py:189
  63.3 18.9 %collective-permute-start.11 = (bf16[4096,128]{1,0:T(8,128)(2,1)S(1)}, bf16[4096,128]{1,0:T(8,128)(2,1)}, u32[]{:S(2)}, u32[]{:S(2)}) collective-permute-start(bf16[4096,128]{1,0:T(8,128)(2,1)S(1)} %bitcast.21), channel_id=1, source_target_pairs={{0,4},{8,12},{16,20},{24,28},{32,36},{40,44},{48,52},{56,60},{64,6... | collective-permute-start | bytes 3145736 | tf_op jit(solution)/shard_map/ppermute | solution.py:189
  65.2 16.9 %collective-permute-start.12 = (bf16[512,1024]{1,0:T(8,128)(2,1)}, bf16[512,1024]{1,0:T(8,128)(2,1)}, u32[]{:S(2)}, u32[]{:S(2)}) collective-permute-start(bf16[512,1024]{1,0:T(8,128)(2,1)} %bitcast.8.down0), channel_id=1, source_target_pairs={{0,4},{8,12},{16,20},{24,28},{32,36},{40,44},{48,52},{56,60},{64,6... | collective-permute-start | bytes 3145736 | tf_op jit(solution)/shard_map/ppermute | solution.py:189
  77.5 22.6 %all-to-all-start.1 = ((bf16[64,4,8,128]{3,2,1,0:T(8,128)(2,1)}), bf16[64,4,8,128]{3,2,1,0:T(8,128)(2,1)S(1)}, u32[]{:S(2)}, u32[]{:S(2)}) async-start(bf16[64,4,8,128]{3,2,1,0:T(8,128)(2,1)} %bitcast.5), calls=%async_computation.1 | async-start | bytes 1048576 | tf_op jit(solution)/shard_map/all_to_all | solution.py:262

commit v7 on v4

--- a/solution.py
+++ b/solution.py
@@ -47,8 +47,7 @@
     shift1 = jnp.where(place[0] >= 1, 0, jnp.int32(4 * BLOCK))
     past = diff + BLOCK > shift1
     visible = jnp.concatenate([past, past, diff <= 0], axis=1)
-    tops = jnp.zeros((BLOCK, HEAD_DIM), f32)
-    sums = jnp.zeros((BLOCK, HEAD_DIM), f32)
+    ones = jnp.ones((3 * BLOCK, HEAD_DIM), bf16)
     for h in range(q.shape[1] // HEAD_DIM):
         s = slice(h * HEAD_DIM, (h + 1) * HEAD_DIM)
         keys = jnp.concatenate([kv[:BLOCK, s] for kv in (kv1, kvx1, kv0)], axis=0)
@@ -56,12 +55,11 @@
         scores = dot_t(q[:, s], keys) * (1.0 / math.sqrt(HEAD_DIM))
         scores = jnp.where(visible, scores, masked_score)
         top = jnp.max(scores, axis=1, keepdims=True)
-        expo = jnp.exp(scores - top)
-        tops = jnp.where(col == h, top, tops)
-        sums = jnp.where(col == h, jnp.sum(expo, axis=1, keepdims=True), sums)
-        held[:, s] = dot(expo.astype(bf16), values)
-    stats[0] = tops
-    stats[1] = sums
+        expo = jnp.exp(scores - top).astype(bf16)
+        both = dot(expo, jnp.concatenate([values, ones], axis=1))
+        held[:, s] = both[:, :HEAD_DIM]
+        stats[0, :, s] = jnp.broadcast_to(top, (BLOCK, HEAD_DIM))
+        stats[1, :, s] = both[:, HEAD_DIM:]
 
 
 def attend_far_kernel(place, q, kv2, kvx0, kvx2, held, stats, res, out, home):
@@ -73,7 +71,9 @@
     big = jnp.int32(4 * BLOCK)
     shift2 = jnp.where(chip >= 2, 0, big)
     shiftx = jnp.where((chip >= 2) | (core == 1), 0, big)
-    visible = jnp.concatenate([diff > shift2, diff + BLOCK > shiftx], axis=1)
+    seen2 = diff > shift2
+    seenx = diff + BLOCK > shiftx
+    ones = jnp.ones((2 * BLOCK, HEAD_DIM), bf16)
     z_count, core_count = out.shape[0], out.shape[2]
     for h in range(q.shape[1] // HEAD_DIM):
         s = slice(h * HEAD_DIM, (h + 1) * HEAD_DIM)
@@ -81,14 +81,17 @@
         keys = jnp.concatenate([kv2[:BLOCK, s], kvx[:BLOCK]], axis=0)
         values = jnp.concatenate([kv2[BLOCK:, s], kvx[BLOCK:]], axis=0)
         scores = dot_t(q[:, s], keys) * (1.0 / math.sqrt(HEAD_DIM))
-        scores = jnp.where(visible, scores, masked_score)
-        near_top = stats[0, :, h : h + 1]
-        top = jnp.maximum(near_top, jnp.max(scores, axis=1, keepdims=True))
-        expo = jnp.exp(scores - top)
+        score2 = jnp.where(seen2, scores[:, :BLOCK], masked_score)
+        scorex = jnp.where(seenx, scores[:, BLOCK:], masked_score)
+        near_top = stats[0, :, s]
+        top = jnp.max(jnp.maximum(score2, scorex), axis=1, keepdims=True)
+        top = jnp.maximum(near_top, top)
+        expo = jnp.concatenate([jnp.exp(score2 - top), jnp.exp(scorex - top)], axis=1)
+        both = dot(expo.astype(bf16), jnp.concatenate([values, ones], axis=1))
         scale = jnp.exp(near_top - top)
-        total = stats[1, :, h : h + 1] * scale + jnp.sum(expo, axis=1, keepdims=True)
-        summed = held[:, s] * scale + dot(expo.astype(bf16), values)
-        stream = res[:, s].astype(f32) + summed * (1.0 / total)
+        total = stats[1, :, s] * scale + both[:, HEAD_DIM:]
+        summed = held[:, s] * scale + both[:, :HEAD_DIM]
+        stream = res[:, s].astype(f32) + summed / total
         home[:, s] = stream.astype(bf16)
         out[:, h] = stream.reshape(z_count, core_count, TILE, HEAD_DIM).astype(bf16)
 
@@ -126,22 +129,24 @@
 
 def hidden_kernel(features, parts, out):
     count = parts.shape[0]
-    rows, width = out.shape
+    rows, width = out.shape[1:]
     tail = parts.shape[1] - rows
-    sums = parts[:, rows:, :rows].reshape(count * tail, rows)
+    squares = parts[:, rows:, :rows].reshape(count * tail, rows)
     weight = jnp.full((count * tail, HEAD_DIM), 1.0 / TILE, bf16)
     square = lax.dot_general(
-        sums, weight, (((0,), (0,)), ((), ())), preferred_element_type=f32
+        squares, weight, (((0,), (0,)), ((), ())), preferred_element_type=f32
     )
     factor = lax.rsqrt(square * (1.0 / features) + epsilon)
     half = width // 2
     for k in range(2):
-        value = sum(
+        sums = sum(
             parts[t, :rows, k * width : (k + 1) * width].astype(f32) for t in range(count)
         )
-        gate = value[:, :half] * factor
-        up = value[:, half:] * factor
-        out[:, k * half : (k + 1) * half] = (gate / (1.0 + jnp.exp(-gate)) * up).astype(bf16)
+        gate = sums[:, :half] * factor
+        up = sums[:, half:] * factor
+        value = (gate / (1.0 + jnp.exp(-gate)) * up).astype(bf16)
+        for t in range(count):
+            out[t, :, k * half : (k + 1) * half] = value
 
 
 def branch_kernel(hidden, down0, down1, out):
@@ -219,7 +224,7 @@
         attend_near_kernel,
         out_shape=(
             jax.ShapeDtypeStruct((rows, width), f32),
-            jax.ShapeDtypeStruct((2, BLOCK, HEAD_DIM), f32),
+            jax.ShapeDtypeStruct((2, rows, width), f32),
         ),
         in_specs=[smem()] + [vmem()] * 5,
         out_specs=(vmem(), vmem()),
@@ -281,13 +286,13 @@
 
     hidden = pl.pallas_call(
         run_hidden,
-        out_shape=jax.ShapeDtypeStruct((work, hid), bf16),
+        out_shape=jax.ShapeDtypeStruct((tp_count, work, hid), bf16),
         in_specs=[vmem()],
         out_specs=vmem(),
         compiler_params=params(),
         name="hidden",
     )(parts)
-    hidden = lax.all_gather(hidden, "tp")
+    hidden = lax.all_to_all(hidden, "tp", 0, 0, tiled=True)
     branch = pl.pallas_call(
         branch_kernel,
         out_shape=jax.ShapeDtypeStruct((z_count, heads, slots, TILE, HEAD_DIM), bf16),

time: 188 us -> 184 us (0.979)
  Pallas kernels: 13.2 us -> 10.2 us
  blocking collectives: 133 us -> 131 us
    all_gather x1 -> x0, blocking collectives: 10.4 us -> none  [local(): hidden = lax.all_gather(hidden, 'tp')]
    all_to_all x0 -> x1, blocking collectives: none -> 9.33 us  [local(): hidden = lax.all_to_all(hidden, 'tp', 0, 0, tiled=True)]
    pallas_call x1, Pallas kernels: 3.8 us -> 1.91 us  [local(): pl.pallas_call(attend_far_kernel, out_shape=(jax.ShapeDtypeStruct((z_coun...]
  transfers between devices with their start and end apart: 8 -> 8, of which waited for: 3 -> 3; matrix products, arithmetic and copies ran while one was open for 2% -> 2% of each run, Pallas kernels for 4% -> 3%
where the time goes in v7:
time: 184 us; the launch traced here: 183 us
  blocking collectives  131 us (71%)
  starting transfers between devices  25.1 us (14%)
  waiting for transfers between devices  10.4 us (6%)
  Pallas kernels  10.2 us (6%)
  other arithmetic  3.48 us (2%)
  local copies, waits for them, and re-layouts  2.65 us (1%)
    all_to_all x2, blocking collectives, same_core_exchange(): lax.all_to_all(x, 'seq', 0, 0, tiled=True, axis_index_groups=same_core)  44 us
    all_to_all x1, blocking collectives, local(): lax.all_to_all(stream.reshape(seq_count, TILE, HEAD_DIM), 'seq', 0, 0, ti...  34.1 us
    all_to_all x1, blocking collectives, local(): finished = lax.all_to_all(pick(slot_of, returned), 'seq', 0, 0, tiled=True)  26.2 us
    ppermute x7, starting transfers between devices, move(): return lax.ppermute(x, 'seq', route)  21 us
    all_to_all x1, blocking collectives, local(): parts = lax.all_to_all(parts, 'tp', 0, 0, tiled=True)  17.7 us
    ppermute x7, waiting for transfers between devices, move(): return lax.ppermute(x, 'seq', route)  10.4 us
    all_to_all x1, blocking collectives, local(): hidden = lax.all_to_all(hidden, 'tp', 0, 0, tiled=True)  9.33 us
    all_to_all x1, starting transfers between devices, local(): first0 = lax.all_to_all(both, 'tp', 0, 0, tiled=True)  4.14 us
  transfers between devices with their start and end apart: 8, of which 3 were waited for; matrix products, arithmetic and copies ran while one was open for 2% of the time, Pallas kernels for 3%

profile of v7, /device:TPU:1, one launch (start us, length us, event | category | flops | bytes accessed | tf_op | source)
XLA Modules:
  0.0 183.4 jit_solution(10066870694710904032)
XLA Ops:
  0.0 1.0 constant_dynamic-update-slice_fusion.1
  1.0 1.0 constant_dynamic-update-slice_fusion.kv0
  1.9 4.8 %collective-permute-start = (bf16[256,1024]{1,0:T(8,128)(2,1)S(1)}, bf16[256,1024]{1,0:T(8,128)(2,1)}, u32[]{:S(2)}, u32[]{:S(2)}) collective-permute-start(bf16[256,1024]{1,0:T(8,128)(2,1)S(1)} %constant_dynamic-update-slice_fusion.kv0), channel_id=1, source_target_pairs={{0,8},{4,12},{8,16},{12,20},{16,24},{20,28},{24,32},{28,36},{32,40... | collective-permute-start | bytes 1572872 | tf_op jit(solution)/shard_map/ppermute | solution.py:193
  6.8 3.1 %pad_maximum_fusion = bf16[4096,256]{1,0:T(8,128)(2,1)} fusion(bf16[4096,128]{1,0:T(8,128)(2,1)} %bitcast.25, bf16[4096,128]{1,0:T(8,128)(2,1)} %bitcast.26), kind=kLoop, calls=%fused_computation | loop fusion | flops 4194304 | bytes 4194304 | tf_op jit(solution)/shard_map/concatenate | solution.py:204
  9.9 4.1 %all-to-all-start = ((bf16[4,1024,256]{2,1,0:T(8,128)(2,1)}), bf16[4,1024,256]{2,1,0:T(8,128)(2,1)S(1)}, u32[]{:S(2)}, u32[]{:S(2)}) async-start(bf16[4,1024,256]{2,1,0:T(8,128)(2,1)} %bitcast.24), calls=%async_computation | async-start | bytes 4194304 | tf_op jit(solution)/shard_map/all_to_all | solution.py:205
  14.0 1.3 collective-permute-start.3
  15.3 6.4 %collective-permute-start.5 = (bf16[512,1024]{1,0:T(8,128)(2,1)}, bf16[512,1024]{1,0:T(8,128)(2,1)}, u32[]{:S(2)}, u32[]{:S(2)}) collective-permute-start(bf16[512,1024]{1,0:T(8,128)(2,1)} %bitcast.19), channel_id=1, source_target_pairs={{0,4},{8,12},{16,20},{24,28},{32,36},{40,44},{48,52},{56,60},{64,6... | collective-permute-start | bytes 3145736 | tf_op jit(solution)/shard_map/ppermute | solution.py:193
  22.5 1.9 %collective-permute-start.2 = (bf16[256,1024]{1,0:T(8,128)(2,1)}, bf16[256,1024]{1,0:T(8,128)(2,1)S(1)}, u32[]{:S(2)}, u32[]{:S(2)}) collective-permute-start(bf16[256,1024]{1,0:T(8,128)(2,1)} %collective-permute-done.kv1), channel_id=1, source_target_pairs={{0,4},{8,12},{16,20},{24,28},{32,36},{40,44},{48,52},{56,60},{64,6... | collective-permute-start | bytes 1572872 | tf_op jit(solution)/shard_map/ppermute | solution.py:193
  24.4 1.3 collective-permute-start.1
  26.5 2.1 %attend_near.1 = (f32[128,1024]{1,0:T(8,128)S(1)}, f32[2,128,1024]{2,1,0:T(8,128)S(1)}) custom-call(s32[2]{0:T(128)S(1)} %pad_add_fusion.place, bf16[128,1024]{1,0:T(8,128)(2,1)S(1)} %copy-done.1, bf16[256,1024]{1,0:T(8,128)(2,1)S(1)} %constant_dynamic-update-slice_fusion.kv0, bf16[256,1024]{1,0:T(8,128)(2,1)} %collective-permute-done.kv1, ...), custom_call_target="tpu_custom_call" | custom-call | tf_op jit(solution)/shard_map/attend_near/pallas_call | solution.py:223
  28.6 8.5 %collective-permute-done.1.kv2 = bf16[256,1024]{1,0:T(8,128)(2,1)S(1)} collective-permute-done((bf16[256,1024]{1,0:T(8,128)(2,1)}, bf16[256,1024]{1,0:T(8,128)(2,1)S(1)}, u32[]{:S(2)}, u32[]{:S(2)}) %collective-permute-start.1) | collective-permute-done | bytes 524320 | tf_op jit(solution)/shard_map/ppermute | solution.py:193
  37.1 2.9 %collective-permute-start.4 = (bf16[256,1024]{1,0:T(8,128)(2,1)S(1)}, bf16[256,1024]{1,0:T(8,128)(2,1)S(1)}, u32[]{:S(2)}, u32[]{:S(2)}) collective-permute-start(bf16[256,1024]{1,0:T(8,128)(2,1)S(1)} %collective-permute-done.1.kv2), channel_id=1, source_target_pairs={{4,0},{12,8},{20,16},{28,24},{36,32},{44,40},{52,48},{60,56},{68,6... | collective-permute-start | bytes 1572872 | tf_op jit(solution)/shard_map/ppermute | solution.py:193
  40.1 1.5 collective-permute-done.4.kvx2
  41.6 1.9 %attend_far.1 = (bf16[8,8,2,8,128]{4,3,2,1,0:T(8,128)(2,1)S(1)}, bf16[128,1024]{1,0:T(8,128)(2,1)S(1)}) custom-call(s32[2]{0:T(128)S(1)} %pad_add_fusion.place, bf16[128,1024]{1,0:T(8,128)(2,1)S(1)} %copy-done.1, bf16[256,1024]{1,0:T(8,128)(2,1)S(1)} %collective-permute-done.1.kv2, bf16[256,1024]{1,0:T(8,128)(2,1)} %collective-permute-done.3.kvx0, ...), custom_call_target="tpu_custom_call" | custom-call | tf_op jit(solution)/shard_map/attend_far/pallas_call | solution.py:236
  43.5 34.1 %all_to_all.35.tiles = bf16[128,8,128]{2,1,0:T(8,128)(2,1)S(1)} all-to-all(bf16[128,8,128]{2,1,0:T(8,128)(2,1)S(1)} %bitcast.22), channel_id=1, replica_groups=mesh['seq'=128,'tp'=4] {'seq'}, dimensions={0} | all-to-all | bytes 524288 | tf_op jit(solution)/shard_map/all_to_all | solution.py:249
  77.6 2.3 %collective-permute-start.6 = (bf16[4,1024,256]{2,1,0:T(8,128)(2,1)S(1)}, bf16[4,1024,256]{2,1,0:T(8,128)(2,1)S(1)}, u32[]{:S(2)}, u32[]{:S(2)}) collective-permute-start(bf16[4,1024,256]{2,1,0:T(8,128)(2,1)S(1)} %all-to-all-done.first0), channel_id=1, source_target_pairs={{0,4},{8,12},{16,20},{24,28},{32,36},{40,44},{48,52},{56,60},{64,6... | collective-permute-start | bytes 6291464 | tf_op jit(solution)/shard_map/ppermute | solution.py:193
  79.9 1.0 pick.2
  80.8 21.9 %all_to_all.36 = bf16[64,4,8,128]{3,2,1,0:T(8,128)(2,1)S(1)} all-to-all(bf16[64,4,8,128]{3,2,1,0:T(8,128)(2,1)S(1)} %bitcast.16), channel_id=1, replica_groups={{0,8,16,24,32,40,48,56,64,72,80,88,96,104,112,120,128,136,144,152,160,1..., dimensions={0} | all-to-all | bytes 1048576 | tf_op jit(solution)/shard_map/all_to_all | solution.py:265
  102.8 1.4 project.1
  104.2 17.7 %all_to_all.37.parts_ref = bf16[4,272,512]{2,1,0:T(8,128)(2,1)S(1)} all-to-all(bf16[4,272,512]{2,1,0:T(8,128)(2,1)S(1)} %project.1), channel_id=1, replica_groups=mesh['seq'=128,'tp'=4] {'tp'}, dimensions={0} | all-to-all | bytes 2228224 | tf_op jit(solution)/shard_map/all_to_all | solution.py:282
  122.3 9.3 %all_to_all.38.hidden = bf16[4,256,256]{2,1,0:T(8,128)(2,1)S(1)} all-to-all(bf16[4,256,256]{2,1,0:T(8,128)(2,1)S(1)} %hidden.1), channel_id=1, replica_groups=mesh['seq'=128,'tp'=4] {'tp'}, dimensions={0} | all-to-all | bytes 1048576 | tf_op jit(solution)/shard_map/all_to_all | solution.py:295
  131.6 1.9 %branch.1 = bf16[8,8,4,8,128]{4,3,2,1,0:T(8,128)(2,1)S(1)} custom-call(bf16[4,256,256]{2,1,0:T(8,128)(2,1)S(1)} %all_to_all.38.hidden, bf16[512,1024]{1,0:T(8,128)(2,1)S(1)} %bitcast.20, bf16[512,1024]{1,0:T(8,128)(2,1)} %collective-permute-done.5.down1), custom_call_target="tpu_custom_call" | custom-call | tf_op jit(solution)/shard_map/branch/pallas_call | solution.py:296
  133.5 22.1 %all_to_all.39 = bf16[64,4,8,128]{3,2,1,0:T(8,128)(2,1)S(1)} all-to-all(bf16[64,4,8,128]{3,2,1,0:T(8,128)(2,1)S(1)} %bitcast.18), channel_id=1, replica_groups={{0,8,16,24,32,40,48,56,64,72,80,88,96,104,112,120,128,136,144,152,160,1..., dimensions={0} | all-to-all | bytes 1048576 | tf_op jit(solution)/shard_map/all_to_all | solution.py:265
  156.4 26.2 %all_to_all.40 = bf16[128,8,128]{2,1,0:T(8,128)(2,1)S(1)} all-to-all(bf16[128,8,128]{2,1,0:T(8,128)(2,1)S(1)} %pick.3), channel_id=1, replica_groups=mesh['seq'=128,'tp'=4] {'seq'}, dimensions={0} | all-to-all | bytes 524288 | tf_op jit(solution)/shard_map/all_to_all | solution.py:305
  (22 shorter events, 3.3 us)
Async XLA Ops:
  1.9 20.5 %collective-permute-start = (bf16[256,1024]{1,0:T(8,128)(2,1)S(1)}, bf16[256,1024]{1,0:T(8,128)(2,1)}, u32[]{:S(2)}, u32[]{:S(2)}) collective-permute-start(bf16[256,1024]{1,0:T(8,128)(2,1)S(1)} %constant_dynamic-update-slice_fusion.kv0), channel_id=1, source_target_pairs={{0,8},{4,12},{8,16},{12,20},{16,24},{20,28},{24,32},{28,36},{32,40... | collective-permute-start | bytes 1572872 | tf_op jit(solution)/shard_map/ppermute | solution.py:193
  9.9 15.9 %copy-start.3 = (s32[128,1]{0,1:T(1,128)S(1)}, s32[128,1]{0,1:T(1,128)}, u32[]{:S(2)}) copy-start(s32[128,1]{0,1:T(1,128)} %param.14) | copy-start | bytes 1540
  9.9 16.6 %copy-start.1 = (bf16[128,1024]{1,0:T(8,128)(2,1)S(1)}, bf16[128,1024]{1,0:T(8,128)(2,1)}, u32[]{:S(2)}) copy-start(bf16[128,1024]{1,0:T(8,128)(2,1)} %q.3) | copy-start | bytes 786436
  9.9 16.6 %copy-start.2 = (bf16[128,1024]{1,0:T(8,128)(2,1)S(1)}, bf16[128,1024]{1,0:T(8,128)(2,1)}, u32[]{:S(2)}) copy-start(bf16[128,1024]{1,0:T(8,128)(2,1)} %res.1) | copy-start | bytes 786436
  9.9 33.6 %all-to-all-start = ((bf16[4,1024,256]{2,1,0:T(8,128)(2,1)}), bf16[4,1024,256]{2,1,0:T(8,128)(2,1)S(1)}, u32[]{:S(2)}, u32[]{:S(2)}) async-start(bf16[4,1024,256]{2,1,0:T(8,128)(2,1)} %bitcast.24), calls=%async_computation | async-start | bytes 4194304 | tf_op jit(solution)/shard_map/all_to_all | solution.py:205
  14.0 26.0 %collective-permute-start.3 = (bf16[256,1024]{1,0:T(8,128)(2,1)S(1)}, bf16[256,1024]{1,0:T(8,128)(2,1)}, u32[]{:S(2)}, u32[]{:S(2)}) collective-permute-start(bf16[256,1024]{1,0:T(8,128)(2,1)S(1)} %constant_dynamic-update-slice_fusion.kv0), channel_id=1, source_target_pairs={{0,4},{8,12},{16,20},{24,28},{32,36},{40,44},{48,52},{56,60},{64,6... | collective-permute-start | bytes 1572872 | tf_op jit(solution)/shard_map/ppermute | solution.py:193
  15.3 28.1 %collective-permute-start.5 = (bf16[512,1024]{1,0:T(8,128)(2,1)}, bf16[512,1024]{1,0:T(8,128)(2,1)}, u32[]{:S(2)}, u32[]{:S(2)}) collective-permute-start(bf16[512,1024]{1,0:T(8,128)(2,1)} %bitcast.19), channel_id=1, source_target_pairs={{0,4},{8,12},{16,20},{24,28},{32,36},{40,44},{48,52},{56,60},{64,6... | collective-permute-start | bytes 3145736 | tf_op jit(solution)/shard_map/ppermute | solution.py:193
  22.5 4.0 %collective-permute-start.2 = (bf16[256,1024]{1,0:T(8,128)(2,1)}, bf16[256,1024]{1,0:T(8,128)(2,1)S(1)}, u32[]{:S(2)}, u32[]{:S(2)}) collective-permute-start(bf16[256,1024]{1,0:T(8,128)(2,1)} %collective-permute-done.kv1), channel_id=1, source_target_pairs={{0,4},{8,12},{16,20},{24,28},{32,36},{40,44},{48,52},{56,60},{64,6... | collective-permute-start | bytes 1572872 | tf_op jit(solution)/shard_map/ppermute | solution.py:193
  24.4 12.7 %collective-permute-start.1 = (bf16[256,1024]{1,0:T(8,128)(2,1)}, bf16[256,1024]{1,0:T(8,128)(2,1)S(1)}, u32[]{:S(2)}, u32[]{:S(2)}) collective-permute-start(bf16[256,1024]{1,0:T(8,128)(2,1)} %collective-permute-done.kv1), channel_id=1, source_target_pairs={{0,8},{4,12},{8,16},{12,20},{16,24},{20,28},{24,32},{28,36},{32,40... | collective-permute-start | bytes 1572872 | tf_op jit(solution)/shard_map/ppermute | solution.py:193
  37.1 4.4 %collective-permute-start.4 = (bf16[256,1024]{1,0:T(8,128)(2,1)S(1)}, bf16[256,1024]{1,0:T(8,128)(2,1)S(1)}, u32[]{:S(2)}, u32[]{:S(2)}) collective-permute-start(bf16[256,1024]{1,0:T(8,128)(2,1)S(1)} %collective-permute-done.1.kv2), channel_id=1, source_target_pairs={{4,0},{12,8},{20,16},{28,24},{36,32},{44,40},{52,48},{60,56},{68,6... | collective-permute-start | bytes 1572872 | tf_op jit(solution)/shard_map/ppermute | solution.py:193
  77.6 25.2 %collective-permute-start.6 = (bf16[4,1024,256]{2,1,0:T(8,128)(2,1)S(1)}, bf16[4,1024,256]{2,1,0:T(8,128)(2,1)S(1)}, u32[]{:S(2)}, u32[]{:S(2)}) collective-permute-start(bf16[4,1024,256]{2,1,0:T(8,128)(2,1)S(1)} %all-to-all-done.first0), channel_id=1, source_target_pairs={{0,4},{8,12},{16,20},{24,28},{32,36},{40,44},{48,52},{56,60},{64,6... | collective-permute-start | bytes 6291464 | tf_op jit(solution)/shard_map/ppermute | solution.py:193
  104.2 27.4 %copy-start = (bf16[1,512,1024]{2,1,0:T(8,128)(2,1)S(1)}, bf16[1,512,1024]{2,1,0:T(8,128)(2,1)}, u32[]{:S(2)}) copy-start(bf16[1,512,1024]{2,1,0:T(8,128)(2,1)} %param.17) | copy-start | bytes 3145732

commit v8 on v7

--- a/solution.py
+++ b/solution.py
@@ -40,18 +40,18 @@
     return lax.dot_general(a, b, (((1,), (1,)), ((), ())), preferred_element_type=f32)
 
 
-def attend_near_kernel(place, q, kv0, kv1, kvx1, _, held, stats):
+def attend_near_kernel(place, q, kv0, kv1, _, held, stats):
     row = lax.broadcasted_iota(jnp.int32, (BLOCK, BLOCK), 0)
     col = lax.broadcasted_iota(jnp.int32, (BLOCK, BLOCK), 1)
     diff = col - row
     shift1 = jnp.where(place[0] >= 1, 0, jnp.int32(4 * BLOCK))
     past = diff + BLOCK > shift1
-    visible = jnp.concatenate([past, past, diff <= 0], axis=1)
-    ones = jnp.ones((3 * BLOCK, HEAD_DIM), bf16)
+    visible = jnp.concatenate([past, diff <= 0], axis=1)
+    ones = jnp.ones((2 * BLOCK, HEAD_DIM), bf16)
     for h in range(q.shape[1] // HEAD_DIM):
         s = slice(h * HEAD_DIM, (h + 1) * HEAD_DIM)
-        keys = jnp.concatenate([kv[:BLOCK, s] for kv in (kv1, kvx1, kv0)], axis=0)
-        values = jnp.concatenate([kv[BLOCK:, s] for kv in (kv1, kvx1, kv0)], axis=0)
+        keys = jnp.concatenate([kv[:BLOCK, s] for kv in (kv1, kv0)], axis=0)
+        values = jnp.concatenate([kv[BLOCK:, s] for kv in (kv1, kv0)], axis=0)
         scores = dot_t(q[:, s], keys) * (1.0 / math.sqrt(HEAD_DIM))
         scores = jnp.where(visible, scores, masked_score)
         top = jnp.max(scores, axis=1, keepdims=True)
@@ -62,7 +62,7 @@
         stats[1, :, s] = both[:, HEAD_DIM:]
 
 
-def attend_far_kernel(place, q, kv2, kvx0, kvx2, held, stats, res, out, home):
+def attend_far_kernel(place, q, kv2, kvx0, kvx1, kvx2, held, stats, res, out, home):
     chip = place[0]
     core = place[1]
     row = lax.broadcasted_iota(jnp.int32, (BLOCK, BLOCK), 0)
@@ -73,20 +73,22 @@
     shiftx = jnp.where((chip >= 2) | (core == 1), 0, big)
     seen2 = diff > shift2
     seenx = diff + BLOCK > shiftx
-    ones = jnp.ones((2 * BLOCK, HEAD_DIM), bf16)
+    seen1 = diff + BLOCK > jnp.where(chip >= 1, 0, big)
+    ones = jnp.ones((3 * BLOCK, HEAD_DIM), bf16)
     z_count, core_count = out.shape[0], out.shape[2]
     for h in range(q.shape[1] // HEAD_DIM):
         s = slice(h * HEAD_DIM, (h + 1) * HEAD_DIM)
         kvx = kvx0[:, s] + kvx2[:, s]
-        keys = jnp.concatenate([kv2[:BLOCK, s], kvx[:BLOCK]], axis=0)
-        values = jnp.concatenate([kv2[BLOCK:, s], kvx[BLOCK:]], axis=0)
+        keys = jnp.concatenate([kv2[:BLOCK, s], kvx[:BLOCK], kvx1[:BLOCK, s]], axis=0)
+        values = jnp.concatenate([kv2[BLOCK:, s], kvx[BLOCK:], kvx1[BLOCK:, s]], axis=0)
         scores = dot_t(q[:, s], keys) * (1.0 / math.sqrt(HEAD_DIM))
         score2 = jnp.where(seen2, scores[:, :BLOCK], masked_score)
-        scorex = jnp.where(seenx, scores[:, BLOCK:], masked_score)
+        scorex = jnp.where(seenx, scores[:, BLOCK : 2 * BLOCK], masked_score)
+        score1 = jnp.where(seen1, scores[:, 2 * BLOCK :], masked_score)
         near_top = stats[0, :, s]
-        top = jnp.max(jnp.maximum(score2, scorex), axis=1, keepdims=True)
-        top = jnp.maximum(near_top, top)
-        expo = jnp.concatenate([jnp.exp(score2 - top), jnp.exp(scorex - top)], axis=1)
+        top = jnp.maximum(jnp.maximum(score2, scorex), score1)
+        top = jnp.maximum(near_top, jnp.max(top, axis=1, keepdims=True))
+        expo = jnp.concatenate([jnp.exp(part - top) for part in (score2, scorex, score1)], axis=1)
         both = dot(expo.astype(bf16), jnp.concatenate([values, ones], axis=1))
         scale = jnp.exp(near_top - top)
         total = stats[1, :, s] * scale + both[:, HEAD_DIM:]
@@ -226,11 +228,11 @@
             jax.ShapeDtypeStruct((rows, width), f32),
             jax.ShapeDtypeStruct((2, rows, width), f32),
         ),
-        in_specs=[smem()] + [vmem()] * 5,
+        in_specs=[smem()] + [vmem()] * 4,
         out_specs=(vmem(), vmem()),
         compiler_params=params(),
         name="attend_near",
-    )(place, queries, kv0, kv1, kvx1, residual_in)
+    )(place, queries, kv0, kv1, residual_in)
     kv2, held, stats = lax.optimization_barrier((kv2, held, stats))
     kvx2 = move(kv2, to_even)
     stream, home = pl.pallas_call(
@@ -239,11 +241,11 @@
             jax.ShapeDtypeStruct((z_count, heads, 2, TILE, HEAD_DIM), bf16),
             jax.ShapeDtypeStruct((rows, width), bf16),
         ),
-        in_specs=[smem()] + [vmem()] * 7,
+        in_specs=[smem()] + [vmem()] * 8,
         out_specs=(vmem(), vmem()),
         compiler_params=params(),
         name="attend_far",
-    )(place, queries, kv2, kvx0, kvx2, held, stats, residual_in)
+    )(place, queries, kv2, kvx0, kvx1, kvx2, held, stats, residual_in)
     stream, first0, down1 = lax.optimization_barrier((stream, first0, down1))
 
     tiles = lax.all_to_all(

time: 184 us -> 181 us (0.984)
  transfers between devices with their start and end apart: 8 -> 8, of which waited for: 3 -> 2; matrix products, arithmetic and copies ran while one was open for 2% -> 2% of each run, Pallas kernels for 3% -> 3%
where the time goes in v8:
time: 181 us; the launch traced here: 180 us
  blocking collectives  130 us (72%)
  starting transfers between devices  24.7 us (14%)
  Pallas kernels  10.2 us (6%)
  waiting for transfers between devices  9.26 us (5%)
  other arithmetic  3.48 us (2%)
  local copies, waits for them, and re-layouts  2.65 us (1%)
    all_to_all x2, blocking collectives, same_core_exchange(): lax.all_to_all(x, 'seq', 0, 0, tiled=True, axis_index_groups=same_core)  44 us
    all_to_all x1, blocking collectives, local(): lax.all_to_all(stream.reshape(seq_count, TILE, HEAD_DIM), 'seq', 0, 0, ti...  32.6 us
    all_to_all x1, blocking collectives, local(): finished = lax.all_to_all(pick(slot_of, returned), 'seq', 0, 0, tiled=True)  26.2 us
    ppermute x7, starting transfers between devices, move(): return lax.ppermute(x, 'seq', route)  20.6 us
    all_to_all x1, blocking collectives, local(): parts = lax.all_to_all(parts, 'tp', 0, 0, tiled=True)  17.7 us
    all_to_all x1, blocking collectives, local(): hidden = lax.all_to_all(hidden, 'tp', 0, 0, tiled=True)  9.33 us
    ppermute x7, waiting for transfers between devices, move(): return lax.ppermute(x, 'seq', route)  9.26 us
    all_to_all x1, starting transfers between devices, local(): first0 = lax.all_to_all(both, 'tp', 0, 0, tiled=True)  4.14 us
  transfers between devices with their start and end apart: 8, of which 2 were waited for; matrix products, arithmetic and copies ran while one was open for 2% of the time, Pallas kernels for 3%

profile of v8, /device:TPU:1, one launch (start us, length us, event | category | flops | bytes accessed | tf_op | source)
XLA Modules:
  0.0 180.3 jit_solution(9695231859723380983)
XLA Ops:
  0.0 1.0 constant_dynamic-update-slice_fusion.1
  1.0 1.0 constant_dynamic-update-slice_fusion.kv0
  1.9 4.8 %collective-permute-start = (bf16[256,1024]{1,0:T(8,128)(2,1)S(1)}, bf16[256,1024]{1,0:T(8,128)(2,1)}, u32[]{:S(2)}, u32[]{:S(2)}) collective-permute-start(bf16[256,1024]{1,0:T(8,128)(2,1)S(1)} %constant_dynamic-update-slice_fusion.kv0), channel_id=1, source_target_pairs={{0,8},{4,12},{8,16},{12,20},{16,24},{20,28},{24,32},{28,36},{32,40... | collective-permute-start | bytes 1572872 | tf_op jit(solution)/shard_map/ppermute | solution.py:195
  6.8 3.1 %pad_maximum_fusion = bf16[4096,256]{1,0:T(8,128)(2,1)} fusion(bf16[4096,128]{1,0:T(8,128)(2,1)} %bitcast.25, bf16[4096,128]{1,0:T(8,128)(2,1)} %bitcast.26), kind=kLoop, calls=%fused_computation | loop fusion | flops 4194304 | bytes 4194304 | tf_op jit(solution)/shard_map/concatenate | solution.py:206
  9.9 4.1 %all-to-all-start = ((bf16[4,1024,256]{2,1,0:T(8,128)(2,1)}), bf16[4,1024,256]{2,1,0:T(8,128)(2,1)S(1)}, u32[]{:S(2)}, u32[]{:S(2)}) async-start(bf16[4,1024,256]{2,1,0:T(8,128)(2,1)} %bitcast.24), calls=%async_computation | async-start | bytes 4194304 | tf_op jit(solution)/shard_map/all_to_all | solution.py:207
  14.0 1.3 collective-permute-start.2
  15.3 6.4 %collective-permute-start.5 = (bf16[512,1024]{1,0:T(8,128)(2,1)}, bf16[512,1024]{1,0:T(8,128)(2,1)}, u32[]{:S(2)}, u32[]{:S(2)}) collective-permute-start(bf16[512,1024]{1,0:T(8,128)(2,1)} %bitcast.19), channel_id=1, source_target_pairs={{0,4},{8,12},{16,20},{24,28},{32,36},{40,44},{48,52},{56,60},{64,6... | collective-permute-start | bytes 3145736 | tf_op jit(solution)/shard_map/ppermute | solution.py:195
  22.5 1.3 collective-permute-start.1
  24.2 1.9 %collective-permute-start.3 = (bf16[256,1024]{1,0:T(8,128)(2,1)}, bf16[256,1024]{1,0:T(8,128)(2,1)S(1)}, u32[]{:S(2)}, u32[]{:S(2)}) collective-permute-start(bf16[256,1024]{1,0:T(8,128)(2,1)} %collective-permute-done.kv1), channel_id=1, source_target_pairs={{0,4},{8,12},{16,20},{24,28},{32,36},{40,44},{48,52},{56,60},{64,6... | collective-permute-start | bytes 1572872 | tf_op jit(solution)/shard_map/ppermute | solution.py:195
  26.1 1.7 attend_near.1
  27.8 7.8 %collective-permute-done.1.kv2 = bf16[256,1024]{1,0:T(8,128)(2,1)S(1)} collective-permute-done((bf16[256,1024]{1,0:T(8,128)(2,1)}, bf16[256,1024]{1,0:T(8,128)(2,1)S(1)}, u32[]{:S(2)}, u32[]{:S(2)}) %collective-permute-start.1) | collective-permute-done | bytes 524320 | tf_op jit(solution)/shard_map/ppermute | solution.py:195
  35.6 2.5 %collective-permute-start.4 = (bf16[256,1024]{1,0:T(8,128)(2,1)S(1)}, bf16[256,1024]{1,0:T(8,128)(2,1)S(1)}, u32[]{:S(2)}, u32[]{:S(2)}) collective-permute-start(bf16[256,1024]{1,0:T(8,128)(2,1)S(1)} %collective-permute-done.1.kv2), channel_id=1, source_target_pairs={{4,0},{12,8},{20,16},{28,24},{36,32},{44,40},{52,48},{60,56},{68,6... | collective-permute-start | bytes 1572872 | tf_op jit(solution)/shard_map/ppermute | solution.py:195
  38.2 1.5 collective-permute-done.4.kvx2
  39.6 2.3 %attend_far.1 = (bf16[8,8,2,8,128]{4,3,2,1,0:T(8,128)(2,1)S(1)}, bf16[128,1024]{1,0:T(8,128)(2,1)S(1)}) custom-call(s32[2]{0:T(128)S(1)} %pad_add_fusion.place, bf16[128,1024]{1,0:T(8,128)(2,1)S(1)} %copy-done.1, bf16[256,1024]{1,0:T(8,128)(2,1)S(1)} %collective-permute-done.1.kv2, bf16[256,1024]{1,0:T(8,128)(2,1)} %collective-permute-done.2.kvx0, ...), custom_call_target="tpu_custom_call" | custom-call | tf_op jit(solution)/shard_map/attend_far/pallas_call | solution.py:238
  41.9 32.6 %all_to_all.35.tiles = bf16[128,8,128]{2,1,0:T(8,128)(2,1)S(1)} all-to-all(bf16[128,8,128]{2,1,0:T(8,128)(2,1)S(1)} %bitcast.22), channel_id=1, replica_groups=mesh['seq'=128,'tp'=4] {'seq'}, dimensions={0} | all-to-all | bytes 524288 | tf_op jit(solution)/shard_map/all_to_all | solution.py:251
  74.5 2.3 %collective-permute-start.6 = (bf16[4,1024,256]{2,1,0:T(8,128)(2,1)S(1)}, bf16[4,1024,256]{2,1,0:T(8,128)(2,1)S(1)}, u32[]{:S(2)}, u32[]{:S(2)}) collective-permute-start(bf16[4,1024,256]{2,1,0:T(8,128)(2,1)S(1)} %all-to-all-done.first0), channel_id=1, source_target_pairs={{0,4},{8,12},{16,20},{24,28},{32,36},{40,44},{48,52},{56,60},{64,6... | collective-permute-start | bytes 6291464 | tf_op jit(solution)/shard_map/ppermute | solution.py:195
  76.8 1.0 pick.2
  77.7 21.9 %all_to_all.36 = bf16[64,4,8,128]{3,2,1,0:T(8,128)(2,1)S(1)} all-to-all(bf16[64,4,8,128]{3,2,1,0:T(8,128)(2,1)S(1)} %bitcast.16), channel_id=1, replica_groups={{0,8,16,24,32,40,48,56,64,72,80,88,96,104,112,120,128,136,144,152,160,1..., dimensions={0} | all-to-all | bytes 1048576 | tf_op jit(solution)/shard_map/all_to_all | solution.py:267
  99.7 1.4 project.1
  101.1 17.7 %all_to_all.37.parts_ref = bf16[4,272,512]{2,1,0:T(8,128)(2,1)S(1)} all-to-all(bf16[4,272,512]{2,1,0:T(8,128)(2,1)S(1)} %project.1), channel_id=1, replica_groups=mesh['seq'=128,'tp'=4] {'tp'}, dimensions={0} | all-to-all | bytes 2228224 | tf_op jit(solution)/shard_map/all_to_all | solution.py:284
  119.2 9.3 %all_to_all.38.hidden = bf16[4,256,256]{2,1,0:T(8,128)(2,1)S(1)} all-to-all(bf16[4,256,256]{2,1,0:T(8,128)(2,1)S(1)} %hidden.1), channel_id=1, replica_groups=mesh['seq'=128,'tp'=4] {'tp'}, dimensions={0} | all-to-all | bytes 1048576 | tf_op jit(solution)/shard_map/all_to_all | solution.py:297
  128.5 1.9 %branch.1 = bf16[8,8,4,8,128]{4,3,2,1,0:T(8,128)(2,1)S(1)} custom-call(bf16[4,256,256]{2,1,0:T(8,128)(2,1)S(1)} %all_to_all.38.hidden, bf16[512,1024]{1,0:T(8,128)(2,1)S(1)} %bitcast.20, bf16[512,1024]{1,0:T(8,128)(2,1)} %collective-permute-done.5.down1), custom_call_target="tpu_custom_call" | custom-call | tf_op jit(solution)/shard_map/branch/pallas_call | solution.py:298
  130.4 22.1 %all_to_all.39 = bf16[64,4,8,128]{3,2,1,0:T(8,128)(2,1)S(1)} all-to-all(bf16[64,4,8,128]{3,2,1,0:T(8,128)(2,1)S(1)} %bitcast.18), channel_id=1, replica_groups={{0,8,16,24,32,40,48,56,64,72,80,88,96,104,112,120,128,136,144,152,160,1..., dimensions={0} | all-to-all | bytes 1048576 | tf_op jit(solution)/shard_map/all_to_all | solution.py:267
  153.3 26.2 %all_to_all.40 = bf16[128,8,128]{2,1,0:T(8,128)(2,1)S(1)} all-to-all(bf16[128,8,128]{2,1,0:T(8,128)(2,1)S(1)} %pick.3), channel_id=1, replica_groups=mesh['seq'=128,'tp'=4] {'seq'}, dimensions={0} | all-to-all | bytes 524288 | tf_op jit(solution)/shard_map/all_to_all | solution.py:307
  (22 shorter events, 3.0 us)
Async XLA Ops:
  1.9 20.5 %collective-permute-start = (bf16[256,1024]{1,0:T(8,128)(2,1)S(1)}, bf16[256,1024]{1,0:T(8,128)(2,1)}, u32[]{:S(2)}, u32[]{:S(2)}) collective-permute-start(bf16[256,1024]{1,0:T(8,128)(2,1)S(1)} %constant_dynamic-update-slice_fusion.kv0), channel_id=1, source_target_pairs={{0,8},{4,12},{8,16},{12,20},{16,24},{20,28},{24,32},{28,36},{32,40... | collective-permute-start | bytes 1572872 | tf_op jit(solution)/shard_map/ppermute | solution.py:195
  9.9 14.0 %copy-start.3 = (s32[128,1]{0,1:T(1,128)S(1)}, s32[128,1]{0,1:T(1,128)}, u32[]{:S(2)}) copy-start(s32[128,1]{0,1:T(1,128)} %param.14) | copy-start | bytes 1540
  9.9 16.2 %copy-start.1 = (bf16[128,1024]{1,0:T(8,128)(2,1)S(1)}, bf16[128,1024]{1,0:T(8,128)(2,1)}, u32[]{:S(2)}) copy-start(bf16[128,1024]{1,0:T(8,128)(2,1)} %q.3) | copy-start | bytes 786436
  9.9 16.2 %copy-start.2 = (bf16[128,1024]{1,0:T(8,128)(2,1)S(1)}, bf16[128,1024]{1,0:T(8,128)(2,1)}, u32[]{:S(2)}) copy-start(bf16[128,1024]{1,0:T(8,128)(2,1)} %res.1) | copy-start | bytes 786436
  9.9 32.0 %all-to-all-start = ((bf16[4,1024,256]{2,1,0:T(8,128)(2,1)}), bf16[4,1024,256]{2,1,0:T(8,128)(2,1)S(1)}, u32[]{:S(2)}, u32[]{:S(2)}) async-start(bf16[4,1024,256]{2,1,0:T(8,128)(2,1)} %bitcast.24), calls=%async_computation | async-start | bytes 4194304 | tf_op jit(solution)/shard_map/all_to_all | solution.py:207
  14.0 24.1 %collective-permute-start.2 = (bf16[256,1024]{1,0:T(8,128)(2,1)S(1)}, bf16[256,1024]{1,0:T(8,128)(2,1)}, u32[]{:S(2)}, u32[]{:S(2)}) collective-permute-start(bf16[256,1024]{1,0:T(8,128)(2,1)S(1)} %constant_dynamic-update-slice_fusion.kv0), channel_id=1, source_target_pairs={{0,4},{8,12},{16,20},{24,28},{32,36},{40,44},{48,52},{56,60},{64,6... | collective-permute-start | bytes 1572872 | tf_op jit(solution)/shard_map/ppermute | solution.py:195
  15.3 26.6 %collective-permute-start.5 = (bf16[512,1024]{1,0:T(8,128)(2,1)}, bf16[512,1024]{1,0:T(8,128)(2,1)}, u32[]{:S(2)}, u32[]{:S(2)}) collective-permute-start(bf16[512,1024]{1,0:T(8,128)(2,1)} %bitcast.19), channel_id=1, source_target_pairs={{0,4},{8,12},{16,20},{24,28},{32,36},{40,44},{48,52},{56,60},{64,6... | collective-permute-start | bytes 3145736 | tf_op jit(solution)/shard_map/ppermute | solution.py:195
  22.5 13.1 %collective-permute-start.1 = (bf16[256,1024]{1,0:T(8,128)(2,1)}, bf16[256,1024]{1,0:T(8,128)(2,1)S(1)}, u32[]{:S(2)}, u32[]{:S(2)}) collective-permute-start(bf16[256,1024]{1,0:T(8,128)(2,1)} %collective-permute-done.kv1), channel_id=1, source_target_pairs={{0,8},{4,12},{8,16},{12,20},{16,24},{20,28},{24,32},{28,36},{32,40... | collective-permute-start | bytes 1572872 | tf_op jit(solution)/shard_map/ppermute | solution.py:195
  24.2 14.0 %collective-permute-start.3 = (bf16[256,1024]{1,0:T(8,128)(2,1)}, bf16[256,1024]{1,0:T(8,128)(2,1)S(1)}, u32[]{:S(2)}, u32[]{:S(2)}) collective-permute-start(bf16[256,1024]{1,0:T(8,128)(2,1)} %collective-permute-done.kv1), channel_id=1, source_target_pairs={{0,4},{8,12},{16,20},{24,28},{32,36},{40,44},{48,52},{56,60},{64,6... | collective-permute-start | bytes 1572872 | tf_op jit(solution)/shard_map/ppermute | solution.py:195
  35.6 4.0 %collective-permute-start.4 = (bf16[256,1024]{1,0:T(8,128)(2,1)S(1)}, bf16[256,1024]{1,0:T(8,128)(2,1)S(1)}, u32[]{:S(2)}, u32[]{:S(2)}) collective-permute-start(bf16[256,1024]{1,0:T(8,128)(2,1)S(1)} %collective-permute-done.1.kv2), channel_id=1, source_target_pairs={{4,0},{12,8},{20,16},{28,24},{36,32},{44,40},{52,48},{60,56},{68,6... | collective-permute-start | bytes 1572872 | tf_op jit(solution)/shard_map/ppermute | solution.py:195
  74.5 25.2 %collective-permute-start.6 = (bf16[4,1024,256]{2,1,0:T(8,128)(2,1)S(1)}, bf16[4,1024,256]{2,1,0:T(8,128)(2,1)S(1)}, u32[]{:S(2)}, u32[]{:S(2)}) collective-permute-start(bf16[4,1024,256]{2,1,0:T(8,128)(2,1)S(1)} %all-to-all-done.first0), channel_id=1, source_target_pairs={{0,4},{8,12},{16,20},{24,28},{32,36},{40,44},{48,52},{56,60},{64,6... | collective-permute-start | bytes 6291464 | tf_op jit(solution)/shard_map/ppermute | solution.py:195
  101.1 27.4 %copy-start = (bf16[1,512,1024]{2,1,0:T(8,128)(2,1)S(1)}, bf16[1,512,1024]{2,1,0:T(8,128)(2,1)}, u32[]{:S(2)}) copy-start(bf16[1,512,1024]{2,1,0:T(8,128)(2,1)} %param.17) | copy-start | bytes 3145732

commit v9 on v8

--- a/solution.py
+++ b/solution.py
@@ -99,7 +99,7 @@
 
 
 def pick_kernel(index, tiles, out):
-    @pl.loop(0, out.shape[0], unroll=8)
+    @pl.loop(0, out.shape[0], unroll=32)
     def _(i):
         out[i] = tiles[index[i]]
 
@@ -151,7 +151,9 @@
             out[t, :, k * half : (k + 1) * half] = value
 
 
-def branch_kernel(hidden, down0, down1, out):
+def branch_kernel(hidden, down0, down1, out, total, held, sem):
+    copy = pltpu.make_async_copy(down1, held, sem)
+    copy.start()
     count = hidden.shape[0]
     half = hidden.shape[2] // 2
     first = jnp.concatenate([hidden[t, :, :half] for t in range(count)], axis=1)
@@ -159,7 +161,10 @@
     z_count, heads, slots = out.shape[:3]
     step = 2 * HEAD_DIM
     for s in range(0, heads * HEAD_DIM, step):
-        value = dot(first, down0[:, s : s + step]) + dot(second, down1[:, s : s + step])
+        total[:, s : s + step] = dot(first, down0[:, s : s + step])
+    copy.wait()
+    for s in range(0, heads * HEAD_DIM, step):
+        value = total[:, s : s + step] + dot(second, held[:, s : s + step])
         for k in range(0, step, HEAD_DIM):
             part = value[:, k : k + HEAD_DIM].reshape(z_count, slots, TILE, HEAD_DIM)
             out[:, (s + k) // HEAD_DIM] = part.astype(bf16)
@@ -298,8 +303,13 @@
     branch = pl.pallas_call(
         branch_kernel,
         out_shape=jax.ShapeDtypeStruct((z_count, heads, slots, TILE, HEAD_DIM), bf16),
-        in_specs=[vmem()] * 3,
+        in_specs=[vmem(), vmem(), pl.BlockSpec(memory_space=pl.ANY)],
         out_specs=vmem(),
+        scratch_shapes=[
+            pltpu.VMEM((work, width), f32),
+            pltpu.VMEM(down1.shape, bf16),
+            pltpu.SemaphoreType.DMA,
+        ],
         compiler_params=params(),
         name="branch",
     )(hidden, down0, down1)

time: 181 us -> 181 us (level)
  no operation moved by 1% of the time
where the time goes in v9:
time: 181 us; the launch traced here: 180 us
  blocking collectives  130 us (72%)
  starting transfers between devices  24.7 us (14%)
  Pallas kernels  9.93 us (5%)
  waiting for transfers between devices  9.26 us (5%)
  other arithmetic  3.48 us (2%)
  local copies, waits for them, and re-layouts  2.65 us (1%)
    all_to_all x2, blocking collectives, same_core_exchange(): lax.all_to_all(x, 'seq', 0, 0, tiled=True, axis_index_groups=same_core)  44 us
    all_to_all x1, blocking collectives, local(): lax.all_to_all(stream.reshape(seq_count, TILE, HEAD_DIM), 'seq', 0, 0, ti...  32.6 us
    all_to_all x1, blocking collectives, local(): finished = lax.all_to_all(pick(slot_of, returned), 'seq', 0, 0, tiled=True)  26.2 us
    ppermute x7, starting transfers between devices, move(): return lax.ppermute(x, 'seq', route)  20.6 us
    all_to_all x1, blocking collectives, local(): parts = lax.all_to_all(parts, 'tp', 0, 0, tiled=True)  17.7 us
    all_to_all x1, blocking collectives, local(): hidden = lax.all_to_all(hidden, 'tp', 0, 0, tiled=True)  9.33 us
    ppermute x7, waiting for transfers between devices, move(): return lax.ppermute(x, 'seq', route)  9.26 us
    all_to_all x1, starting transfers between devices, local(): first0 = lax.all_to_all(both, 'tp', 0, 0, tiled=True)  4.14 us
  transfers between devices with their start and end apart: 8, of which 2 were waited for; matrix products, arithmetic and copies ran while one was open for 2% of the time, Pallas kernels for 3%

profile of v9, /device:TPU:1, one launch (start us, length us, event | category | flops | bytes accessed | tf_op | source)
XLA Modules:
  0.0 180.0 jit_solution(650520799883235539)
XLA Ops:
  0.0 1.0 constant_dynamic-update-slice_fusion.1
  1.0 1.0 constant_dynamic-update-slice_fusion.kv0
  1.9 4.8 %collective-permute-start = (bf16[256,1024]{1,0:T(8,128)(2,1)S(1)}, bf16[256,1024]{1,0:T(8,128)(2,1)}, u32[]{:S(2)}, u32[]{:S(2)}) collective-permute-start(bf16[256,1024]{1,0:T(8,128)(2,1)S(1)} %constant_dynamic-update-slice_fusion.kv0), channel_id=1, source_target_pairs={{0,8},{4,12},{8,16},{12,20},{16,24},{20,28},{24,32},{28,36},{32,40... | collective-permute-start | bytes 1572872 | tf_op jit(solution)/shard_map/ppermute | solution.py:200
  6.8 3.1 %pad_maximum_fusion = bf16[4096,256]{1,0:T(8,128)(2,1)} fusion(bf16[4096,128]{1,0:T(8,128)(2,1)} %bitcast.25, bf16[4096,128]{1,0:T(8,128)(2,1)} %bitcast.26), kind=kLoop, calls=%fused_computation | loop fusion | flops 4194304 | bytes 4194304 | tf_op jit(solution)/shard_map/concatenate | solution.py:211
  9.9 4.1 %all-to-all-start = ((bf16[4,1024,256]{2,1,0:T(8,128)(2,1)}), bf16[4,1024,256]{2,1,0:T(8,128)(2,1)S(1)}, u32[]{:S(2)}, u32[]{:S(2)}) async-start(bf16[4,1024,256]{2,1,0:T(8,128)(2,1)} %bitcast.24), calls=%async_computation | async-start | bytes 4194304 | tf_op jit(solution)/shard_map/all_to_all | solution.py:212
  14.0 1.3 collective-permute-start.2
  15.3 6.4 %collective-permute-start.5 = (bf16[512,1024]{1,0:T(8,128)(2,1)}, bf16[512,1024]{1,0:T(8,128)(2,1)}, u32[]{:S(2)}, u32[]{:S(2)}) collective-permute-start(bf16[512,1024]{1,0:T(8,128)(2,1)} %bitcast.19), channel_id=1, source_target_pairs={{0,4},{8,12},{16,20},{24,28},{32,36},{40,44},{48,52},{56,60},{64,6... | collective-permute-start | bytes 3145736 | tf_op jit(solution)/shard_map/ppermute | solution.py:200
  22.5 1.3 collective-permute-start.1
  24.2 1.9 %collective-permute-start.3 = (bf16[256,1024]{1,0:T(8,128)(2,1)}, bf16[256,1024]{1,0:T(8,128)(2,1)S(1)}, u32[]{:S(2)}, u32[]{:S(2)}) collective-permute-start(bf16[256,1024]{1,0:T(8,128)(2,1)} %collective-permute-done.kv1), channel_id=1, source_target_pairs={{0,4},{8,12},{16,20},{24,28},{32,36},{40,44},{48,52},{56,60},{64,6... | collective-permute-start | bytes 1572872 | tf_op jit(solution)/shard_map/ppermute | solution.py:200
  26.1 1.7 attend_near.1
  27.8 7.8 %collective-permute-done.1.kv2 = bf16[256,1024]{1,0:T(8,128)(2,1)S(1)} collective-permute-done((bf16[256,1024]{1,0:T(8,128)(2,1)}, bf16[256,1024]{1,0:T(8,128)(2,1)S(1)}, u32[]{:S(2)}, u32[]{:S(2)}) %collective-permute-start.1) | collective-permute-done | bytes 524320 | tf_op jit(solution)/shard_map/ppermute | solution.py:200
  35.6 2.5 %collective-permute-start.4 = (bf16[256,1024]{1,0:T(8,128)(2,1)S(1)}, bf16[256,1024]{1,0:T(8,128)(2,1)S(1)}, u32[]{:S(2)}, u32[]{:S(2)}) collective-permute-start(bf16[256,1024]{1,0:T(8,128)(2,1)S(1)} %collective-permute-done.1.kv2), channel_id=1, source_target_pairs={{4,0},{12,8},{20,16},{28,24},{36,32},{44,40},{52,48},{60,56},{68,6... | collective-permute-start | bytes 1572872 | tf_op jit(solution)/shard_map/ppermute | solution.py:200
  38.2 1.5 collective-permute-done.4.kvx2
  39.6 2.3 %attend_far.1 = (bf16[8,8,2,8,128]{4,3,2,1,0:T(8,128)(2,1)S(1)}, bf16[128,1024]{1,0:T(8,128)(2,1)S(1)}) custom-call(s32[2]{0:T(128)S(1)} %pad_add_fusion.place, bf16[128,1024]{1,0:T(8,128)(2,1)S(1)} %copy-done.1, bf16[256,1024]{1,0:T(8,128)(2,1)S(1)} %collective-permute-done.1.kv2, bf16[256,1024]{1,0:T(8,128)(2,1)} %collective-permute-done.2.kvx0, ...), custom_call_target="tpu_custom_call" | custom-call | tf_op jit(solution)/shard_map/attend_far/pallas_call | solution.py:243
  41.9 32.6 %all_to_all.35.tiles = bf16[128,8,128]{2,1,0:T(8,128)(2,1)S(1)} all-to-all(bf16[128,8,128]{2,1,0:T(8,128)(2,1)S(1)} %bitcast.22), channel_id=1, replica_groups=mesh['seq'=128,'tp'=4] {'seq'}, dimensions={0} | all-to-all | bytes 524288 | tf_op jit(solution)/shard_map/all_to_all | solution.py:256
  74.5 2.3 %collective-permute-start.6 = (bf16[4,1024,256]{2,1,0:T(8,128)(2,1)S(1)}, bf16[4,1024,256]{2,1,0:T(8,128)(2,1)S(1)}, u32[]{:S(2)}, u32[]{:S(2)}) collective-permute-start(bf16[4,1024,256]{2,1,0:T(8,128)(2,1)S(1)} %all-to-all-done.first0), channel_id=1, source_target_pairs={{0,4},{8,12},{16,20},{24,28},{32,36},{40,44},{48,52},{56,60},{64,6... | collective-permute-start | bytes 6291464 | tf_op jit(solution)/shard_map/ppermute | solution.py:200
  76.8 0.8 pick.2
  77.6 21.9 %all_to_all.36 = bf16[64,4,8,128]{3,2,1,0:T(8,128)(2,1)S(1)} all-to-all(bf16[64,4,8,128]{3,2,1,0:T(8,128)(2,1)S(1)} %bitcast.16), channel_id=1, replica_groups={{0,8,16,24,32,40,48,56,64,72,80,88,96,104,112,120,128,136,144,152,160,1..., dimensions={0} | all-to-all | bytes 1048576 | tf_op jit(solution)/shard_map/all_to_all | solution.py:272
  99.5 1.4 project.1
  101.0 17.7 %all_to_all.37.parts_ref = bf16[4,272,512]{2,1,0:T(8,128)(2,1)S(1)} all-to-all(bf16[4,272,512]{2,1,0:T(8,128)(2,1)S(1)} %project.1), channel_id=1, replica_groups=mesh['seq'=128,'tp'=4] {'tp'}, dimensions={0} | all-to-all | bytes 2228224 | tf_op jit(solution)/shard_map/all_to_all | solution.py:289
  119.0 9.3 %all_to_all.38.hidden = bf16[4,256,256]{2,1,0:T(8,128)(2,1)S(1)} all-to-all(bf16[4,256,256]{2,1,0:T(8,128)(2,1)S(1)} %hidden.1), channel_id=1, replica_groups=mesh['seq'=128,'tp'=4] {'tp'}, dimensions={0} | all-to-all | bytes 1048576 | tf_op jit(solution)/shard_map/all_to_all | solution.py:302
  128.4 1.9 %branch.1 = bf16[8,8,4,8,128]{4,3,2,1,0:T(8,128)(2,1)S(1)} custom-call(bf16[4,256,256]{2,1,0:T(8,128)(2,1)S(1)} %all_to_all.38.hidden, bf16[512,1024]{1,0:T(8,128)(2,1)S(1)} %bitcast.20, bf16[512,1024]{1,0:T(8,128)(2,1)} %collective-permute-done.5.down1), custom_call_target="tpu_custom_call" | custom-call | tf_op jit(solution)/shard_map/branch/pallas_call | solution.py:303
  130.3 22.1 %all_to_all.39 = bf16[64,4,8,128]{3,2,1,0:T(8,128)(2,1)S(1)} all-to-all(bf16[64,4,8,128]{3,2,1,0:T(8,128)(2,1)S(1)} %bitcast.18), channel_id=1, replica_groups={{0,8,16,24,32,40,48,56,64,72,80,88,96,104,112,120,128,136,144,152,160,1..., dimensions={0} | all-to-all | bytes 1048576 | tf_op jit(solution)/shard_map/all_to_all | solution.py:272
  153.1 26.2 %all_to_all.40 = bf16[128,8,128]{2,1,0:T(8,128)(2,1)S(1)} all-to-all(bf16[128,8,128]{2,1,0:T(8,128)(2,1)S(1)} %pick.3), channel_id=1, replica_groups=mesh['seq'=128,'tp'=4] {'seq'}, dimensions={0} | all-to-all | bytes 524288 | tf_op jit(solution)/shard_map/all_to_all | solution.py:317
  (22 shorter events, 2.9 us)
Async XLA Ops:
  1.9 20.5 %collective-permute-start = (bf16[256,1024]{1,0:T(8,128)(2,1)S(1)}, bf16[256,1024]{1,0:T(8,128)(2,1)}, u32[]{:S(2)}, u32[]{:S(2)}) collective-permute-start(bf16[256,1024]{1,0:T(8,128)(2,1)S(1)} %constant_dynamic-update-slice_fusion.kv0), channel_id=1, source_target_pairs={{0,8},{4,12},{8,16},{12,20},{16,24},{20,28},{24,32},{28,36},{32,40... | collective-permute-start | bytes 1572872 | tf_op jit(solution)/shard_map/ppermute | solution.py:200
  9.9 14.0 %copy-start.3 = (s32[128,1]{0,1:T(1,128)S(1)}, s32[128,1]{0,1:T(1,128)}, u32[]{:S(2)}) copy-start(s32[128,1]{0,1:T(1,128)} %param.14) | copy-start | bytes 1540
  9.9 16.2 %copy-start.1 = (bf16[128,1024]{1,0:T(8,128)(2,1)S(1)}, bf16[128,1024]{1,0:T(8,128)(2,1)}, u32[]{:S(2)}) copy-start(bf16[128,1024]{1,0:T(8,128)(2,1)} %q.3) | copy-start | bytes 786436
  9.9 16.2 %copy-start.2 = (bf16[128,1024]{1,0:T(8,128)(2,1)S(1)}, bf16[128,1024]{1,0:T(8,128)(2,1)}, u32[]{:S(2)}) copy-start(bf16[128,1024]{1,0:T(8,128)(2,1)} %res.1) | copy-start | bytes 786436
  9.9 32.0 %all-to-all-start = ((bf16[4,1024,256]{2,1,0:T(8,128)(2,1)}), bf16[4,1024,256]{2,1,0:T(8,128)(2,1)S(1)}, u32[]{:S(2)}, u32[]{:S(2)}) async-start(bf16[4,1024,256]{2,1,0:T(8,128)(2,1)} %bitcast.24), calls=%async_computation | async-start | bytes 4194304 | tf_op jit(solution)/shard_map/all_to_all | solution.py:212
  14.0 24.1 %collective-permute-start.2 = (bf16[256,1024]{1,0:T(8,128)(2,1)S(1)}, bf16[256,1024]{1,0:T(8,128)(2,1)}, u32[]{:S(2)}, u32[]{:S(2)}) collective-permute-start(bf16[256,1024]{1,0:T(8,128)(2,1)S(1)} %constant_dynamic-update-slice_fusion.kv0), channel_id=1, source_target_pairs={{0,4},{8,12},{16,20},{24,28},{32,36},{40,44},{48,52},{56,60},{64,6... | collective-permute-start | bytes 1572872 | tf_op jit(solution)/shard_map/ppermute | solution.py:200
  15.3 26.6 %collective-permute-start.5 = (bf16[512,1024]{1,0:T(8,128)(2,1)}, bf16[512,1024]{1,0:T(8,128)(2,1)}, u32[]{:S(2)}, u32[]{:S(2)}) collective-permute-start(bf16[512,1024]{1,0:T(8,128)(2,1)} %bitcast.19), channel_id=1, source_target_pairs={{0,4},{8,12},{16,20},{24,28},{32,36},{40,44},{48,52},{56,60},{64,6... | collective-permute-start | bytes 3145736 | tf_op jit(solution)/shard_map/ppermute | solution.py:200
  22.5 13.1 %collective-permute-start.1 = (bf16[256,1024]{1,0:T(8,128)(2,1)}, bf16[256,1024]{1,0:T(8,128)(2,1)S(1)}, u32[]{:S(2)}, u32[]{:S(2)}) collective-permute-start(bf16[256,1024]{1,0:T(8,128)(2,1)} %collective-permute-done.kv1), channel_id=1, source_target_pairs={{0,8},{4,12},{8,16},{12,20},{16,24},{20,28},{24,32},{28,36},{32,40... | collective-permute-start | bytes 1572872 | tf_op jit(solution)/shard_map/ppermute | solution.py:200
  24.2 14.0 %collective-permute-start.3 = (bf16[256,1024]{1,0:T(8,128)(2,1)}, bf16[256,1024]{1,0:T(8,128)(2,1)S(1)}, u32[]{:S(2)}, u32[]{:S(2)}) collective-permute-start(bf16[256,1024]{1,0:T(8,128)(2,1)} %collective-permute-done.kv1), channel_id=1, source_target_pairs={{0,4},{8,12},{16,20},{24,28},{32,36},{40,44},{48,52},{56,60},{64,6... | collective-permute-start | bytes 1572872 | tf_op jit(solution)/shard_map/ppermute | solution.py:200
  35.6 4.0 %collective-permute-start.4 = (bf16[256,1024]{1,0:T(8,128)(2,1)S(1)}, bf16[256,1024]{1,0:T(8,128)(2,1)S(1)}, u32[]{:S(2)}, u32[]{:S(2)}) collective-permute-start(bf16[256,1024]{1,0:T(8,128)(2,1)S(1)} %collective-permute-done.1.kv2), channel_id=1, source_target_pairs={{4,0},{12,8},{20,16},{28,24},{36,32},{44,40},{52,48},{60,56},{68,6... | collective-permute-start | bytes 1572872 | tf_op jit(solution)/shard_map/ppermute | solution.py:200
  74.5 25.1 %collective-permute-start.6 = (bf16[4,1024,256]{2,1,0:T(8,128)(2,1)S(1)}, bf16[4,1024,256]{2,1,0:T(8,128)(2,1)S(1)}, u32[]{:S(2)}, u32[]{:S(2)}) collective-permute-start(bf16[4,1024,256]{2,1,0:T(8,128)(2,1)S(1)} %all-to-all-done.first0), channel_id=1, source_target_pairs={{0,4},{8,12},{16,20},{24,28},{32,36},{40,44},{48,52},{56,60},{64,6... | collective-permute-start | bytes 6291464 | tf_op jit(solution)/shard_map/ppermute | solution.py:200
  101.0 27.4 %copy-start = (bf16[1,512,1024]{2,1,0:T(8,128)(2,1)S(1)}, bf16[1,512,1024]{2,1,0:T(8,128)(2,1)}, u32[]{:S(2)}) copy-start(bf16[1,512,1024]{2,1,0:T(8,128)(2,1)} %param.17) | copy-start | bytes 3145732

commit v10 on v9

--- a/solution.py
+++ b/solution.py
@@ -38,6 +38,18 @@
 
 def dot_t(a, b):
     return lax.dot_general(a, b, (((1,), (1,)), ((), ())), preferred_element_type=f32)
+
+
+def join_kernel(first, second, out, sems):
+    rows = first.shape[0]
+    copies = [
+        pltpu.make_async_copy(first, out.at[:rows], sems.at[0]),
+        pltpu.make_async_copy(second, out.at[rows:], sems.at[1]),
+    ]
+    for copy in copies:
+        copy.start()
+    for copy in copies:
+        copy.wait()
 
 
 def attend_near_kernel(place, q, kv0, kv1, _, held, stats):
@@ -199,7 +211,15 @@
     def move(x, route):
         return lax.ppermute(x, "seq", route)
 
-    kv0 = jnp.concatenate([keys, values], axis=0)
+    kv0 = pl.pallas_call(
+        join_kernel,
+        out_shape=jax.ShapeDtypeStruct((2 * rows, width), bf16),
+        in_specs=[pl.BlockSpec(memory_space=pl.ANY)] * 2,
+        out_specs=vmem(),
+        scratch_shapes=[pltpu.SemaphoreType.DMA((2,))],
+        compiler_params=pltpu.CompilerParams(vmem_limit_bytes=56 * 1024 * 1024),
+        name="join",
+    )(keys, values)
     kv1 = move(kv0, onward)
     kv2 = move(kv1, onward)
     kvx0 = move(kv0, to_odd)

time: 181 us -> 181 us (level)
  local copies, waits for them, and re-layouts: 2.65 us -> 0.71 us
  Pallas kernels: 9.93 us -> 11.8 us
    pallas_call x0 -> x1, Pallas kernels: none -> 1.83 us  [local(): pl.pallas_call(join_kernel, out_shape=jax.ShapeDtypeStruct((2 * rows, wid...]
where the time goes in v10:
time: 181 us; the launch traced here: 180 us
  blocking collectives  130 us (72%)
  starting transfers between devices  24.8 us (14%)
  Pallas kernels  11.8 us (7%)
  waiting for transfers between devices  9.26 us (5%)
  other arithmetic  3.47 us (2%)
    all_to_all x2, blocking collectives, same_core_exchange(): lax.all_to_all(x, 'seq', 0, 0, tiled=True, axis_index_groups=same_core)  44 us
    all_to_all x1, blocking collectives, local(): lax.all_to_all(stream.reshape(seq_count, TILE, HEAD_DIM), 'seq', 0, 0, ti...  32.7 us
    all_to_all x1, blocking collectives, local(): finished = lax.all_to_all(pick(slot_of, returned), 'seq', 0, 0, tiled=True)  26.2 us
    ppermute x7, starting transfers between devices, move(): return lax.ppermute(x, 'seq', route)  20.6 us
    all_to_all x1, blocking collectives, local(): parts = lax.all_to_all(parts, 'tp', 0, 0, tiled=True)  17.7 us
    all_to_all x1, blocking collectives, local(): hidden = lax.all_to_all(hidden, 'tp', 0, 0, tiled=True)  9.33 us
    ppermute x7, waiting for transfers between devices, move(): return lax.ppermute(x, 'seq', route)  9.26 us
    all_to_all x1, starting transfers between devices, local(): first0 = lax.all_to_all(both, 'tp', 0, 0, tiled=True)  4.16 us
  transfers between devices with their start and end apart: 8, of which 2 were waited for; matrix products, arithmetic and copies ran while one was open for 2% of the time, Pallas kernels for 3%

profile of v10, /device:TPU:1, one launch (start us, length us, event | category | flops | bytes accessed | tf_op | source)
XLA Modules:
  0.0 180.1 jit_solution(18196402903036613639)
XLA Ops:
  0.0 1.8 %join.1.kv0 = bf16[256,1024]{1,0:T(8,128)(2,1)} custom-call(bf16[128,1024]{1,0:T(8,128)(2,1)} %first.1, bf16[128,1024]{1,0:T(8,128)(2,1)} %second.1), custom_call_target="tpu_custom_call" | custom-call | tf_op jit(solution)/shard_map/join/pallas_call | solution.py:214
  1.8 4.8 %collective-permute-start = (bf16[256,1024]{1,0:T(8,128)(2,1)}, bf16[256,1024]{1,0:T(8,128)(2,1)}, u32[]{:S(2)}, u32[]{:S(2)}) collective-permute-start(bf16[256,1024]{1,0:T(8,128)(2,1)} %join.1.kv0), channel_id=1, source_target_pairs={{0,8},{4,12},{8,16},{12,20},{16,24},{20,28},{24,32},{28,36},{32,40... | collective-permute-start | bytes 1572872 | tf_op jit(solution)/shard_map/ppermute | solution.py:212
  6.7 3.1 %pad_maximum_fusion = bf16[4096,256]{1,0:T(8,128)(2,1)} fusion(bf16[4096,128]{1,0:T(8,128)(2,1)} %bitcast.25, bf16[4096,128]{1,0:T(8,128)(2,1)} %bitcast.26), kind=kLoop, calls=%fused_computation | loop fusion | flops 4194304 | bytes 4194304 | tf_op jit(solution)/shard_map/concatenate | solution.py:231
  9.8 4.2 %all-to-all-start = ((bf16[4,1024,256]{2,1,0:T(8,128)(2,1)}), bf16[4,1024,256]{2,1,0:T(8,128)(2,1)S(1)}, u32[]{:S(2)}, u32[]{:S(2)}) async-start(bf16[4,1024,256]{2,1,0:T(8,128)(2,1)} %bitcast.24), calls=%async_computation | async-start | bytes 4194304 | tf_op jit(solution)/shard_map/all_to_all | solution.py:232
  14.0 1.3 collective-permute-start.2
  15.2 6.5 %collective-permute-start.5 = (bf16[512,1024]{1,0:T(8,128)(2,1)}, bf16[512,1024]{1,0:T(8,128)(2,1)}, u32[]{:S(2)}, u32[]{:S(2)}) collective-permute-start(bf16[512,1024]{1,0:T(8,128)(2,1)} %bitcast.19), channel_id=1, source_target_pairs={{0,4},{8,12},{16,20},{24,28},{32,36},{40,44},{48,52},{56,60},{64,6... | collective-permute-start | bytes 3145736 | tf_op jit(solution)/shard_map/ppermute | solution.py:212
  22.4 1.3 collective-permute-start.1
  24.1 1.9 %collective-permute-start.3 = (bf16[256,1024]{1,0:T(8,128)(2,1)}, bf16[256,1024]{1,0:T(8,128)(2,1)S(1)}, u32[]{:S(2)}, u32[]{:S(2)}) collective-permute-start(bf16[256,1024]{1,0:T(8,128)(2,1)} %collective-permute-done.kv1), channel_id=1, source_target_pairs={{0,4},{8,12},{16,20},{24,28},{32,36},{40,44},{48,52},{56,60},{64,6... | collective-permute-start | bytes 1572872 | tf_op jit(solution)/shard_map/ppermute | solution.py:212
  26.1 1.7 attend_near.1
  27.8 7.8 %collective-permute-done.1.kv2 = bf16[256,1024]{1,0:T(8,128)(2,1)S(1)} collective-permute-done((bf16[256,1024]{1,0:T(8,128)(2,1)}, bf16[256,1024]{1,0:T(8,128)(2,1)S(1)}, u32[]{:S(2)}, u32[]{:S(2)}) %collective-permute-start.1) | collective-permute-done | bytes 524320 | tf_op jit(solution)/shard_map/ppermute | solution.py:212
  35.6 2.5 %collective-permute-start.4 = (bf16[256,1024]{1,0:T(8,128)(2,1)S(1)}, bf16[256,1024]{1,0:T(8,128)(2,1)S(1)}, u32[]{:S(2)}, u32[]{:S(2)}) collective-permute-start(bf16[256,1024]{1,0:T(8,128)(2,1)S(1)} %collective-permute-done.1.kv2), channel_id=1, source_target_pairs={{4,0},{12,8},{20,16},{28,24},{36,32},{44,40},{52,48},{60,56},{68,6... | collective-permute-start | bytes 1572872 | tf_op jit(solution)/shard_map/ppermute | solution.py:212
  38.1 1.5 collective-permute-done.4.kvx2
  39.6 2.3 %attend_far.1 = (bf16[8,8,2,8,128]{4,3,2,1,0:T(8,128)(2,1)S(1)}, bf16[128,1024]{1,0:T(8,128)(2,1)S(1)}) custom-call(s32[2]{0:T(128)S(1)} %pad_add_fusion.place, bf16[128,1024]{1,0:T(8,128)(2,1)S(1)} %copy-done.2, bf16[256,1024]{1,0:T(8,128)(2,1)S(1)} %collective-permute-done.1.kv2, bf16[256,1024]{1,0:T(8,128)(2,1)} %collective-permute-done.2.kvx0, ...), custom_call_target="tpu_custom_call" | custom-call | tf_op jit(solution)/shard_map/attend_far/pallas_call | solution.py:263
  41.9 32.7 %all_to_all.35.tiles = bf16[128,8,128]{2,1,0:T(8,128)(2,1)S(1)} all-to-all(bf16[128,8,128]{2,1,0:T(8,128)(2,1)S(1)} %bitcast.22), channel_id=1, replica_groups=mesh['seq'=128,'tp'=4] {'seq'}, dimensions={0} | all-to-all | bytes 524288 | tf_op jit(solution)/shard_map/all_to_all | solution.py:276
  74.6 2.3 %collective-permute-start.6 = (bf16[4,1024,256]{2,1,0:T(8,128)(2,1)S(1)}, bf16[4,1024,256]{2,1,0:T(8,128)(2,1)S(1)}, u32[]{:S(2)}, u32[]{:S(2)}) collective-permute-start(bf16[4,1024,256]{2,1,0:T(8,128)(2,1)S(1)} %all-to-all-done.first0), channel_id=1, source_target_pairs={{0,4},{8,12},{16,20},{24,28},{32,36},{40,44},{48,52},{56,60},{64,6... | collective-permute-start | bytes 6291464 | tf_op jit(solution)/shard_map/ppermute | solution.py:212
  76.9 0.8 pick.2
  77.7 21.9 %all_to_all.36 = bf16[64,4,8,128]{3,2,1,0:T(8,128)(2,1)S(1)} all-to-all(bf16[64,4,8,128]{3,2,1,0:T(8,128)(2,1)S(1)} %bitcast.16), channel_id=1, replica_groups={{0,8,16,24,32,40,48,56,64,72,80,88,96,104,112,120,128,136,144,152,160,1..., dimensions={0} | all-to-all | bytes 1048576 | tf_op jit(solution)/shard_map/all_to_all | solution.py:292
  99.7 1.4 project.1
  101.1 17.7 %all_to_all.37.parts_ref = bf16[4,272,512]{2,1,0:T(8,128)(2,1)S(1)} all-to-all(bf16[4,272,512]{2,1,0:T(8,128)(2,1)S(1)} %project.1), channel_id=1, replica_groups=mesh['seq'=128,'tp'=4] {'tp'}, dimensions={0} | all-to-all | bytes 2228224 | tf_op jit(solution)/shard_map/all_to_all | solution.py:309
  119.1 9.3 %all_to_all.38.hidden = bf16[4,256,256]{2,1,0:T(8,128)(2,1)S(1)} all-to-all(bf16[4,256,256]{2,1,0:T(8,128)(2,1)S(1)} %hidden.1), channel_id=1, replica_groups=mesh['seq'=128,'tp'=4] {'tp'}, dimensions={0} | all-to-all | bytes 1048576 | tf_op jit(solution)/shard_map/all_to_all | solution.py:322
  128.5 1.9 %branch.1 = bf16[8,8,4,8,128]{4,3,2,1,0:T(8,128)(2,1)S(1)} custom-call(bf16[4,256,256]{2,1,0:T(8,128)(2,1)S(1)} %all_to_all.38.hidden, bf16[512,1024]{1,0:T(8,128)(2,1)S(1)} %bitcast.20, bf16[512,1024]{1,0:T(8,128)(2,1)} %collective-permute-done.5.down1), custom_call_target="tpu_custom_call" | custom-call | tf_op jit(solution)/shard_map/branch/pallas_call | solution.py:323
  130.4 22.1 %all_to_all.39 = bf16[64,4,8,128]{3,2,1,0:T(8,128)(2,1)S(1)} all-to-all(bf16[64,4,8,128]{3,2,1,0:T(8,128)(2,1)S(1)} %bitcast.18), channel_id=1, replica_groups={{0,8,16,24,32,40,48,56,64,72,80,88,96,104,112,120,128,136,144,152,160,1..., dimensions={0} | all-to-all | bytes 1048576 | tf_op jit(solution)/shard_map/all_to_all | solution.py:292
  153.2 26.2 %all_to_all.40 = bf16[128,8,128]{2,1,0:T(8,128)(2,1)S(1)} all-to-all(bf16[128,8,128]{2,1,0:T(8,128)(2,1)S(1)} %pick.3), channel_id=1, replica_groups=mesh['seq'=128,'tp'=4] {'seq'}, dimensions={0} | all-to-all | bytes 524288 | tf_op jit(solution)/shard_map/all_to_all | solution.py:337
  179.3 0.8 finish.1
  (23 shorter events, 2.1 us)
Async XLA Ops:
  1.8 20.6 %collective-permute-start = (bf16[256,1024]{1,0:T(8,128)(2,1)}, bf16[256,1024]{1,0:T(8,128)(2,1)}, u32[]{:S(2)}, u32[]{:S(2)}) collective-permute-start(bf16[256,1024]{1,0:T(8,128)(2,1)} %join.1.kv0), channel_id=1, source_target_pairs={{0,8},{4,12},{8,16},{12,20},{16,24},{20,28},{24,32},{28,36},{32,40... | collective-permute-start | bytes 1572872 | tf_op jit(solution)/shard_map/ppermute | solution.py:212
  9.8 4.2 %copy-start = (bf16[256,1024]{1,0:T(8,128)(2,1)S(1)}, bf16[256,1024]{1,0:T(8,128)(2,1)}, u32[]{:S(2)}) copy-start(bf16[256,1024]{1,0:T(8,128)(2,1)} %join.1.kv0) | copy-start | bytes 1572868
  9.8 14.0 %copy-start.4 = (s32[128,1]{0,1:T(1,128)S(1)}, s32[128,1]{0,1:T(1,128)}, u32[]{:S(2)}) copy-start(s32[128,1]{0,1:T(1,128)} %param.14) | copy-start | bytes 1540
  9.8 16.3 %copy-start.2 = (bf16[128,1024]{1,0:T(8,128)(2,1)S(1)}, bf16[128,1024]{1,0:T(8,128)(2,1)}, u32[]{:S(2)}) copy-start(bf16[128,1024]{1,0:T(8,128)(2,1)} %q.3) | copy-start | bytes 786436
  9.8 16.3 %copy-start.3 = (bf16[128,1024]{1,0:T(8,128)(2,1)S(1)}, bf16[128,1024]{1,0:T(8,128)(2,1)}, u32[]{:S(2)}) copy-start(bf16[128,1024]{1,0:T(8,128)(2,1)} %res.1) | copy-start | bytes 786436
  9.8 32.1 %all-to-all-start = ((bf16[4,1024,256]{2,1,0:T(8,128)(2,1)}), bf16[4,1024,256]{2,1,0:T(8,128)(2,1)S(1)}, u32[]{:S(2)}, u32[]{:S(2)}) async-start(bf16[4,1024,256]{2,1,0:T(8,128)(2,1)} %bitcast.24), calls=%async_computation | async-start | bytes 4194304 | tf_op jit(solution)/shard_map/all_to_all | solution.py:232
  14.0 24.1 %collective-permute-start.2 = (bf16[256,1024]{1,0:T(8,128)(2,1)S(1)}, bf16[256,1024]{1,0:T(8,128)(2,1)}, u32[]{:S(2)}, u32[]{:S(2)}) collective-permute-start(bf16[256,1024]{1,0:T(8,128)(2,1)S(1)} %copy-done), channel_id=1, source_target_pairs={{0,4},{8,12},{16,20},{24,28},{32,36},{40,44},{48,52},{56,60},{64,6... | collective-permute-start | bytes 1572872 | tf_op jit(solution)/shard_map/ppermute | solution.py:212
  15.2 26.6 %collective-permute-start.5 = (bf16[512,1024]{1,0:T(8,128)(2,1)}, bf16[512,1024]{1,0:T(8,128)(2,1)}, u32[]{:S(2)}, u32[]{:S(2)}) collective-permute-start(bf16[512,1024]{1,0:T(8,128)(2,1)} %bitcast.19), channel_id=1, source_target_pairs={{0,4},{8,12},{16,20},{24,28},{32,36},{40,44},{48,52},{56,60},{64,6... | collective-permute-start | bytes 3145736 | tf_op jit(solution)/shard_map/ppermute | solution.py:212
  22.4 13.1 %collective-permute-start.1 = (bf16[256,1024]{1,0:T(8,128)(2,1)}, bf16[256,1024]{1,0:T(8,128)(2,1)S(1)}, u32[]{:S(2)}, u32[]{:S(2)}) collective-permute-start(bf16[256,1024]{1,0:T(8,128)(2,1)} %collective-permute-done.kv1), channel_id=1, source_target_pairs={{0,8},{4,12},{8,16},{12,20},{16,24},{20,28},{24,32},{28,36},{32,40... | collective-permute-start | bytes 1572872 | tf_op jit(solution)/shard_map/ppermute | solution.py:212
  24.1 14.0 %collective-permute-start.3 = (bf16[256,1024]{1,0:T(8,128)(2,1)}, bf16[256,1024]{1,0:T(8,128)(2,1)S(1)}, u32[]{:S(2)}, u32[]{:S(2)}) collective-permute-start(bf16[256,1024]{1,0:T(8,128)(2,1)} %collective-permute-done.kv1), channel_id=1, source_target_pairs={{0,4},{8,12},{16,20},{24,28},{32,36},{40,44},{48,52},{56,60},{64,6... | collective-permute-start | bytes 1572872 | tf_op jit(solution)/shard_map/ppermute | solution.py:212
  35.6 4.0 %collective-permute-start.4 = (bf16[256,1024]{1,0:T(8,128)(2,1)S(1)}, bf16[256,1024]{1,0:T(8,128)(2,1)S(1)}, u32[]{:S(2)}, u32[]{:S(2)}) collective-permute-start(bf16[256,1024]{1,0:T(8,128)(2,1)S(1)} %collective-permute-done.1.kv2), channel_id=1, source_target_pairs={{4,0},{12,8},{20,16},{28,24},{36,32},{44,40},{52,48},{60,56},{68,6... | collective-permute-start | bytes 1572872 | tf_op jit(solution)/shard_map/ppermute | solution.py:212
  74.6 25.1 %collective-permute-start.6 = (bf16[4,1024,256]{2,1,0:T(8,128)(2,1)S(1)}, bf16[4,1024,256]{2,1,0:T(8,128)(2,1)S(1)}, u32[]{:S(2)}, u32[]{:S(2)}) collective-permute-start(bf16[4,1024,256]{2,1,0:T(8,128)(2,1)S(1)} %all-to-all-done.first0), channel_id=1, source_target_pairs={{0,4},{8,12},{16,20},{24,28},{32,36},{40,44},{48,52},{56,60},{64,6... | collective-permute-start | bytes 6291464 | tf_op jit(solution)/shard_map/ppermute | solution.py:212
  101.1 27.4 %copy-start.1 = (bf16[1,512,1024]{2,1,0:T(8,128)(2,1)S(1)}, bf16[1,512,1024]{2,1,0:T(8,128)(2,1)}, u32[]{:S(2)}) copy-start(bf16[1,512,1024]{2,1,0:T(8,128)(2,1)} %param.17) | copy-start | bytes 3145732
